TPU v7x, 256 devices: a whole 4x4x8 slice. The times are simulated.
256 devices in a mesh: stream: 4 (over x), cy: 8 (over y, core), cz: 8 (over z).
Axes of the slice: x: 4, y: 4, z: 8, core: 2. Of those that a mesh axis runs over, the one named last changes fastest.
Arguments:
- state: float32 [5, 8, 128, 1024], P(None, 'stream', 'cy', 'cz'), may hold values from -3 to 3
- source: float32 [5, 8, 128, 1024], P(None, 'stream', 'cy', 'cz'), may hold values from -3 to 3
- diag_scale: float32 [5, 8, 128, 1024], P(None, 'stream', 'cy', 'cz'), may hold values from 1.5 to 3
- diag_inverse: float32 [5, 5, 8, 128, 1024], P(None, None, 'stream', 'cy', 'cz'), may hold values from -0.1 to 0.9
- couple: float32 [7, 5, 5], replicated, may hold values from -2 to 2
- fluid: int32 [8, 128, 1024], P('stream', 'cy', 'cz'), may hold values 0 or 1
- donor_index: int32 [4, 8, 8, 64, 256], P('stream', 'cy', 'cz'), may hold values from 0 to 4095
- donor_count: int32 [4, 8, 8, 64], P('stream', 'cy', 'cz'), may hold values from 0 to 256, as said below
- ghost_cell: int32 [4, 8, 8, 1024], P('stream', 'cy', 'cz'), may hold values from 0 to 4095, as said below
- ghost_source: int32 [4, 8, 8, 1024, 8], P('stream', 'cy', 'cz'), may hold values from 0 to 16383
- ghost_weight: float32 [4, 8, 8, 1024, 8], P('stream', 'cy', 'cz'), may hold values from 0.02 to 0.25
Outputs:
- new_state: float32 [5, 8, 128, 1024], P(None, 'stream', 'cy', 'cz')
Inputs may be any that keep to these rules, and one draw needn't show every extreme that they name: donor_count counts the live leading slots; every device has one destination whose 256 slots are all live. `ghost_cell`: the ghost cells of one device are distinct local cells.
All inputs are finite; a program needn't handle non-finite values. No bound on the sum of `fluid` on one device may be relied on, other than what follows from the above.
Results may differ from a plain program's by a relative error of at most 0.0001.
Values sent between devices are 32-bit elements; how exact they have to be, the bound alone decides.
No kernel may reach another device: no remote copies, remote signals or barrier semaphores. Data moves between devices by JAX's collectives and lax.ppermute only.
A program may use at most 64 MiB of HBM per device.

v0:
```python
import jax
import jax.numpy as jnp
from jax import lax
from jax.sharding import PartitionSpec as P

HIGH = lax.Precision.HIGHEST
RELAX = 0.8
LANES = 128
SECTIONS = 4


def with_halo(x, sides, width):
    for axis, dim in sides:
        count, length = (lax.axis_size(axis), x.shape[dim])
        up = [(i, (i + 1) % count) for i in range(count - 1)]
        down = [(j, i) for i, j in up]
        last = lax.slice_in_dim(x, length - width, length, axis=dim)
        leading = lax.slice_in_dim(x, 0, width, axis=dim)
        before = lax.ppermute(last, axis, up)
        after = lax.ppermute(leading, axis, down)
        x = jnp.concatenate([before, x, after], axis=dim)
    return x


def shifted(value, axis, steps):
    count = lax.axis_size(axis)
    leading, last = (max(0, -steps), min(count, count - steps))
    return lax.ppermute(value, axis, [(source, source + steps) for source in range(leading, last)])


def apply_block(matrix, field):
    return jnp.einsum("ij,j...->i...", matrix, field, precision=HIGH)


def cell_apply(pmat, vector):
    return jnp.sum(pmat * vector[None], axis=1)


def pick_columns(table, wanted):
    nvar, total = table.shape
    row_count = total // LANES
    tiled = table.reshape(nvar * row_count, LANES)
    grouped = wanted.reshape(SECTIONS, -1)
    lane_ids = jnp.arange(LANES, dtype=jnp.int32)
    row_ids = jnp.arange(row_count, dtype=jnp.int32)

    def select_block(chosen):
        lane_onehot = (lane_ids[:, None] == (chosen % LANES)[None, :]).astype(jnp.float32)
        partial_rows = jnp.dot(
            tiled, lane_onehot, precision=HIGH, preferred_element_type=jnp.float32
        )
        partial_rows = partial_rows.reshape(nvar, row_count, chosen.shape[0])
        row_onehot = (row_ids[:, None] == (chosen // LANES)[None, :]).astype(jnp.float32)
        return jnp.sum(partial_rows * row_onehot[None], axis=1)

    picked = lax.map(select_block, grouped)
    return jnp.moveaxis(picked, 0, 1).reshape(nvar, wanted.shape[0])


def lower_sweep(inv_planes, res_planes, link, inflow):

    def lower_step(prev, xs):
        pmat, rhs = xs
        cur = cell_apply(pmat, rhs - apply_block(link, prev))
        return (cur, cur)

    last, planes = lax.scan(lower_step, inflow, (inv_planes, res_planes))
    return (planes, last)


def upper_sweep(inv_planes, low_planes, link, inflow):

    def upper_step(prev, xs):
        pmat, low = xs
        cur = low - cell_apply(pmat, apply_block(link, prev))
        return (cur, cur)

    first, planes = lax.scan(upper_step, inflow, (inv_planes, low_planes), reverse=True)
    return (planes, first)


def on_device(
    state,
    source,
    diag_scale,
    diag_inverse,
    couple,
    fluid,
    donor_index,
    donor_count,
    ghost_cell,
    ghost_source,
    ghost_weight,
):
    nvar, cx, cy, cz = state.shape
    cells = cx * cy * cz
    group = donor_index.shape[3]
    slots = donor_index.shape[4]
    ghosts = ghost_source.shape[3]
    donors = ghost_source.shape[4]
    flat = state.reshape(nvar, cells)
    picked = pick_columns(flat, donor_index.reshape(group * slots)).reshape(nvar, group, slots)
    live = jnp.arange(slots, dtype=jnp.int32)[None, :] < donor_count.reshape(group)[:, None]
    sent = jnp.where(live[None], picked, jnp.zeros_like(picked))
    received = lax.all_to_all(sent, ("cy", "cz"), split_axis=1, concat_axis=1, tiled=True)
    received = received.reshape(nvar, group * slots)
    values = pick_columns(received, ghost_source.reshape(ghosts * donors)).reshape(
        nvar, ghosts, donors
    )
    ghost_value = jnp.sum(values * ghost_weight.reshape(1, ghosts, donors), axis=-1)
    cell_onehot = (
        ghost_cell.reshape(ghosts)[:, None] == jnp.arange(cells, dtype=jnp.int32)[None, :]
    ).astype(jnp.float32)
    placed = jnp.dot(ghost_value, cell_onehot, precision=HIGH, preferred_element_type=jnp.float32)
    covered = jnp.sum(cell_onehot, axis=0)
    populated_ghosts = jnp.where(covered[None] > 0.5, placed, flat).reshape(nvar, cx, cy, cz)
    padded = with_halo(populated_ghosts, (("stream", 1), ("cy", 2), ("cz", 3)), 1)
    near = [
        padded[:, :-2, 1:-1, 1:-1],
        padded[:, 2:, 1:-1, 1:-1],
        padded[:, 1:-1, :-2, 1:-1],
        padded[:, 1:-1, 2:, 1:-1],
        padded[:, 1:-1, 1:-1, :-2],
        padded[:, 1:-1, 1:-1, 2:],
    ]
    image = diag_scale * populated_ghosts + apply_block(couple[0], populated_ghosts)
    for direction in range(6):
        image = image + apply_block(couple[direction + 1], near[direction])
    maskf = fluid.astype(jnp.float32)
    residual = maskf[None] * (source - image)
    inv_planes = jnp.moveaxis(diag_inverse, 2, 0)
    res_planes = jnp.moveaxis(residual, 1, 0)
    zero = jnp.zeros((nvar, cy, cz), jnp.float32)
    rounds = lax.axis_size("stream") - 1

    def lower_round(step, inflow):
        _, last = lower_sweep(inv_planes, res_planes, couple[1], inflow)
        return shifted(last, "stream", 1)

    lower_in = lax.fori_loop(0, rounds, lower_round, zero)
    low_planes, _ = lower_sweep(inv_planes, res_planes, couple[1], lower_in)

    def upper_exchange_round(step, inflow):
        _, first = upper_sweep(inv_planes, low_planes, couple[2], inflow)
        return shifted(first, "stream", -1)

    upper_incoming = lax.fori_loop(0, rounds, upper_exchange_round, zero)
    up_planes, _ = upper_sweep(inv_planes, low_planes, couple[2], upper_incoming)
    return populated_ghosts + RELAX * maskf[None] * jnp.moveaxis(up_planes, 0, 1)


def solution(mesh):
    in_specs = (
        P(None, "stream", "cy", "cz"),
        P(None, "stream", "cy", "cz"),
        P(None, "stream", "cy", "cz"),
        P(None, None, "stream", "cy", "cz"),
        P(),
        P("stream", "cy", "cz"),
        P("stream", "cy", "cz", None, None),
        P("stream", "cy", "cz", None),
        P("stream", "cy", "cz", None),
        P("stream", "cy", "cz", None, None),
        P("stream", "cy", "cz", None, None),
    )
    out_specs = P(None, "stream", "cy", "cz")
    return jax.shard_map(
        on_device, mesh=mesh, in_specs=in_specs, out_specs=out_specs, check_vma=False
    )
```

profile of v0, /device:TPU:10, one launch (start us, length us, event | category | flops | bytes accessed | tf_op | source)
XLA Modules:
  0.0 138.8 jit_solution(8709009852904694738)
XLA Ops:
  0.9 11.0 %while.122 = (s32[]{:T(128)}, f32[4,5,4096]{2,1,0:T(8,128)S(1)}, s32[4,4096]{1,0:T(4,128)S(1)}, f32[160,128]{1,0:T(8,128)}, s32[]{:T(128)}) while((s32[]{:T(128)}, f32[4,5,4096]{2,1,0:T(8,128)S(1)}, s32[4,4096]{1,0:T(4,128)S(1)}, f32[160,128]{1,0:T(8,128)}, s32[]{:T(128)}) %tuple.249), condition=%wide.region_3.4_spmd.clone, body=%wide.region_1.3_spmd.clone.sunk | while | flops 1008791552 | bytes 6832197 | solution.py:56
  13.6 12.1 %all-to-all-start = ((f32[5,64,256]{2,0,1:T(8,128)}), f32[5,64,256]{2,0,1:T(8,128)S(1)}, u32[]{:S(2)}, u32[]{:S(2)}) async-start(f32[5,64,256]{2,0,1:T(8,128)} %copy.151), calls=%async_computation | async-start | bytes 1048576 | tf_op jit(solution)/shard_map/all_to_all | solution.py:105
  27.2 2.8 %convert_reduce_fusion = f32[4096]{0:T(1024)S(1)} fusion(s32[1024]{0:T(1024)S(1)} %bitcast.261), kind=kLoop, calls=%fused_computation.54 | loop fusion | flops 12578816 | bytes 20480 | tf_op jit(solution)/shard_map/reduce_sum | solution.py:115
  30.1 13.6 %all-to-all-done = f32[5,64,256]{2,0,1:T(8,128)S(1)} async-done(((f32[5,64,256]{2,0,1:T(8,128)}), f32[5,64,256]{2,0,1:T(8,128)S(1)}, u32[]{:S(2)}, u32[]{:S(2)}) %all-to-all-start) | async-done | bytes 327712 | tf_op jit(solution)/shard_map/all_to_all | solution.py:105
  43.9 13.3 %while.123 = (s32[]{:T(128)}, f32[4,5,2048]{2,1,0:T(8,128)S(1)}, s32[4,2048]{1,0:T(4,128)S(1)}, f32[640,128]{1,0:T(8,128)S(1)}, s32[]{:T(128)}) while((s32[]{:T(128)}, f32[4,5,2048]{2,1,0:T(8,128)S(1)}, s32[4,2048]{1,0:T(4,128)S(1)}, f32[640,128]{1,0:T(8,128)S(1)}, s32[]{:T(128)}) %tuple.228), condition=%wide.region_6.7_spmd.clone.clone, body=%wide.region_4.6_spmd.clone.clone.sunk | while | flops 2016704512 | bytes 13140037 | solution.py:56
  60.6 5.4 %fusion.28 = f32[5,4096]{1,0:T(8,128)S(1)} fusion(f32[5,1024]{1,0:T(8,128)S(1)} %multiply_reduce_fusion.2, s32[1024]{0:T(1024)S(1)} %bitcast.262, f32[1,5,32,128]{3,2,1,0:T(8,128)S(1)} %bitcast.252, pred[4096]{0:T(1024)(128)(4,1)S(1)} %broadcast_compare_fusion), kind=kOutput, calls=%fused_computation.58 | convolution fusion | flops 255873024 | bytes 192512 | tf_op jit(solution)/shard_map/dot_general | solution.py:114
  66.0 3.4 %collective-permute-start.2 = (f32[5,1,16,128]{3,0,2,1:T(8,128)S(1)}, f32[5,1,16,128]{3,0,2,1:T(8,128)S(1)}, u32[]{:S(2)}, u32[]{:S(2)}) collective-permute-start(f32[5,1,16,128]{3,0,2,1:T(8,128)S(1)} %get-tuple-element.779), channel_id=1, source_target_pairs={{0,64},{64,128},{128,192},{1,65},{65,129},{129,193},{2,66},{66,130... | collective-permute-start | bytes 122888 | tf_op jit(solution)/shard_map/ppermute | solution.py:19
  69.4 2.4 %collective-permute-start.3 = (f32[5,1,16,128]{3,0,2,1:T(8,128)S(1)}, f32[5,1,16,128]{3,0,2,1:T(8,128)S(1)}, u32[]{:S(2)}, u32[]{:S(2)}) collective-permute-start(f32[5,1,16,128]{3,0,2,1:T(8,128)S(1)} %get-tuple-element.780), channel_id=1, source_target_pairs={{64,0},{128,64},{192,128},{65,1},{129,65},{193,129},{66,2},{130,66... | collective-permute-start | bytes 122888 | tf_op jit(solution)/shard_map/ppermute | solution.py:20
  72.1 3.4 %collective-permute-done.3 = f32[5,1,16,128]{3,0,2,1:T(8,128)S(1)} collective-permute-done((f32[5,1,16,128]{3,0,2,1:T(8,128)S(1)}, f32[5,1,16,128]{3,0,2,1:T(8,128)S(1)}, u32[]{:S(2)}, u32[]{:S(2)}) %collective-permute-start.3) | collective-permute-done | bytes 40992 | tf_op jit(solution)/shard_map/ppermute | solution.py:20
  77.5 3.6 %collective-permute-start.5 = (f32[5,4,1,128]{3,0,2,1:T(8,128)S(1)}, f32[5,4,1,128]{3,0,2,1:T(8,128)S(1)}, u32[]{:S(2)}, u32[]{:S(2)}) collective-permute-start(f32[5,4,1,128]{3,0,2,1:T(8,128)S(1)} %get-tuple-element.778), channel_id=1, source_target_pairs={{8,0},{16,8},{24,16},{32,24},{40,32},{48,40},{56,48},{9,1},{17,9},... | collective-permute-start | bytes 30728 | tf_op jit(solution)/shard_map/ppermute | solution.py:20
  82.7 2.9 %collective-permute-start.6 = (f32[5,4,18,1]{3,0,2,1:T(8,128)S(1)}, f32[5,4,18,1]{3,0,2,1:T(8,128)S(1)}, u32[]{:S(2)}, u32[]{:S(2)}) collective-permute-start(f32[5,4,18,1]{3,0,2,1:T(8,128)S(1)} %get-tuple-element.775), channel_id=1, source_target_pairs={{0,1},{1,2},{2,3},{3,4},{4,5},{5,6},{6,7},{8,9},{9,10},{10,11},{11... | collective-permute-start | bytes 4328 | tf_op jit(solution)/shard_map/ppermute | solution.py:19
  87.5 5.2 %collective-permute-done.6 = f32[5,4,18,1]{3,0,2,1:T(8,128)S(1)} collective-permute-done((f32[5,4,18,1]{3,0,2,1:T(8,128)S(1)}, f32[5,4,18,1]{3,0,2,1:T(8,128)S(1)}, u32[]{:S(2)}, u32[]{:S(2)}) %collective-permute-start.6) | collective-permute-done | bytes 1472 | tf_op jit(solution)/shard_map/ppermute | solution.py:19
  93.0 4.3 %collective-permute-done.7 = f32[5,4,18,1]{3,0,2,1:T(8,128)S(1)} collective-permute-done((f32[5,4,18,1]{3,0,2,1:T(8,128)S(1)}, f32[5,4,18,1]{3,0,2,1:T(8,128)S(1)}, u32[]{:S(2)}, u32[]{:S(2)}) %collective-permute-start.7) | collective-permute-done | bytes 1472 | tf_op jit(solution)/shard_map/ppermute | solution.py:20
  98.0 19.3 %while.117 = (s32[]{:T(128)}, f32[5,16,128]{2,1,0:T(8,128)S(1)}, f32[7,5,5]{2,1,0:T(8,128)S(1)}, f32[2,5,5,16,128]{4,3,2,1,0:T(8,128)S(1)}, f32[2,5,16,128]{3,1,...) while((s32[]{:T(128)}, f32[5,16,128]{2,1,0:T(8,128)S(1)}, f32[7,5,5]{2,1,0:T(8,128)S(1)}, ...), condition=%wide.region_12.13_spmd, body=%wide.region_8.12_spmd.sunk | while | flops 716804 | bytes 737838 | solution.py:140
  98.5 3.1 %collective-permute-start.1 = (f32[5,16,128]{2,1,0:T(8,128)S(1)}, f32[5,16,128]{2,1,0:T(8,128)S(1)}, u32[]{:S(2)}, u32[]{:S(2)}) collective-permute-start(f32[5,16,128]{2,1,0:T(8,128)S(1)} %get-tuple-element.1022), channel_id=1, source_target_pairs={{0,64},{64,128},{128,192},{1,65},{65,129},{129,193},{2,66},{66,130... | collective-permute-start | bytes 122888 | tf_op jit(solution)/shard_map/while/body/eval_jaxpr/ppermute | solution.py:28
  101.7 2.8 %collective-permute-done.1 = f32[5,16,128]{2,1,0:T(8,128)S(1)} collective-permute-done((f32[5,16,128]{2,1,0:T(8,128)S(1)}, f32[5,16,128]{2,1,0:T(8,128)S(1)}, u32[]{:S(2)}, u32[]{:S(2)}) %collective-permute-start.1) | collective-permute-done | bytes 40992 | tf_op jit(solution)/shard_map/while/body/eval_jaxpr/ppermute | solution.py:28
  105.0 3.1 %collective-permute-start.1 = (f32[5,16,128]{2,1,0:T(8,128)S(1)}, f32[5,16,128]{2,1,0:T(8,128)S(1)}, u32[]{:S(2)}, u32[]{:S(2)}) collective-permute-start(f32[5,16,128]{2,1,0:T(8,128)S(1)} %get-tuple-element.1022), channel_id=1, source_target_pairs={{0,64},{64,128},{128,192},{1,65},{65,129},{129,193},{2,66},{66,130... | collective-permute-start | bytes 122888 | tf_op jit(solution)/shard_map/while/body/eval_jaxpr/ppermute | solution.py:28
  108.1 2.8 %collective-permute-done.1 = f32[5,16,128]{2,1,0:T(8,128)S(1)} collective-permute-done((f32[5,16,128]{2,1,0:T(8,128)S(1)}, f32[5,16,128]{2,1,0:T(8,128)S(1)}, u32[]{:S(2)}, u32[]{:S(2)}) %collective-permute-start.1) | collective-permute-done | bytes 40992 | tf_op jit(solution)/shard_map/while/body/eval_jaxpr/ppermute | solution.py:28
  111.4 3.1 %collective-permute-start.1 = (f32[5,16,128]{2,1,0:T(8,128)S(1)}, f32[5,16,128]{2,1,0:T(8,128)S(1)}, u32[]{:S(2)}, u32[]{:S(2)}) collective-permute-start(f32[5,16,128]{2,1,0:T(8,128)S(1)} %get-tuple-element.1022), channel_id=1, source_target_pairs={{0,64},{64,128},{128,192},{1,65},{65,129},{129,193},{2,66},{66,130... | collective-permute-start | bytes 122888 | tf_op jit(solution)/shard_map/while/body/eval_jaxpr/ppermute | solution.py:28
  114.5 2.8 %collective-permute-done.1 = f32[5,16,128]{2,1,0:T(8,128)S(1)} collective-permute-done((f32[5,16,128]{2,1,0:T(8,128)S(1)}, f32[5,16,128]{2,1,0:T(8,128)S(1)}, u32[]{:S(2)}, u32[]{:S(2)}) %collective-permute-start.1) | collective-permute-done | bytes 40992 | tf_op jit(solution)/shard_map/while/body/eval_jaxpr/ppermute | solution.py:28
  117.8 19.7 %while.120 = (s32[]{:T(128)}, f32[5,16,128]{2,1,0:T(8,128)S(1)}, f32[7,5,5]{2,1,0:T(8,128)S(1)}, f32[2,5,16,128]{3,2,1,0:T(8,128)S(1)}, f32[2,5,5,16,128]{4,3,2,...) while((s32[]{:T(128)}, f32[5,16,128]{2,1,0:T(8,128)S(1)}, f32[7,5,5]{2,1,0:T(8,128)S(1)}, ...), condition=%wide.region_20.21_spmd, body=%wide.region_16.20_spmd.sunk | while | flops 716805 | bytes 819770 | solution.py:147
  120.4 4.0 %collective-permute-done = f32[5,16,128]{2,1,0:T(8,128)S(1)} collective-permute-done((f32[5,16,128]{2,1,0:T(8,128)S(1)}, f32[5,16,128]{2,1,0:T(8,128)S(1)}, u32[]{:S(2)}, u32[]{:S(2)}) %collective-permute-start) | collective-permute-done | bytes 40992 | tf_op jit(solution)/shard_map/while/body/eval_jaxpr/ppermute | solution.py:28
  126.8 4.3 %collective-permute-done = f32[5,16,128]{2,1,0:T(8,128)S(1)} collective-permute-done((f32[5,16,128]{2,1,0:T(8,128)S(1)}, f32[5,16,128]{2,1,0:T(8,128)S(1)}, u32[]{:S(2)}, u32[]{:S(2)}) %collective-permute-start) | collective-permute-done | bytes 40992 | tf_op jit(solution)/shard_map/while/body/eval_jaxpr/ppermute | solution.py:28
  133.6 4.0 %collective-permute-done = f32[5,16,128]{2,1,0:T(8,128)S(1)} collective-permute-done((f32[5,16,128]{2,1,0:T(8,128)S(1)}, f32[5,16,128]{2,1,0:T(8,128)S(1)}, u32[]{:S(2)}, u32[]{:S(2)}) %collective-permute-start) | collective-permute-done | bytes 40992 | tf_op jit(solution)/shard_map/while/body/eval_jaxpr/ppermute | solution.py:28
  (195 shorter events, 52.2 us)
Async XLA Ops:
  0.9 11.6 %copy-start.8 = (s32[1,1,1,64]{3,2,1,0:T(1,128)S(1)}, s32[1,1,1,64]{3,2,1,0:T(1,128)}, u32[]{:S(2)}) copy-start(s32[1,1,1,64]{3,2,1,0:T(1,128)} %param.34) | copy-start | bytes 772
  0.9 24.8 %copy-start.5 = (s32[1,1,1,1024,8]{3,4,2,1,0:T(8,128)S(1)}, s32[1,1,1,1024,8]{3,4,2,1,0:T(8,128)}, u32[]{:S(2)}) copy-start(s32[1,1,1,1024,8]{3,4,2,1,0:T(8,128)} %param.36) | copy-start | bytes 98308
  11.9 14.3 %copy-start.6 = (f32[1,1,1,1024,8]{3,4,2,1,0:T(8,128)S(1)}, f32[1,1,1,1024,8]{3,4,2,1,0:T(8,128)}, u32[]{:S(2)}) copy-start(f32[1,1,1,1024,8]{3,4,2,1,0:T(8,128)} %param.37) | copy-start | bytes 98308
  12.0 15.3 %copy-start.9 = (s32[1,1,1,1024]{3,2,1,0:T(1,128)S(1)}, s32[1,1,1,1024]{3,2,1,0:T(1,128)}, u32[]{:S(2)}) copy-start(s32[1,1,1,1024]{3,2,1,0:T(1,128)} %param.35) | copy-start | bytes 12292
  12.0 18.0 %copy-start.7 = (f32[7,5,5]{2,0,1:T(8,128)S(1)}, f32[7,5,5]{2,0,1:T(8,128)}, u32[]{:S(2)}) copy-start(f32[7,5,5]{2,0,1:T(8,128)} %param.31) | copy-start | bytes 2104
  12.0 18.0 %copy-start.4 = (s32[2,16,128]{2,1,0:T(8,128)S(1)}, s32[2,16,128]{2,1,0:T(8,128)}, u32[]{:S(2)}) copy-start(s32[2,16,128]{2,1,0:T(8,128)} %param.32) | copy-start | bytes 49156
  12.0 18.0 %copy-start.1 = (f32[5,5,2,16,128]{4,3,2,1,0:T(8,128)S(1)}, f32[5,5,2,16,128]{4,3,2,1,0:T(8,128)}, u32[]{:S(2)}) copy-start(f32[5,5,2,16,128]{4,3,2,1,0:T(8,128)} %param.30) | copy-start | bytes 1228804
  13.6 30.2 %all-to-all-start = ((f32[5,64,256]{2,0,1:T(8,128)}), f32[5,64,256]{2,0,1:T(8,128)S(1)}, u32[]{:S(2)}, u32[]{:S(2)}) async-start(f32[5,64,256]{2,0,1:T(8,128)} %copy.151), calls=%async_computation | async-start | bytes 1048576 | tf_op jit(solution)/shard_map/all_to_all | solution.py:105
  57.2 3.4 %copy-start = (f32[160,128]{1,0:T(8,128)S(1)}, f32[160,128]{1,0:T(8,128)}, u32[]{:S(2)}) copy-start(f32[160,128]{1,0:T(8,128)} %get-tuple-element.1235) | copy-start | bytes 245764
  58.7 13.1 %copy-start.2 = (f32[5,2,16,128]{3,2,1,0:T(8,128)S(1)}, f32[5,2,16,128]{3,2,1,0:T(8,128)}, u32[]{:S(2)}) copy-start(f32[5,2,16,128]{3,2,1,0:T(8,128)} %param.29) | copy-start | bytes 245764
  60.6 37.1 %copy-start.3 = (f32[5,2,16,128]{3,2,1,0:T(8,128)S(1)}, f32[5,2,16,128]{3,2,1,0:T(8,128)}, u32[]{:S(2)}) copy-start(f32[5,2,16,128]{3,2,1,0:T(8,128)} %param.28) | copy-start | bytes 245764
  66.0 6.2 %collective-permute-start.2 = (f32[5,1,16,128]{3,0,2,1:T(8,128)S(1)}, f32[5,1,16,128]{3,0,2,1:T(8,128)S(1)}, u32[]{:S(2)}, u32[]{:S(2)}) collective-permute-start(f32[5,1,16,128]{3,0,2,1:T(8,128)S(1)} %get-tuple-element.779), channel_id=1, source_target_pairs={{0,64},{64,128},{128,192},{1,65},{65,129},{129,193},{2,66},{66,130... | collective-permute-start | bytes 122888 | tf_op jit(solution)/shard_map/ppermute | solution.py:19
  69.4 6.2 %collective-permute-start.3 = (f32[5,1,16,128]{3,0,2,1:T(8,128)S(1)}, f32[5,1,16,128]{3,0,2,1:T(8,128)S(1)}, u32[]{:S(2)}, u32[]{:S(2)}) collective-permute-start(f32[5,1,16,128]{3,0,2,1:T(8,128)S(1)} %get-tuple-element.780), channel_id=1, source_target_pairs={{64,0},{128,64},{192,128},{65,1},{129,65},{193,129},{66,2},{130,66... | collective-permute-start | bytes 122888 | tf_op jit(solution)/shard_map/ppermute | solution.py:20
  75.5 5.8 %collective-permute-start.4 = (f32[5,4,1,128]{3,0,2,1:T(8,128)S(1)}, f32[5,4,1,128]{3,0,2,1:T(8,128)S(1)}, u32[]{:S(2)}, u32[]{:S(2)}) collective-permute-start(f32[5,4,1,128]{3,0,2,1:T(8,128)S(1)} %get-tuple-element.777), channel_id=1, source_target_pairs={{0,8},{8,16},{16,24},{24,32},{32,40},{40,48},{48,56},{1,9},{9,17},... | collective-permute-start | bytes 30728 | tf_op jit(solution)/shard_map/ppermute | solution.py:19
  77.5 5.1 %collective-permute-start.5 = (f32[5,4,1,128]{3,0,2,1:T(8,128)S(1)}, f32[5,4,1,128]{3,0,2,1:T(8,128)S(1)}, u32[]{:S(2)}, u32[]{:S(2)}) collective-permute-start(f32[5,4,1,128]{3,0,2,1:T(8,128)S(1)} %get-tuple-element.778), channel_id=1, source_target_pairs={{8,0},{16,8},{24,16},{32,24},{40,32},{48,40},{56,48},{9,1},{17,9},... | collective-permute-start | bytes 30728 | tf_op jit(solution)/shard_map/ppermute | solution.py:20
  82.7 10.0 %collective-permute-start.6 = (f32[5,4,18,1]{3,0,2,1:T(8,128)S(1)}, f32[5,4,18,1]{3,0,2,1:T(8,128)S(1)}, u32[]{:S(2)}, u32[]{:S(2)}) collective-permute-start(f32[5,4,18,1]{3,0,2,1:T(8,128)S(1)} %get-tuple-element.775), channel_id=1, source_target_pairs={{0,1},{1,2},{2,3},{3,4},{4,5},{5,6},{6,7},{8,9},{9,10},{10,11},{11... | collective-permute-start | bytes 4328 | tf_op jit(solution)/shard_map/ppermute | solution.py:19
  85.6 11.7 %collective-permute-start.7 = (f32[5,4,18,1]{3,0,2,1:T(8,128)S(1)}, f32[5,4,18,1]{3,0,2,1:T(8,128)S(1)}, u32[]{:S(2)}, u32[]{:S(2)}) collective-permute-start(f32[5,4,18,1]{3,0,2,1:T(8,128)S(1)} %get-tuple-element.776), channel_id=1, source_target_pairs={{1,0},{2,1},{3,2},{4,3},{5,4},{6,5},{7,6},{9,8},{10,9},{11,10},{12... | collective-permute-start | bytes 4328 | tf_op jit(solution)/shard_map/ppermute | solution.py:20
  98.5 5.9 %collective-permute-start.1 = (f32[5,16,128]{2,1,0:T(8,128)S(1)}, f32[5,16,128]{2,1,0:T(8,128)S(1)}, u32[]{:S(2)}, u32[]{:S(2)}) collective-permute-start(f32[5,16,128]{2,1,0:T(8,128)S(1)} %get-tuple-element.1022), channel_id=1, source_target_pairs={{0,64},{64,128},{128,192},{1,65},{65,129},{129,193},{2,66},{66,130... | collective-permute-start | bytes 122888 | tf_op jit(solution)/shard_map/while/body/eval_jaxpr/ppermute | solution.py:28
  105.0 5.9 %collective-permute-start.1 = (f32[5,16,128]{2,1,0:T(8,128)S(1)}, f32[5,16,128]{2,1,0:T(8,128)S(1)}, u32[]{:S(2)}, u32[]{:S(2)}) collective-permute-start(f32[5,16,128]{2,1,0:T(8,128)S(1)} %get-tuple-element.1022), channel_id=1, source_target_pairs={{0,64},{64,128},{128,192},{1,65},{65,129},{129,193},{2,66},{66,130... | collective-permute-start | bytes 122888 | tf_op jit(solution)/shard_map/while/body/eval_jaxpr/ppermute | solution.py:28
  111.4 5.9 %collective-permute-start.1 = (f32[5,16,128]{2,1,0:T(8,128)S(1)}, f32[5,16,128]{2,1,0:T(8,128)S(1)}, u32[]{:S(2)}, u32[]{:S(2)}) collective-permute-start(f32[5,16,128]{2,1,0:T(8,128)S(1)} %get-tuple-element.1022), channel_id=1, source_target_pairs={{0,64},{64,128},{128,192},{1,65},{65,129},{129,193},{2,66},{66,130... | collective-permute-start | bytes 122888 | tf_op jit(solution)/shard_map/while/body/eval_jaxpr/ppermute | solution.py:28
  118.4 5.9 %collective-permute-start = (f32[5,16,128]{2,1,0:T(8,128)S(1)}, f32[5,16,128]{2,1,0:T(8,128)S(1)}, u32[]{:S(2)}, u32[]{:S(2)}) collective-permute-start(f32[5,16,128]{2,1,0:T(8,128)S(1)} %get-tuple-element.1035), channel_id=1, source_target_pairs={{64,0},{128,64},{192,128},{65,1},{129,65},{193,129},{66,2},{130,66... | collective-permute-start | bytes 122888 | tf_op jit(solution)/shard_map/while/body/eval_jaxpr/ppermute | solution.py:28
  124.9 6.2 %collective-permute-start = (f32[5,16,128]{2,1,0:T(8,128)S(1)}, f32[5,16,128]{2,1,0:T(8,128)S(1)}, u32[]{:S(2)}, u32[]{:S(2)}) collective-permute-start(f32[5,16,128]{2,1,0:T(8,128)S(1)} %get-tuple-element.1035), channel_id=1, source_target_pairs={{64,0},{128,64},{192,128},{65,1},{129,65},{193,129},{66,2},{130,66... | collective-permute-start | bytes 122888 | tf_op jit(solution)/shard_map/while/body/eval_jaxpr/ppermute | solution.py:28
  131.7 5.9 %collective-permute-start = (f32[5,16,128]{2,1,0:T(8,128)S(1)}, f32[5,16,128]{2,1,0:T(8,128)S(1)}, u32[]{:S(2)}, u32[]{:S(2)}) collective-permute-start(f32[5,16,128]{2,1,0:T(8,128)S(1)} %get-tuple-element.1035), channel_id=1, source_target_pairs={{64,0},{128,64},{192,128},{65,1},{129,65},{193,129},{66,2},{130,66... | collective-permute-start | bytes 122888 | tf_op jit(solution)/shard_map/while/body/eval_jaxpr/ppermute | solution.py:28
where the time goes:
time: 140 us; the launch traced here: 139 us
  waiting for transfers between devices  48.3 us (34%)
  starting transfers between devices  42.8 us (31%)
  matrix products  28.1 us (20%)
  other arithmetic  11.7 us (8%)
  local copies, waits for them, and re-layouts  6.04 us (4%)
  loops' own time  1.43 us (1%)
    ppermute x6, waiting for transfers between devices, shifted(): lax.ppermute(value, axis, [(source, source + steps) for source in range(l...  20.5 us
    dot_general x8, matrix products, select_block(): jnp.dot(tiled, lane_onehot, precision=HIGH, preferred_element_type=jnp.fl...  17.8 us
    ppermute x6, starting transfers between devices, shifted(): lax.ppermute(value, axis, [(source, source + steps) for source in range(l...  15.1 us
    all_to_all x1, waiting for transfers between devices, on_device(): lax.all_to_all(sent, ('cy', 'cz'), split_axis=1, concat_axis=1, tiled=True)  13.6 us
    all_to_all x1, starting transfers between devices, on_device(): lax.all_to_all(sent, ('cy', 'cz'), split_axis=1, concat_axis=1, tiled=True)  12.1 us
    ppermute x3, waiting for transfers between devices, with_halo(): after = lax.ppermute(leading, axis, down)  8.84 us
    ppermute x3, starting transfers between devices, with_halo(): before = lax.ppermute(last, axis, up)  8.23 us
    ppermute x3, starting transfers between devices, with_halo(): after = lax.ppermute(leading, axis, down)  7.38 us
  transfers between devices with their start and end apart: 13, of which 11 were waited for; matrix products, arithmetic and copies ran while one was open for 4% of the time, Pallas kernels for 0%

commit v1 on v0

v1 whole, which is shorter than its diff:
```python
import jax
import jax.numpy as jnp
from jax import lax
from jax.experimental import pallas as pl
from jax.experimental.pallas import tpu as pltpu
from jax.sharding import PartitionSpec as P

RELAX = 0.8
LANES = 128
F32 = jnp.float32
BF16 = jnp.bfloat16
VMEM = pl.BlockSpec(memory_space=pltpu.VMEM)
SMEM = pl.BlockSpec(memory_space=pltpu.SMEM)
BYTES = 24 << 20


def ring(x, axis, steps):
    count = lax.axis_size(axis)
    return lax.ppermute(x, axis, [(i, (i + steps) % count) for i in range(count)])


def call(kernel, outs, args, specs, name):
    return pl.pallas_call(
        kernel,
        out_shape=outs,
        in_specs=specs,
        out_specs=jax.tree.map(lambda _: VMEM, outs),
        name=name,
        compiler_params=pltpu.CompilerParams(vmem_limit_bytes=BYTES),
    )(*args)


def lane_pick(rows, lane):
    return jnp.take_along_axis(rows, lane, axis=1, mode="promise_in_bounds")


def donor_kernel(idx_ref, count_ref, state_ref, out_ref):
    lanes = lax.broadcasted_iota(jnp.int32, (8, LANES), 1)
    subs = lax.broadcasted_iota(jnp.int32, (8, LANES), 0)

    def body(g, carry):
        base = pl.multiple_of(g * 8, 8)
        count = jnp.zeros((8, LANES), jnp.int32)
        for q in range(8):
            count = jnp.where(subs == q, count_ref[0, g * 8 + q], count)
        for h in range(2):
            idx = idx_ref[pl.ds(base, 8), h * LANES : (h + 1) * LANES]
            lane = idx & (LANES - 1)
            row = idx >> 7
            acc = [jnp.zeros((8, LANES), F32) for _ in range(5)]
            for r in range(32):
                hit = row == r
                for v in range(5):
                    line = state_ref[v * 32 + r : v * 32 + r + 1, :]
                    line = jnp.broadcast_to(line, (8, LANES))
                    acc[v] = jnp.where(hit, lane_pick(line, lane), acc[v])
            live = lanes + h * LANES < count
            for v in range(5):
                at = (v * 2 + h) * LANES
                out_ref[pl.ds(base, 8), 0, at : at + LANES] = jnp.where(live, acc[v], 0.0)
        return carry

    lax.fori_loop(0, 8, body, 0)


def ghost_kernel(
    rec_ref, src_ref, w_ref, cell_ref, state_ref, f_ref, x0_ref, x1_ref, y_ref, z_ref
):
    tabs = []
    for v in range(5):
        t = rec_ref[:, 0, v * 256 : (v + 1) * 256]
        hi = t.astype(BF16)
        lo = (t - hi.astype(F32)).astype(BF16)
        tabs.append(jnp.concatenate([hi, lo], axis=1))
    tab = jnp.concatenate(tabs, axis=0)
    width = 256
    lane_ids = lax.broadcasted_iota(jnp.int32, (256, width), 0)
    row_ids = lax.broadcasted_iota(jnp.int32, (64, width), 0)
    parts = [[] for _ in range(5)]
    for j in range(1024 // width):
        at = slice(j * width, (j + 1) * width)
        acc = [jnp.zeros((8, width), F32) for _ in range(5)]
        for k in range(8):
            entry = src_ref[k : k + 1, at]
            weight = w_ref[k : k + 1, at]
            onehot = (lane_ids == (entry & 255)).astype(BF16)
            onehot = jnp.concatenate([onehot, onehot], axis=0)
            p = jnp.dot(tab, onehot, preferred_element_type=F32)
            m = jnp.where(row_ids == (entry >> 8), weight, 0.0)
            for v in range(5):
                q = p[v * 64 : (v + 1) * 64] * m
                acc[v] = acc[v] + jnp.sum(q.reshape(8, 8, width), axis=0)
        for v in range(5):
            parts[v].append(jnp.sum(acc[v], axis=0, keepdims=True))
    values = [jnp.concatenate(p, axis=1) for p in parts]

    cell = cell_ref[...]
    in_row = lax.broadcasted_iota(jnp.int32, (32, 1024), 0) == (cell >> 7)
    in_lane = lax.broadcasted_iota(jnp.int32, (LANES, 1024), 0) == (cell & (LANES - 1))
    pieces = [[], [], []]
    for v in range(5):
        x = jnp.where(in_row, values[v], 0.0)
        hi = x.astype(BF16)
        rest = x - hi.astype(F32)
        mid = rest.astype(BF16)
        pieces[0].append(hi)
        pieces[1].append(mid)
        pieces[2].append((rest - mid.astype(F32)).astype(BF16))
    left = jnp.concatenate([in_row.astype(BF16)] + pieces[0] + pieces[1] + pieces[2], axis=0)
    placed = lax.dot_general(
        left, in_lane.astype(BF16), (((1,), (1,)), ((), ())), preferred_element_type=F32
    )
    covered = placed[0:32] > 0.5
    diag = lax.broadcasted_iota(jnp.int32, (16, LANES), 0) == lax.broadcasted_iota(
        jnp.int32, (16, LANES), 1
    )
    for v in range(5):
        hi, mid, lo = (placed[32 * (1 + v + 5 * p) : 32 * (2 + v + 5 * p)] for p in range(3))
        old = state_ref[32 * v : 32 * v + 32, :]
        new = jnp.where(covered, hi + (mid + lo), old)
        f_ref[32 * v : 32 * v + 32, :] = new
        x0_ref[v] = new[0:16]
        x1_ref[v] = new[16:32]
        for x in range(2):
            plane = new[16 * x : 16 * x + 16]
            row = 2 * v + x
            y_ref[0, row : row + 1, :] = plane[0:1]
            y_ref[1, row : row + 1, :] = plane[15:16]
            for side, col in ((0, 0), (1, LANES - 1)):
                face = jnp.where(diag, plane[:, col : col + 1], 0.0)
                z_ref[side, row : row + 1, :] = jnp.sum(face, axis=0, keepdims=True)


def residual_kernel(
    f_ref, xm_ref, xp_ref, ym_ref, yp_ref, zm_ref, zp_ref, source_ref, scale_ref, fluid_ref,
    couple_ref, out_ref,
):
    s, a, b = (lax.axis_index(n) for n in ("stream", "cy", "cz"))
    ns, na, nb = (lax.axis_size(n) for n in ("stream", "cy", "cz"))
    shape = (16, LANES)
    subs = lax.broadcasted_iota(jnp.int32, shape, 0)
    lanes = lax.broadcasted_iota(jnp.int32, shape, 1)

    def column(ref, row):
        line = jnp.broadcast_to(ref[row : row + 1, :], shape)
        return jnp.concatenate(
            [lane_pick(line[0:8], subs[0:8]), lane_pick(line[8:16], subs[8:16])], axis=0
        )

    for x in range(2):
        near = [[] for _ in range(7)]
        for v in range(5):
            row = 2 * v + x
            mid = f_ref[32 * v + 16 * x : 32 * v + 16 * x + 16, :]
            other = f_ref[32 * v + 16 * (1 - x) : 32 * v + 16 * (1 - x) + 16, :]
            if x == 0:
                xm, xp = jnp.where(s > 0, xm_ref[v], 0.0), other
            else:
                xm, xp = other, jnp.where(s < ns - 1, xp_ref[v], 0.0)
            ym = jnp.where(a > 0, ym_ref[row : row + 1, :], 0.0)
            yp = jnp.where(a < na - 1, yp_ref[row : row + 1, :], 0.0)
            zm = jnp.where(b > 0, column(zm_ref, row), 0.0)
            zp = jnp.where(b < nb - 1, column(zp_ref, row), 0.0)
            near[0].append(mid)
            near[1].append(xm)
            near[2].append(xp)
            near[3].append(jnp.where(subs == 0, ym, pltpu.roll(mid, 1, 0)))
            near[4].append(jnp.where(subs == 15, yp, pltpu.roll(mid, 15, 0)))
            near[5].append(jnp.where(lanes == 0, zm, pltpu.roll(mid, 1, 1)))
            near[6].append(jnp.where(lanes == LANES - 1, zp, pltpu.roll(mid, LANES - 1, 1)))
        wet = fluid_ref[x].astype(F32)
        for i in range(5):
            image = scale_ref[i, x] * near[0][i]
            for d in range(7):
                for j in range(5):
                    image = image + couple_ref[d, i, j] * near[d][j]
            out_ref[x, i] = wet * (source_ref[i, x] - image)


def sweep_kernel(
    res_ref, prev_ref, next_ref, far_ref, inv_ref, f_ref, fluid_ref, couple_ref, out_ref, low_ref
):
    s = lax.axis_index("stream")
    count = 4
    zero = jnp.zeros((16, LANES), F32)
    prev = [zero] * 5
    for q in range(count):
        o = lax.rem(q - s + count, count)
        for x in range(2):
            t = []
            for i in range(5):
                r = jnp.where(
                    o == 0,
                    res_ref[x, i],
                    jnp.where(
                        o == 1, next_ref[x, i], jnp.where(o == 2, far_ref[x, i], prev_ref[x, i])
                    ),
                )
                for j in range(5):
                    r = r - couple_ref[1, i, j] * prev[j]
                t.append(r)
            cur = []
            for i in range(5):
                c = inv_ref[o, i, 0, x] * t[0]
                for j in range(1, 5):
                    c = c + inv_ref[o, i, j, x] * t[j]
                cur.append(c)
                low_ref[2 * q + x, i] = c
            prev = cur
    prev = [zero] * 5
    for q in reversed(range(count)):
        o = lax.rem(q - s + count, count)
        for x in (1, 0):
            t = []
            for i in range(5):
                r = couple_ref[2, i, 0] * prev[0]
                for j in range(1, 5):
                    r = r + couple_ref[2, i, j] * prev[j]
                t.append(r)
            cur = []
            for i in range(5):
                c = low_ref[2 * q + x, i]
                for j in range(5):
                    c = c - inv_ref[o, i, j, x] * t[j]
                cur.append(c)
            prev = cur

            @pl.when(o == 0)
            def _():
                wet = RELAX * fluid_ref[x].astype(F32)
                for i in range(5):
                    at = 32 * i + 16 * x
                    out_ref[i, x] = f_ref[at : at + 16, :] + wet * cur[i]


def on_device(
    state,
    source,
    diag_scale,
    diag_inverse,
    couple,
    fluid,
    donor_index,
    donor_count,
    ghost_cell,
    ghost_source,
    ghost_weight,
):
    table = state.reshape(160, LANES)
    sent = call(
        donor_kernel,
        jax.ShapeDtypeStruct((64, 1, 1280), F32),
        (donor_index.reshape(64, 256), donor_count.reshape(1, 64), table),
        [VMEM, SMEM, VMEM],
        "donor_pick",
    )
    received = lax.all_to_all(sent, ("cy", "cz"), split_axis=0, concat_axis=0, tiled=True)
    inv = jnp.stack(
        [diag_inverse] + [ring(diag_inverse, "stream", step) for step in (-1, 2, 1)]
    )
    plane = jax.ShapeDtypeStruct((5, 16, LANES), F32)
    faces = jax.ShapeDtypeStruct((2, 10, LANES), F32)
    filled, first, last, yface, zface = call(
        ghost_kernel,
        (jax.ShapeDtypeStruct((160, LANES), F32), plane, plane, faces, faces),
        (
            received,
            ghost_source.reshape(1024, 8).T,
            ghost_weight.reshape(1024, 8).T,
            ghost_cell.reshape(1, 1024),
            table,
        ),
        [VMEM] * 5,
        "ghost_fill",
    )
    xm, xp = ring(last, "stream", 1), ring(first, "stream", -1)
    ym, yp = ring(yface[1], "cy", 1), ring(yface[0], "cy", -1)
    zm, zp = ring(zface[1], "cz", 1), ring(zface[0], "cz", -1)
    residual = call(
        residual_kernel,
        jax.ShapeDtypeStruct((2, 5, 16, LANES), F32),
        (filled, xm, xp, ym, yp, zm, zp, source, diag_scale, fluid, couple),
        [VMEM] * 10 + [SMEM],
        "residual",
    )
    after, far, before = (ring(residual, "stream", step) for step in (-1, 2, 1))
    return pl.pallas_call(
        sweep_kernel,
        out_shape=jax.ShapeDtypeStruct((5, 2, 16, LANES), F32),
        in_specs=[VMEM] * 7 + [SMEM],
        out_specs=VMEM,
        scratch_shapes=[pltpu.VMEM((8, 5, 16, LANES), F32)],
        name="sweeps",
        compiler_params=pltpu.CompilerParams(vmem_limit_bytes=BYTES),
    )(residual, before, after, far, inv, filled, fluid, couple)


def solution(mesh):
    in_specs = (
        P(None, "stream", "cy", "cz"),
        P(None, "stream", "cy", "cz"),
        P(None, "stream", "cy", "cz"),
        P(None, None, "stream", "cy", "cz"),
        P(),
        P("stream", "cy", "cz"),
        P("stream", "cy", "cz", None, None),
        P("stream", "cy", "cz", None),
        P("stream", "cy", "cz", None),
        P("stream", "cy", "cz", None, None),
        P("stream", "cy", "cz", None, None),
    )
    out_specs = P(None, "stream", "cy", "cz")
    return jax.shard_map(
        on_device, mesh=mesh, in_specs=in_specs, out_specs=out_specs, check_vma=False
    )
```

time: 140 us -> 69.3 us (0.49)
  the two profiles are of different devices: /device:TPU:10 before, /device:TPU:4 now
where the time goes in v1:
time: 69.3 us; the launch traced here: 68.9 us
  waiting for transfers between devices  26.4 us (38%)
  starting transfers between devices  23.4 us (34%)
  Pallas kernels  13.4 us (19%)
  local copies, waits for them, and re-layouts  5.5 us (8%)
    ppermute x12, waiting for transfers between devices, ring(): lax.ppermute(x, axis, [(i, (i + steps) % count) for i in range(count)])  15.7 us
    all_to_all x1, starting transfers between devices, on_device(): lax.all_to_all(sent, ('cy', 'cz'), split_axis=0, concat_axis=0, tiled=True)  12.1 us
    ppermute x12, starting transfers between devices, ring(): lax.ppermute(x, axis, [(i, (i + steps) % count) for i in range(count)])  11.3 us
    pallas_call x3, Pallas kernels, call(): pl.pallas_call(kernel, out_shape=outs, in_specs=specs, out_specs=jax.tree...  11.2 us
    all_to_all x1, waiting for transfers between devices, on_device(): lax.all_to_all(sent, ('cy', 'cz'), split_axis=0, concat_axis=0, tiled=True)  10.7 us
    unnamed x25, local copies, waits for them, and re-layouts  5.5 us
    pallas_call x1, Pallas kernels, on_device(): pl.pallas_call(sweep_kernel, out_shape=jax.ShapeDtypeStruct((5, 2, 16, LA...  2.18 us
  transfers between devices with their start and end apart: 13, of which 7 were waited for; matrix products, arithmetic and copies ran while one was open for 0% of the time, Pallas kernels for 9%

profile of v1, /device:TPU:4, one launch (start us, length us, event | category | flops | bytes accessed | tf_op | source)
XLA Modules:
  0.0 68.9 jit_solution(560326355524302715)
XLA Ops:
  0.0 0.9 %copy-done = f32[5,2,16,128]{3,2,1,0:T(8,128)S(1)} copy-done((f32[5,2,16,128]{3,2,1,0:T(8,128)S(1)}, f32[5,2,16,128]{3,2,1,0:T(8,128)}, u32[]{:S(2)}) %copy-start) | copy-done | bytes 81944
  0.9 0.8 %copy-done.5 = s32[1,1,1,64,256]{4,3,2,1,0:T(8,128)S(1)} copy-done((s32[1,1,1,64,256]{4,3,2,1,0:T(8,128)S(1)}, s32[1,1,1,64,256]{4,3,2,1,0:T(8,128)}, u32[]{:S(2)}) %copy-start.5) | copy-done | bytes 65560
  2.4 4.7 %donor_pick.1 = f32[64,1,1280]{2,1,0:T(1,128)} custom-call(s32[64,256]{1,0:T(8,128)S(1)} %bitcast.24, s32[1,64]{1,0:T(1,128)S(1)} %bitcast.28, f32[160,128]{1,0:T(8,128)S(1)} %bitcast.22), custom_call_target="tpu_custom_call" | custom-call | tf_op jit(solution)/shard_map/donor_pick/pallas_call | solution.py:23
  7.1 12.1 %all-to-all-start = ((f32[64,1,1280]{2,1,0:T(1,128)}), f32[64,1,1280]{2,1,0:T(1,128)S(1)}, u32[]{:S(2)}, u32[]{:S(2)}) async-start(f32[64,1,1280]{2,1,0:T(1,128)} %donor_pick.1), calls=%async_computation | async-start | bytes 655360 | tf_op jit(solution)/shard_map/all_to_all | solution.py:257
  19.9 1.5 %collective-permute-start.11 = (f32[5,5,2,16,128]{4,3,2,1,0:T(8,128)}, f32[5,5,2,16,128]{4,3,2,1,0:T(8,128)S(1)}, u32[]{:S(2)}, u32[]{:S(2)}) collective-permute-start(f32[5,5,2,16,128]{4,3,2,1,0:T(8,128)} %param.14), channel_id=1, source_target_pairs={{0,64},{64,128},{128,192},{192,0},{1,65},{65,129},{129,193},{193,1... | collective-permute-start | bytes 1228808 | tf_op jit(solution)/shard_map/ppermute | solution.py:19
  21.4 1.2 %collective-permute-start.10 = (f32[5,5,2,16,128]{4,3,2,1,0:T(8,128)}, f32[5,5,2,16,128]{4,3,2,1,0:T(8,128)S(1)}, u32[]{:S(2)}, u32[]{:S(2)}) collective-permute-start(f32[5,5,2,16,128]{4,3,2,1,0:T(8,128)} %param.14), channel_id=1, source_target_pairs={{0,128},{64,192},{128,0},{192,64},{1,129},{65,193},{129,1},{193,65... | collective-permute-start | bytes 1228808 | tf_op jit(solution)/shard_map/ppermute | solution.py:19
  22.6 10.7 %all-to-all-done.rec_ref = f32[64,1,1280]{2,1,0:T(1,128)S(1)} async-done(((f32[64,1,1280]{2,1,0:T(1,128)}), f32[64,1,1280]{2,1,0:T(1,128)S(1)}, u32[]{:S(2)}, u32[]{:S(2)}) %all-to-all-start) | async-done | bytes 327712 | tf_op jit(solution)/shard_map/all_to_all | solution.py:257
  33.3 0.9 %copy-done.1 = f32[5,2,16,128]{3,2,1,0:T(8,128)S(1)} copy-done((f32[5,2,16,128]{3,2,1,0:T(8,128)S(1)}, f32[5,2,16,128]{3,2,1,0:T(8,128)}, u32[]{:S(2)}) %copy-start.1) | copy-done | bytes 81944
  34.2 0.8 %copy-done.6 = s32[1,1,1,1024,8]{3,4,2,1,0:T(8,128)S(1)} copy-done((s32[1,1,1,1024,8]{3,4,2,1,0:T(8,128)S(1)}, s32[1,1,1,1024,8]{3,4,2,1,0:T(8,128)}, u32[]{:S(2)}) %copy-start.6) | copy-done | bytes 32792
  35.0 0.8 %copy-done.7 = f32[1,1,1,1024,8]{3,4,2,1,0:T(8,128)S(1)} copy-done((f32[1,1,1,1024,8]{3,4,2,1,0:T(8,128)S(1)}, f32[1,1,1,1024,8]{3,4,2,1,0:T(8,128)}, u32[]{:S(2)}) %copy-start.7) | copy-done | bytes 32792
  35.7 0.7 copy-done.8
  36.4 5.1 %ghost_fill.1 = (f32[160,128]{1,0:T(8,128)S(1)}, f32[5,16,128]{2,1,0:T(8,128)S(1)}, f32[5,16,128]{2,1,0:T(8,128)S(1)}, f32[2,10,128]{2,1,0:T(8,128)S(1)}, f32[2,10,128]{2,1,0:T(8,128)S(1)}) custom-call(f32[64,1,1280]{2,1,0:T(1,128)S(1)} %all-to-all-done.rec_ref, s32[8,1024]{1,0:T(8,128)S(1)} %bitcast.25, f32[8,1024]{1,0:T(8,128)S(1)} %bitcast.26, ...), custom_call_target="tpu_custom_call" | custom-call | tf_op jit(solution)/shard_map/ghost_fill/pallas_call | solution.py:23
  41.5 2.2 %collective-permute-start.5 = (f32[10,128]{1,0:T(8,128)S(1)}, f32[10,128]{1,0:T(8,128)S(1)}, u32[]{:S(2)}, u32[]{:S(2)}) collective-permute-start(f32[10,128]{1,0:T(8,128)S(1)} %get-tuple-element.15), channel_id=1, source_target_pairs={{0,7},{1,0},{2,1},{3,2},{4,3},{5,4},{6,5},{7,6},{8,15},{9,8},{10,9... | collective-permute-start | bytes 15368 | tf_op jit(solution)/shard_map/ppermute | solution.py:19
  43.7 1.5 %collective-permute-done.5.zp_ref = f32[10,128]{1,0:T(8,128)S(1)} collective-permute-done((f32[10,128]{1,0:T(8,128)S(1)}, f32[10,128]{1,0:T(8,128)S(1)}, u32[]{:S(2)}, u32[]{:S(2)}) %collective-permute-start.5) | collective-permute-done | bytes 5152 | tf_op jit(solution)/shard_map/ppermute | solution.py:19
  45.2 3.4 %collective-permute-done.4.zm_ref = f32[10,128]{1,0:T(8,128)S(1)} collective-permute-done((f32[10,128]{1,0:T(8,128)S(1)}, f32[10,128]{1,0:T(8,128)S(1)}, u32[]{:S(2)}, u32[]{:S(2)}) %collective-permute-start.4) | collective-permute-done | bytes 5152 | tf_op jit(solution)/shard_map/ppermute | solution.py:19
  48.6 1.2 %collective-permute-start = (f32[5,16,128]{2,1,0:T(8,128)S(1)}, f32[5,16,128]{2,1,0:T(8,128)S(1)}, u32[]{:S(2)}, u32[]{:S(2)}) collective-permute-start(f32[5,16,128]{2,1,0:T(8,128)S(1)} %get-tuple-element.11), channel_id=1, source_target_pairs={{0,64},{64,128},{128,192},{192,0},{1,65},{65,129},{129,193},{193,1... | collective-permute-start | bytes 122888 | tf_op jit(solution)/shard_map/ppermute | solution.py:19
  49.8 3.1 %collective-permute-done.2.ym_ref = f32[10,128]{1,0:T(8,128)S(1)} collective-permute-done((f32[10,128]{1,0:T(8,128)S(1)}, f32[10,128]{1,0:T(8,128)S(1)}, u32[]{:S(2)}, u32[]{:S(2)}) %collective-permute-start.2) | collective-permute-done | bytes 5152 | tf_op jit(solution)/shard_map/ppermute | solution.py:19
  53.5 3.4 %collective-permute-done.1.xp_ref = f32[5,16,128]{2,1,0:T(8,128)S(1)} collective-permute-done((f32[5,16,128]{2,1,0:T(8,128)S(1)}, f32[5,16,128]{2,1,0:T(8,128)S(1)}, u32[]{:S(2)}, u32[]{:S(2)}) %collective-permute-start.1) | collective-permute-done | bytes 40992 | tf_op jit(solution)/shard_map/ppermute | solution.py:19
  56.9 1.4 %residual.1.res_ref = f32[2,5,16,128]{3,2,1,0:T(8,128)S(1)} custom-call(f32[160,128]{1,0:T(8,128)S(1)} %get-tuple-element.10.f_ref, f32[5,16,128]{2,1,0:T(8,128)S(1)} %collective-permute-done.xm_ref, f32[5,16,128]{2,1,0:T(8,128)S(1)} %collective-permute-done.1.xp_ref, f32[10,128]{1,0:T(8,128)S(1)} %collective-permute-done.2.ym_ref, ...), custom_call_target="tpu_custom_call" | custom-call | tf_op jit(solution)/shard_map/residual/pallas_call | solution.py:23
  58.3 1.0 %collective-permute-start.8 = (f32[2,5,16,128]{3,2,1,0:T(8,128)S(1)}, f32[2,5,16,128]{3,2,1,0:T(8,128)S(1)}, u32[]{:S(2)}, u32[]{:S(2)}) collective-permute-start(f32[2,5,16,128]{3,2,1,0:T(8,128)S(1)} %residual.1.res_ref), channel_id=1, source_target_pairs={{0,128},{64,192},{128,0},{192,64},{1,129},{65,193},{129,1},{193,65... | collective-permute-start | bytes 245768 | tf_op jit(solution)/shard_map/ppermute | solution.py:19
  59.3 2.9 %collective-permute-start.7 = (f32[2,5,16,128]{3,2,1,0:T(8,128)S(1)}, f32[2,5,16,128]{3,2,1,0:T(8,128)S(1)}, u32[]{:S(2)}, u32[]{:S(2)}) collective-permute-start(f32[2,5,16,128]{3,2,1,0:T(8,128)S(1)} %residual.1.res_ref), channel_id=1, source_target_pairs={{0,192},{64,0},{128,64},{192,128},{1,193},{65,1},{129,65},{193,129... | collective-permute-start | bytes 245768 | tf_op jit(solution)/shard_map/ppermute | solution.py:19
  62.4 1.9 %collective-permute-done.8.far_ref = f32[2,5,16,128]{3,2,1,0:T(8,128)S(1)} collective-permute-done((f32[2,5,16,128]{3,2,1,0:T(8,128)S(1)}, f32[2,5,16,128]{3,2,1,0:T(8,128)S(1)}, u32[]{:S(2)}, u32[]{:S(2)}) %collective-permute-start.8) | collective-permute-done | bytes 81952 | tf_op jit(solution)/shard_map/ppermute | solution.py:19
  64.3 2.4 %collective-permute-done.6.prev_ref = f32[2,5,16,128]{3,2,1,0:T(8,128)S(1)} collective-permute-done((f32[2,5,16,128]{3,2,1,0:T(8,128)S(1)}, f32[2,5,16,128]{3,2,1,0:T(8,128)S(1)}, u32[]{:S(2)}, u32[]{:S(2)}) %collective-permute-start.6) | collective-permute-done | bytes 81952 | tf_op jit(solution)/shard_map/ppermute | solution.py:19
  66.7 2.2 %sweeps.1 = f32[5,2,16,128]{3,2,1,0:T(8,128)} custom-call(f32[2,5,16,128]{3,2,1,0:T(8,128)S(1)} %residual.1.res_ref, f32[2,5,16,128]{3,2,1,0:T(8,128)S(1)} %collective-permute-done.6.prev_ref, f32[2,5,16,128]{3,2,1,0:T(8,128)S(1)} %collective-permute-done.7.next_ref, f32[2,5,16,128]{3,2,1,0:T(8,128)S(1)} %collective-permute-done.8.far_ref, ...), custom_call_target="tpu_custom_call" | custom-call | tf_op jit(solution)/shard_map/sweeps/pallas_call | solution.py:287
  (34 shorter events, 2.0 us)
Async XLA Ops:
  0.0 0.9 %copy-start = (f32[5,2,16,128]{3,2,1,0:T(8,128)S(1)}, f32[5,2,16,128]{3,2,1,0:T(8,128)}, u32[]{:S(2)}) copy-start(f32[5,2,16,128]{3,2,1,0:T(8,128)} %param.11) | copy-start | bytes 245764
  0.9 0.8 %copy-start.5 = (s32[1,1,1,64,256]{4,3,2,1,0:T(8,128)S(1)}, s32[1,1,1,64,256]{4,3,2,1,0:T(8,128)}, u32[]{:S(2)}) copy-start(s32[1,1,1,64,256]{4,3,2,1,0:T(8,128)} %param.17) | copy-start | bytes 196612
  2.4 51.0 %copy-start.11 = (f32[7,5,5]{2,0,1:T(8,128)S(1)}, f32[7,5,5]{2,0,1:T(8,128)}, u32[]{:S(2)}) copy-start(f32[7,5,5]{2,0,1:T(8,128)} %param.15) | copy-start | bytes 2104
  2.4 54.5 %copy-start.2 = (f32[5,2,16,128]{3,2,1,0:T(8,128)S(1)}, f32[5,2,16,128]{3,2,1,0:T(8,128)}, u32[]{:S(2)}) copy-start(f32[5,2,16,128]{3,2,1,0:T(8,128)} %source_ref.1) | copy-start | bytes 245764
  2.4 54.5 %copy-start.3 = (f32[5,2,16,128]{3,2,1,0:T(8,128)S(1)}, f32[5,2,16,128]{3,2,1,0:T(8,128)}, u32[]{:S(2)}) copy-start(f32[5,2,16,128]{3,2,1,0:T(8,128)} %scale_ref.1) | copy-start | bytes 245764
  2.4 54.5 %copy-start.4 = (s32[2,16,128]{2,1,0:T(8,128)S(1)}, s32[2,16,128]{2,1,0:T(8,128)}, u32[]{:S(2)}) copy-start(s32[2,16,128]{2,1,0:T(8,128)} %fluid_ref.3) | copy-start | bytes 49156
  2.4 59.9 %copy-start.10 = (f32[5,5,2,16,128]{4,3,2,1,0:T(8,128)S(1)}, f32[5,5,2,16,128]{4,3,2,1,0:T(8,128)}, u32[]{:S(2)}) copy-start(f32[5,5,2,16,128]{4,3,2,1,0:T(8,128)} %param.14) | copy-start | bytes 1228804
  7.1 26.2 %all-to-all-start = ((f32[64,1,1280]{2,1,0:T(1,128)}), f32[64,1,1280]{2,1,0:T(1,128)S(1)}, u32[]{:S(2)}, u32[]{:S(2)}) async-start(f32[64,1,1280]{2,1,0:T(1,128)} %donor_pick.1), calls=%async_computation | async-start | bytes 655360 | tf_op jit(solution)/shard_map/all_to_all | solution.py:257
  19.3 43.0 %collective-permute-start.9 = (f32[5,5,2,16,128]{4,3,2,1,0:T(8,128)}, f32[5,5,2,16,128]{4,3,2,1,0:T(8,128)S(1)}, u32[]{:S(2)}, u32[]{:S(2)}) collective-permute-start(f32[5,5,2,16,128]{4,3,2,1,0:T(8,128)} %param.14), channel_id=1, source_target_pairs={{0,192},{64,0},{128,64},{192,128},{1,193},{65,1},{129,65},{193,129... | collective-permute-start | bytes 1228808 | tf_op jit(solution)/shard_map/ppermute | solution.py:19
  19.9 42.4 %collective-permute-start.11 = (f32[5,5,2,16,128]{4,3,2,1,0:T(8,128)}, f32[5,5,2,16,128]{4,3,2,1,0:T(8,128)S(1)}, u32[]{:S(2)}, u32[]{:S(2)}) collective-permute-start(f32[5,5,2,16,128]{4,3,2,1,0:T(8,128)} %param.14), channel_id=1, source_target_pairs={{0,64},{64,128},{128,192},{192,0},{1,65},{65,129},{129,193},{193,1... | collective-permute-start | bytes 1228808 | tf_op jit(solution)/shard_map/ppermute | solution.py:19
  21.4 40.9 %collective-permute-start.10 = (f32[5,5,2,16,128]{4,3,2,1,0:T(8,128)}, f32[5,5,2,16,128]{4,3,2,1,0:T(8,128)S(1)}, u32[]{:S(2)}, u32[]{:S(2)}) collective-permute-start(f32[5,5,2,16,128]{4,3,2,1,0:T(8,128)} %param.14), channel_id=1, source_target_pairs={{0,128},{64,192},{128,0},{192,64},{1,129},{65,193},{129,1},{193,65... | collective-permute-start | bytes 1228808 | tf_op jit(solution)/shard_map/ppermute | solution.py:19
  33.3 0.9 %copy-start.1 = (f32[5,2,16,128]{3,2,1,0:T(8,128)S(1)}, f32[5,2,16,128]{3,2,1,0:T(8,128)}, u32[]{:S(2)}) copy-start(f32[5,2,16,128]{3,2,1,0:T(8,128)} %param.11) | copy-start | bytes 245764
  34.2 0.8 %copy-start.6 = (s32[1,1,1,1024,8]{3,4,2,1,0:T(8,128)S(1)}, s32[1,1,1,1024,8]{3,4,2,1,0:T(8,128)}, u32[]{:S(2)}) copy-start(s32[1,1,1,1024,8]{3,4,2,1,0:T(8,128)} %param.20) | copy-start | bytes 98308
  34.9 0.8 %copy-start.7 = (f32[1,1,1,1024,8]{3,4,2,1,0:T(8,128)S(1)}, f32[1,1,1,1024,8]{3,4,2,1,0:T(8,128)}, u32[]{:S(2)}) copy-start(f32[1,1,1,1024,8]{3,4,2,1,0:T(8,128)} %param.21) | copy-start | bytes 98308
  35.7 0.7 copy-start.8
  41.5 3.7 %collective-permute-start.5 = (f32[10,128]{1,0:T(8,128)S(1)}, f32[10,128]{1,0:T(8,128)S(1)}, u32[]{:S(2)}, u32[]{:S(2)}) collective-permute-start(f32[10,128]{1,0:T(8,128)S(1)} %get-tuple-element.15), channel_id=1, source_target_pairs={{0,7},{1,0},{2,1},{3,2},{4,3},{5,4},{6,5},{7,6},{8,15},{9,8},{10,9... | collective-permute-start | bytes 15368 | tf_op jit(solution)/shard_map/ppermute | solution.py:19
  43.7 4.9 %collective-permute-start.4 = (f32[10,128]{1,0:T(8,128)S(1)}, f32[10,128]{1,0:T(8,128)S(1)}, u32[]{:S(2)}, u32[]{:S(2)}) collective-permute-start(f32[10,128]{1,0:T(8,128)S(1)} %get-tuple-element.16), channel_id=1, source_target_pairs={{0,1},{1,2},{2,3},{3,4},{4,5},{5,6},{6,7},{7,0},{8,9},{9,10},{10,1... | collective-permute-start | bytes 15368 | tf_op jit(solution)/shard_map/ppermute | solution.py:19
  45.2 3.4 %collective-permute-start.3 = (f32[10,128]{1,0:T(8,128)S(1)}, f32[10,128]{1,0:T(8,128)S(1)}, u32[]{:S(2)}, u32[]{:S(2)}) collective-permute-start(f32[10,128]{1,0:T(8,128)S(1)} %get-tuple-element.17), channel_id=1, source_target_pairs={{0,56},{8,0},{16,8},{24,16},{32,24},{40,32},{48,40},{56,48},{1,57}... | collective-permute-start | bytes 15368 | tf_op jit(solution)/shard_map/ppermute | solution.py:19
  48.6 4.3 %collective-permute-start.2 = (f32[10,128]{1,0:T(8,128)S(1)}, f32[10,128]{1,0:T(8,128)S(1)}, u32[]{:S(2)}, u32[]{:S(2)}) collective-permute-start(f32[10,128]{1,0:T(8,128)S(1)} %get-tuple-element.18), channel_id=1, source_target_pairs={{0,8},{8,16},{16,24},{24,32},{32,40},{40,48},{48,56},{56,0},{1,9},... | collective-permute-start | bytes 15368 | tf_op jit(solution)/shard_map/ppermute | solution.py:19
  48.6 4.8 %collective-permute-start = (f32[5,16,128]{2,1,0:T(8,128)S(1)}, f32[5,16,128]{2,1,0:T(8,128)S(1)}, u32[]{:S(2)}, u32[]{:S(2)}) collective-permute-start(f32[5,16,128]{2,1,0:T(8,128)S(1)} %get-tuple-element.11), channel_id=1, source_target_pairs={{0,64},{64,128},{128,192},{192,0},{1,65},{65,129},{129,193},{193,1... | collective-permute-start | bytes 122888 | tf_op jit(solution)/shard_map/ppermute | solution.py:19
  52.9 4.0 %collective-permute-start.1 = (f32[5,16,128]{2,1,0:T(8,128)S(1)}, f32[5,16,128]{2,1,0:T(8,128)S(1)}, u32[]{:S(2)}, u32[]{:S(2)}) collective-permute-start(f32[5,16,128]{2,1,0:T(8,128)S(1)} %get-tuple-element.12), channel_id=1, source_target_pairs={{0,192},{64,0},{128,64},{192,128},{1,193},{65,1},{129,65},{193,129... | collective-permute-start | bytes 122888 | tf_op jit(solution)/shard_map/ppermute | solution.py:19
  58.3 6.0 %collective-permute-start.8 = (f32[2,5,16,128]{3,2,1,0:T(8,128)S(1)}, f32[2,5,16,128]{3,2,1,0:T(8,128)S(1)}, u32[]{:S(2)}, u32[]{:S(2)}) collective-permute-start(f32[2,5,16,128]{3,2,1,0:T(8,128)S(1)} %residual.1.res_ref), channel_id=1, source_target_pairs={{0,128},{64,192},{128,0},{192,64},{1,129},{65,193},{129,1},{193,65... | collective-permute-start | bytes 245768 | tf_op jit(solution)/shard_map/ppermute | solution.py:19
  59.3 5.0 %collective-permute-start.7 = (f32[2,5,16,128]{3,2,1,0:T(8,128)S(1)}, f32[2,5,16,128]{3,2,1,0:T(8,128)S(1)}, u32[]{:S(2)}, u32[]{:S(2)}) collective-permute-start(f32[2,5,16,128]{3,2,1,0:T(8,128)S(1)} %residual.1.res_ref), channel_id=1, source_target_pairs={{0,192},{64,0},{128,64},{192,128},{1,193},{65,1},{129,65},{193,129... | collective-permute-start | bytes 245768 | tf_op jit(solution)/shard_map/ppermute | solution.py:19
  62.3 4.4 %collective-permute-start.6 = (f32[2,5,16,128]{3,2,1,0:T(8,128)S(1)}, f32[2,5,16,128]{3,2,1,0:T(8,128)S(1)}, u32[]{:S(2)}, u32[]{:S(2)}) collective-permute-start(f32[2,5,16,128]{3,2,1,0:T(8,128)S(1)} %residual.1.res_ref), channel_id=1, source_target_pairs={{0,64},{64,128},{128,192},{192,0},{1,65},{65,129},{129,193},{193,1... | collective-permute-start | bytes 245768 | tf_op jit(solution)/shard_map/ppermute | solution.py:19
  (1 other events, 0.7 us)

commit v2 on v1

--- a/solution.py
+++ b/solution.py
@@ -34,7 +34,23 @@
     return jnp.take_along_axis(rows, lane, axis=1, mode="promise_in_bounds")
 
 
-def donor_kernel(idx_ref, count_ref, state_ref, out_ref):
+def donor_kernel(
+    idx_hbm, count_hbm, state_hbm, out_ref, idx_ref, count_ref, state_ref, sems
+):
+    moves = [
+        pltpu.make_async_copy(src, dst, sems.at[n])
+        for n, (src, dst) in enumerate(
+            (
+                (count_hbm, count_ref),
+                (state_hbm, state_ref),
+                (idx_hbm, idx_ref),
+            )
+        )
+    ]
+    for move in moves:
+        move.start()
+    for move in moves:
+        move.wait()
     lanes = lax.broadcasted_iota(jnp.int32, (8, LANES), 1)
     subs = lax.broadcasted_iota(jnp.int32, (8, LANES), 0)
 
@@ -61,6 +77,12 @@
         return carry
 
     lax.fori_loop(0, 8, body, 0)
+
+
+def stage_kernel(*refs):
+    half = len(refs) // 2
+    for src, dst in zip(refs[:half], refs[half:]):
+        dst[...] = src[...]
 
 
 def ghost_kernel(
@@ -247,17 +269,38 @@
     ghost_weight,
 ):
     table = state.reshape(160, LANES)
-    sent = call(
+    sent = pl.pallas_call(
         donor_kernel,
-        jax.ShapeDtypeStruct((64, 1, 1280), F32),
-        (donor_index.reshape(64, 256), donor_count.reshape(1, 64), table),
-        [VMEM, SMEM, VMEM],
-        "donor_pick",
+        out_shape=jax.ShapeDtypeStruct((64, 1, 1280), F32),
+        in_specs=[pl.BlockSpec(memory_space=pl.ANY)] * 3,
+        out_specs=VMEM,
+        scratch_shapes=[
+            pltpu.VMEM((64, 256), jnp.int32),
+            pltpu.SMEM((1, 64), jnp.int32),
+            pltpu.VMEM((160, LANES), F32),
+            pltpu.SemaphoreType.DMA((3,)),
+        ],
+        name="donor_pick",
+        compiler_params=pltpu.CompilerParams(vmem_limit_bytes=60 << 20),
+    )(donor_index.reshape(64, 256), donor_count.reshape(1, 64), table)
+    lists = (
+        ghost_source.reshape(1024, 8).T,
+        ghost_weight.reshape(1024, 8).T,
+        ghost_cell.reshape(1, 1024),
+        table,
+    )
+    entries, weights, cells, table = call(
+        stage_kernel,
+        tuple(jax.ShapeDtypeStruct(x.shape, x.dtype) for x in lists),
+        lists,
+        [VMEM] * 4,
+        "stage_lists",
     )
     received = lax.all_to_all(sent, ("cy", "cz"), split_axis=0, concat_axis=0, tiled=True)
-    inv = jnp.stack(
-        [diag_inverse] + [ring(diag_inverse, "stream", step) for step in (-1, 2, 1)]
-    )
+    inv_prev = ring(diag_inverse, "stream", 1)
+    inv_next = ring(diag_inverse, "stream", -1)
+    received, inv_prev, inv_next = lax.optimization_barrier((received, inv_prev, inv_next))
+    far_a, far_b = ring(inv_prev[:3], "stream", 1), ring(inv_next[3:], "stream", -1)
     plane = jax.ShapeDtypeStruct((5, 16, LANES), F32)
     faces = jax.ShapeDtypeStruct((2, 10, LANES), F32)
     filled, first, last, yface, zface = call(
@@ -265,14 +308,18 @@
         (jax.ShapeDtypeStruct((160, LANES), F32), plane, plane, faces, faces),
         (
             received,
-            ghost_source.reshape(1024, 8).T,
-            ghost_weight.reshape(1024, 8).T,
-            ghost_cell.reshape(1, 1024),
+            entries,
+            weights,
+            cells,
             table,
         ),
         [VMEM] * 5,
         "ghost_fill",
     )
+    filled, first, last, yface, zface, far_a, far_b = lax.optimization_barrier(
+        (filled, first, last, yface, zface, far_a, far_b)
+    )
+    inv = jnp.stack([diag_inverse, inv_next, jnp.concatenate([far_a, far_b]), inv_prev])
     xm, xp = ring(last, "stream", 1), ring(first, "stream", -1)
     ym, yp = ring(yface[1], "cy", 1), ring(yface[0], "cy", -1)
     zm, zp = ring(zface[1], "cz", 1), ring(zface[0], "cz", -1)

time: 69.3 us -> 64.7 us (0.934)
  the two profiles are of different devices: /device:TPU:4 before, /device:TPU:32 now
where the time goes in v2:
time: 64.7 us; the launch traced here: 63.7 us
  starting transfers between devices  29.9 us (46%)
  waiting for transfers between devices  19.6 us (30%)
  Pallas kernels  13.8 us (21%)
    ppermute x13, waiting for transfers between devices, ring(): lax.ppermute(x, axis, [(i, (i + steps) % count) for i in range(count)])  18.8 us
    ppermute x13, starting transfers between devices, ring(): lax.ppermute(x, axis, [(i, (i + steps) % count) for i in range(count)])  18 us
    all_to_all x1, starting transfers between devices, on_device(): lax.all_to_all(sent, ('cy', 'cz'), split_axis=0, concat_axis=0, tiled=True)  11.9 us
    pallas_call x3, Pallas kernels, call(): pl.pallas_call(kernel, out_shape=outs, in_specs=specs, out_specs=jax.tree...  6.51 us
    pallas_call x1, Pallas kernels, on_device(): pl.pallas_call(donor_kernel, out_shape=jax.ShapeDtypeStruct((64, 1, 1280)...  5.08 us
    pallas_call x1, Pallas kernels, on_device(): pl.pallas_call(sweep_kernel, out_shape=jax.ShapeDtypeStruct((5, 2, 16, LA...  2.19 us
  transfers between devices with their start and end apart: 14, of which 9 were waited for; matrix products, arithmetic and copies ran while one was open for 0% of the time, Pallas kernels for 8%

profile of v2, /device:TPU:32, one launch (start us, length us, event | category | flops | bytes accessed | tf_op | source)
XLA Modules:
  0.0 63.7 jit_solution(7772967540964374982)
XLA Ops:
  0.0 5.1 %donor_pick.1 = f32[64,1,1280]{2,1,0:T(1,128)} custom-call(s32[64,256]{1,0:T(8,128)} %bitcast.31, s32[1,64]{1,0:T(1,128)} %bitcast.32, f32[160,128]{1,0:T(8,128)} %bitcast.23), custom_call_target="tpu_custom_call" | custom-call | tf_op jit(solution)/shard_map/donor_pick/pallas_call | solution.py:272
  5.2 11.9 %all-to-all-start = ((f32[64,1,1280]{2,1,0:T(1,128)}), f32[64,1,1280]{2,1,0:T(1,128)S(1)}, u32[]{:S(2)}, u32[]{:S(2)}) async-start(f32[64,1,1280]{2,1,0:T(1,128)} %donor_pick.1), calls=%async_computation | async-start | bytes 655360 | tf_op jit(solution)/shard_map/all_to_all | solution.py:299
  17.1 1.6 %collective-permute-start = (f32[5,5,2,16,128]{4,3,2,1,0:T(8,128)}, f32[5,5,2,16,128]{4,3,2,1,0:T(8,128)S(1)}, u32[]{:S(2)}, u32[]{:S(2)}) collective-permute-start(f32[5,5,2,16,128]{4,3,2,1,0:T(8,128)} %param.14), channel_id=1, source_target_pairs={{0,64},{64,128},{128,192},{192,0},{1,65},{65,129},{129,193},{193,1... | collective-permute-start | bytes 1228808 | tf_op jit(solution)/shard_map/ppermute | solution.py:19
  18.6 1.7 %collective-permute-start.1 = (f32[5,5,2,16,128]{4,3,2,1,0:T(8,128)}, f32[5,5,2,16,128]{4,3,2,1,0:T(8,128)S(1)}, u32[]{:S(2)}, u32[]{:S(2)}) collective-permute-start(f32[5,5,2,16,128]{4,3,2,1,0:T(8,128)} %param.14), channel_id=1, source_target_pairs={{0,192},{64,0},{128,64},{192,128},{1,193},{65,1},{129,65},{193,129... | collective-permute-start | bytes 1228808 | tf_op jit(solution)/shard_map/ppermute | solution.py:19
  20.4 9.7 %collective-permute-done = f32[5,5,2,16,128]{4,3,2,1,0:T(8,128)S(1)} collective-permute-done((f32[5,5,2,16,128]{4,3,2,1,0:T(8,128)}, f32[5,5,2,16,128]{4,3,2,1,0:T(8,128)S(1)}, u32[]{:S(2)}, u32[]{:S(2)}) %collective-permute-start) | collective-permute-done | bytes 409632 | tf_op jit(solution)/shard_map/ppermute | solution.py:19
  30.1 0.9 %all-to-all-done.rec_ref = f32[64,1,1280]{2,1,0:T(1,128)S(1)} async-done(((f32[64,1,1280]{2,1,0:T(1,128)}), f32[64,1,1280]{2,1,0:T(1,128)S(1)}, u32[]{:S(2)}, u32[]{:S(2)}) %all-to-all-start) | async-done | bytes 327712 | tf_op jit(solution)/shard_map/all_to_all | solution.py:299
  31.0 1.6 %collective-permute-start.2 = (f32[3,5,2,16,128]{4,3,2,1,0:T(8,128)S(1)}, f32[3,5,2,16,128]{4,3,2,1,0:T(8,128)S(1)}, u32[]{:S(2)}, u32[]{:S(2)}) collective-permute-start(f32[3,5,2,16,128]{4,3,2,1,0:T(8,128)S(1)} %slice.18), channel_id=1, source_target_pairs={{0,64},{64,128},{128,192},{192,0},{1,65},{65,129},{129,193},{193,1... | collective-permute-start | bytes 737288 | tf_op jit(solution)/shard_map/ppermute | solution.py:19
  32.6 1.8 %collective-permute-start.3 = (f32[2,5,2,16,128]{4,3,2,1,0:T(8,128)S(1)}, f32[2,5,2,16,128]{4,3,2,1,0:T(8,128)S(1)}, u32[]{:S(2)}, u32[]{:S(2)}) collective-permute-start(f32[2,5,2,16,128]{4,3,2,1,0:T(8,128)S(1)} %slice.19), channel_id=1, source_target_pairs={{0,192},{64,0},{128,64},{192,128},{1,193},{65,1},{129,65},{193,129... | collective-permute-start | bytes 491528 | tf_op jit(solution)/shard_map/ppermute | solution.py:19
  34.5 5.1 %ghost_fill.1 = (f32[160,128]{1,0:T(8,128)S(1)}, f32[5,16,128]{2,1,0:T(8,128)S(1)}, f32[5,16,128]{2,1,0:T(8,128)S(1)}, f32[2,10,128]{2,1,0:T(8,128)S(1)}, f32[2,10,128]{2,1,0:T(8,128)S(1)}) custom-call(f32[64,1,1280]{2,1,0:T(1,128)S(1)} %all-to-all-done.rec_ref, s32[8,1024]{1,0:T(8,128)S(1)} %get-tuple-element.25.src_ref, ...), custom_call_target="tpu_custom_call" | custom-call | tf_op jit(solution)/shard_map/ghost_fill/pallas_call | solution.py:23
  39.6 0.3 collective-permute-start.4
  39.9 3.0 %collective-permute-start.5 = (f32[5,16,128]{2,1,0:T(8,128)S(1)}, f32[5,16,128]{2,1,0:T(8,128)S(1)}, u32[]{:S(2)}, u32[]{:S(2)}) collective-permute-start(f32[5,16,128]{2,1,0:T(8,128)S(1)} %get-tuple-element.38), channel_id=1, source_target_pairs={{0,192},{64,0},{128,64},{192,128},{1,193},{65,1},{129,65},{193,129... | collective-permute-start | bytes 122888 | tf_op jit(solution)/shard_map/ppermute | solution.py:19
  42.9 3.0 %collective-permute-start.7 = (f32[10,128]{1,0:T(8,128)S(1)}, f32[10,128]{1,0:T(8,128)S(1)}, u32[]{:S(2)}, u32[]{:S(2)}) collective-permute-start(f32[10,128]{1,0:T(8,128)S(1)} %get-tuple-element.45), channel_id=1, source_target_pairs={{0,56},{8,0},{16,8},{24,16},{32,24},{40,32},{48,40},{56,48},{1,57}... | collective-permute-start | bytes 15368 | tf_op jit(solution)/shard_map/ppermute | solution.py:19
  45.9 1.0 %collective-permute-start.8 = (f32[10,128]{1,0:T(8,128)S(1)}, f32[10,128]{1,0:T(8,128)S(1)}, u32[]{:S(2)}, u32[]{:S(2)}) collective-permute-start(f32[10,128]{1,0:T(8,128)S(1)} %get-tuple-element.44), channel_id=1, source_target_pairs={{0,1},{1,2},{2,3},{3,4},{4,5},{5,6},{6,7},{7,0},{8,9},{9,10},{10,1... | collective-permute-start | bytes 15368 | tf_op jit(solution)/shard_map/ppermute | solution.py:19
  46.9 0.3 collective-permute-done.6.ym_ref
  47.2 0.7 %collective-permute-start.9 = (f32[10,128]{1,0:T(8,128)S(1)}, f32[10,128]{1,0:T(8,128)S(1)}, u32[]{:S(2)}, u32[]{:S(2)}) collective-permute-start(f32[10,128]{1,0:T(8,128)S(1)} %get-tuple-element.43), channel_id=1, source_target_pairs={{0,7},{1,0},{2,1},{3,2},{4,3},{5,4},{6,5},{7,6},{8,15},{9,8},{10,9... | collective-permute-start | bytes 15368 | tf_op jit(solution)/shard_map/ppermute | solution.py:19
  47.9 1.6 %collective-permute-done.8.zm_ref = f32[10,128]{1,0:T(8,128)S(1)} collective-permute-done((f32[10,128]{1,0:T(8,128)S(1)}, f32[10,128]{1,0:T(8,128)S(1)}, u32[]{:S(2)}, u32[]{:S(2)}) %collective-permute-start.8) | collective-permute-done | bytes 5152 | tf_op jit(solution)/shard_map/ppermute | solution.py:19
  49.5 1.3 %collective-permute-done.9.zp_ref = f32[10,128]{1,0:T(8,128)S(1)} collective-permute-done((f32[10,128]{1,0:T(8,128)S(1)}, f32[10,128]{1,0:T(8,128)S(1)}, u32[]{:S(2)}, u32[]{:S(2)}) %collective-permute-start.9) | collective-permute-done | bytes 5152 | tf_op jit(solution)/shard_map/ppermute | solution.py:19
  50.9 1.4 %residual.1.res_ref = f32[2,5,16,128]{3,2,1,0:T(8,128)S(1)} custom-call(f32[160,128]{1,0:T(8,128)S(1)} %get-tuple-element.36.f_ref, f32[5,16,128]{2,1,0:T(8,128)S(1)} %collective-permute-done.4.xm_ref, f32[5,16,128]{2,1,0:T(8,128)S(1)} %collective-permute-done.5.xp_ref, f32[10,128]{1,0:T(8,128)S(1)} %collective-permute-done.6.ym_ref, ...), custom_call_target="tpu_custom_call" | custom-call | tf_op jit(solution)/shard_map/residual/pallas_call | solution.py:23
  52.4 3.2 %collective-permute-start.11 = (f32[2,5,16,128]{3,2,1,0:T(8,128)S(1)}, f32[2,5,16,128]{3,2,1,0:T(8,128)S(1)}, u32[]{:S(2)}, u32[]{:S(2)}) collective-permute-start(f32[2,5,16,128]{3,2,1,0:T(8,128)S(1)} %residual.1.res_ref), channel_id=1, source_target_pairs={{0,192},{64,0},{128,64},{192,128},{1,193},{65,1},{129,65},{193,129... | collective-permute-start | bytes 245768 | tf_op jit(solution)/shard_map/ppermute | solution.py:19
  55.6 0.1 pad_maximum_fusion.inv_ref
  55.7 2.5 %collective-permute-done.10.prev_ref = f32[2,5,16,128]{3,2,1,0:T(8,128)S(1)} collective-permute-done((f32[2,5,16,128]{3,2,1,0:T(8,128)S(1)}, f32[2,5,16,128]{3,2,1,0:T(8,128)S(1)}, u32[]{:S(2)}, u32[]{:S(2)}) %collective-permute-start.10) | collective-permute-done | bytes 81952 | tf_op jit(solution)/shard_map/ppermute | solution.py:19
  58.2 0.3 collective-permute-done.11.next_ref
  58.5 3.1 %collective-permute-done.12.far_ref = f32[2,5,16,128]{3,2,1,0:T(8,128)S(1)} collective-permute-done((f32[2,5,16,128]{3,2,1,0:T(8,128)S(1)}, f32[2,5,16,128]{3,2,1,0:T(8,128)S(1)}, u32[]{:S(2)}, u32[]{:S(2)}) %collective-permute-start.12) | collective-permute-done | bytes 81952 | tf_op jit(solution)/shard_map/ppermute | solution.py:19
  61.5 2.2 %sweeps.1 = f32[5,2,16,128]{3,2,1,0:T(8,128)} custom-call(f32[2,5,16,128]{3,2,1,0:T(8,128)S(1)} %residual.1.res_ref, f32[2,5,16,128]{3,2,1,0:T(8,128)S(1)} %collective-permute-done.10.prev_ref, f32[2,5,16,128]{3,2,1,0:T(8,128)S(1)} %collective-permute-done.11.next_ref, f32[2,5,16,128]{3,2,1,0:T(8,128)S(1)} %collective-permute-done.12.far_ref, ...), custom_call_target="tpu_custom_call" | custom-call | tf_op jit(solution)/shard_map/sweeps/pallas_call | solution.py:334
  (34 shorter events, 0.3 us)
Async XLA Ops:
  0.0 34.4 %copy-start = (f32[5,2,16,128]{3,2,1,0:T(8,128)S(1)}, f32[5,2,16,128]{3,2,1,0:T(8,128)}, u32[]{:S(2)}) copy-start(f32[5,2,16,128]{3,2,1,0:T(8,128)} %param.11) | copy-start | bytes 245764
  0.0 34.4 %copy-start.8 = (f32[7,5,5]{2,0,1:T(8,128)S(1)}, f32[7,5,5]{2,0,1:T(8,128)}, u32[]{:S(2)}) copy-start(f32[7,5,5]{2,0,1:T(8,128)} %param.15) | copy-start | bytes 2104
  0.0 34.4 %copy-start.4 = (s32[1,1,1,1024,8]{3,4,2,1,0:T(8,128)S(1)}, s32[1,1,1,1024,8]{3,4,2,1,0:T(8,128)}, u32[]{:S(2)}) copy-start(s32[1,1,1,1024,8]{3,4,2,1,0:T(8,128)} %param.20) | copy-start | bytes 98308
  0.0 34.4 %copy-start.5 = (f32[1,1,1,1024,8]{3,4,2,1,0:T(8,128)S(1)}, f32[1,1,1,1024,8]{3,4,2,1,0:T(8,128)}, u32[]{:S(2)}) copy-start(f32[1,1,1,1024,8]{3,4,2,1,0:T(8,128)} %param.21) | copy-start | bytes 98308
  0.0 34.4 %copy-start.6 = (s32[1,1,1,1024]{3,2,1,0:T(1,128)S(1)}, s32[1,1,1,1024]{3,2,1,0:T(1,128)}, u32[]{:S(2)}) copy-start(s32[1,1,1,1024]{3,2,1,0:T(1,128)} %param.19) | copy-start | bytes 12292
  5.1 45.7 %copy-start.1 = (f32[5,2,16,128]{3,2,1,0:T(8,128)S(1)}, f32[5,2,16,128]{3,2,1,0:T(8,128)}, u32[]{:S(2)}) copy-start(f32[5,2,16,128]{3,2,1,0:T(8,128)} %source_ref.1) | copy-start | bytes 245764
  5.1 45.7 %copy-start.2 = (f32[5,2,16,128]{3,2,1,0:T(8,128)S(1)}, f32[5,2,16,128]{3,2,1,0:T(8,128)}, u32[]{:S(2)}) copy-start(f32[5,2,16,128]{3,2,1,0:T(8,128)} %scale_ref.1) | copy-start | bytes 245764
  5.1 45.7 %copy-start.3 = (s32[2,16,128]{2,1,0:T(8,128)S(1)}, s32[2,16,128]{2,1,0:T(8,128)}, u32[]{:S(2)}) copy-start(s32[2,16,128]{2,1,0:T(8,128)} %fluid_ref.3) | copy-start | bytes 49156
  5.2 50.4 %copy-start.7 = (f32[5,5,2,16,128]{4,3,2,1,0:T(8,128)S(1)}, f32[5,5,2,16,128]{4,3,2,1,0:T(8,128)}, u32[]{:S(2)}) copy-start(f32[5,5,2,16,128]{4,3,2,1,0:T(8,128)} %param.14) | copy-start | bytes 1228804
  5.2 25.8 %all-to-all-start = ((f32[64,1,1280]{2,1,0:T(1,128)}), f32[64,1,1280]{2,1,0:T(1,128)S(1)}, u32[]{:S(2)}, u32[]{:S(2)}) async-start(f32[64,1,1280]{2,1,0:T(1,128)} %donor_pick.1), calls=%async_computation | async-start | bytes 655360 | tf_op jit(solution)/shard_map/all_to_all | solution.py:299
  17.1 13.0 %collective-permute-start = (f32[5,5,2,16,128]{4,3,2,1,0:T(8,128)}, f32[5,5,2,16,128]{4,3,2,1,0:T(8,128)S(1)}, u32[]{:S(2)}, u32[]{:S(2)}) collective-permute-start(f32[5,5,2,16,128]{4,3,2,1,0:T(8,128)} %param.14), channel_id=1, source_target_pairs={{0,64},{64,128},{128,192},{192,0},{1,65},{65,129},{129,193},{193,1... | collective-permute-start | bytes 1228808 | tf_op jit(solution)/shard_map/ppermute | solution.py:19
  18.6 11.5 %collective-permute-start.1 = (f32[5,5,2,16,128]{4,3,2,1,0:T(8,128)}, f32[5,5,2,16,128]{4,3,2,1,0:T(8,128)S(1)}, u32[]{:S(2)}, u32[]{:S(2)}) collective-permute-start(f32[5,5,2,16,128]{4,3,2,1,0:T(8,128)} %param.14), channel_id=1, source_target_pairs={{0,192},{64,0},{128,64},{192,128},{1,193},{65,1},{129,65},{193,129... | collective-permute-start | bytes 1228808 | tf_op jit(solution)/shard_map/ppermute | solution.py:19
  31.0 8.7 %collective-permute-start.2 = (f32[3,5,2,16,128]{4,3,2,1,0:T(8,128)S(1)}, f32[3,5,2,16,128]{4,3,2,1,0:T(8,128)S(1)}, u32[]{:S(2)}, u32[]{:S(2)}) collective-permute-start(f32[3,5,2,16,128]{4,3,2,1,0:T(8,128)S(1)} %slice.18), channel_id=1, source_target_pairs={{0,64},{64,128},{128,192},{192,0},{1,65},{65,129},{129,193},{193,1... | collective-permute-start | bytes 737288 | tf_op jit(solution)/shard_map/ppermute | solution.py:19
  32.6 7.0 %collective-permute-start.3 = (f32[2,5,2,16,128]{4,3,2,1,0:T(8,128)S(1)}, f32[2,5,2,16,128]{4,3,2,1,0:T(8,128)S(1)}, u32[]{:S(2)}, u32[]{:S(2)}) collective-permute-start(f32[2,5,2,16,128]{4,3,2,1,0:T(8,128)S(1)} %slice.19), channel_id=1, source_target_pairs={{0,192},{64,0},{128,64},{192,128},{1,193},{65,1},{129,65},{193,129... | collective-permute-start | bytes 491528 | tf_op jit(solution)/shard_map/ppermute | solution.py:19
  39.6 11.2 %collective-permute-start.4 = (f32[5,16,128]{2,1,0:T(8,128)S(1)}, f32[5,16,128]{2,1,0:T(8,128)S(1)}, u32[]{:S(2)}, u32[]{:S(2)}) collective-permute-start(f32[5,16,128]{2,1,0:T(8,128)S(1)} %get-tuple-element.37), channel_id=1, source_target_pairs={{0,64},{64,128},{128,192},{192,0},{1,65},{65,129},{129,193},{193,1... | collective-permute-start | bytes 122888 | tf_op jit(solution)/shard_map/ppermute | solution.py:19
  39.9 10.9 %collective-permute-start.5 = (f32[5,16,128]{2,1,0:T(8,128)S(1)}, f32[5,16,128]{2,1,0:T(8,128)S(1)}, u32[]{:S(2)}, u32[]{:S(2)}) collective-permute-start(f32[5,16,128]{2,1,0:T(8,128)S(1)} %get-tuple-element.38), channel_id=1, source_target_pairs={{0,192},{64,0},{128,64},{192,128},{1,193},{65,1},{129,65},{193,129... | collective-permute-start | bytes 122888 | tf_op jit(solution)/shard_map/ppermute | solution.py:19
  42.9 4.3 %collective-permute-start.6 = (f32[10,128]{1,0:T(8,128)S(1)}, f32[10,128]{1,0:T(8,128)S(1)}, u32[]{:S(2)}, u32[]{:S(2)}) collective-permute-start(f32[10,128]{1,0:T(8,128)S(1)} %get-tuple-element.46), channel_id=1, source_target_pairs={{0,8},{8,16},{16,24},{24,32},{32,40},{40,48},{48,56},{56,0},{1,9},... | collective-permute-start | bytes 15368 | tf_op jit(solution)/shard_map/ppermute | solution.py:19
  42.9 5.0 %collective-permute-start.7 = (f32[10,128]{1,0:T(8,128)S(1)}, f32[10,128]{1,0:T(8,128)S(1)}, u32[]{:S(2)}, u32[]{:S(2)}) collective-permute-start(f32[10,128]{1,0:T(8,128)S(1)} %get-tuple-element.45), channel_id=1, source_target_pairs={{0,56},{8,0},{16,8},{24,16},{32,24},{40,32},{48,40},{56,48},{1,57}... | collective-permute-start | bytes 15368 | tf_op jit(solution)/shard_map/ppermute | solution.py:19
  45.9 3.7 %collective-permute-start.8 = (f32[10,128]{1,0:T(8,128)S(1)}, f32[10,128]{1,0:T(8,128)S(1)}, u32[]{:S(2)}, u32[]{:S(2)}) collective-permute-start(f32[10,128]{1,0:T(8,128)S(1)} %get-tuple-element.44), channel_id=1, source_target_pairs={{0,1},{1,2},{2,3},{3,4},{4,5},{5,6},{6,7},{7,0},{8,9},{9,10},{10,1... | collective-permute-start | bytes 15368 | tf_op jit(solution)/shard_map/ppermute | solution.py:19
  47.2 3.7 %collective-permute-start.9 = (f32[10,128]{1,0:T(8,128)S(1)}, f32[10,128]{1,0:T(8,128)S(1)}, u32[]{:S(2)}, u32[]{:S(2)}) collective-permute-start(f32[10,128]{1,0:T(8,128)S(1)} %get-tuple-element.43), channel_id=1, source_target_pairs={{0,7},{1,0},{2,1},{3,2},{4,3},{5,4},{6,5},{7,6},{8,15},{9,8},{10,9... | collective-permute-start | bytes 15368 | tf_op jit(solution)/shard_map/ppermute | solution.py:19
  52.3 5.9 %collective-permute-start.10 = (f32[2,5,16,128]{3,2,1,0:T(8,128)S(1)}, f32[2,5,16,128]{3,2,1,0:T(8,128)S(1)}, u32[]{:S(2)}, u32[]{:S(2)}) collective-permute-start(f32[2,5,16,128]{3,2,1,0:T(8,128)S(1)} %residual.1.res_ref), channel_id=1, source_target_pairs={{0,64},{64,128},{128,192},{192,0},{1,65},{65,129},{129,193},{193,1... | collective-permute-start | bytes 245768 | tf_op jit(solution)/shard_map/ppermute | solution.py:19
  52.4 6.1 %collective-permute-start.11 = (f32[2,5,16,128]{3,2,1,0:T(8,128)S(1)}, f32[2,5,16,128]{3,2,1,0:T(8,128)S(1)}, u32[]{:S(2)}, u32[]{:S(2)}) collective-permute-start(f32[2,5,16,128]{3,2,1,0:T(8,128)S(1)} %residual.1.res_ref), channel_id=1, source_target_pairs={{0,192},{64,0},{128,64},{192,128},{1,193},{65,1},{129,65},{193,129... | collective-permute-start | bytes 245768 | tf_op jit(solution)/shard_map/ppermute | solution.py:19
  55.6 5.9 %collective-permute-start.12 = (f32[2,5,16,128]{3,2,1,0:T(8,128)S(1)}, f32[2,5,16,128]{3,2,1,0:T(8,128)S(1)}, u32[]{:S(2)}, u32[]{:S(2)}) collective-permute-start(f32[2,5,16,128]{3,2,1,0:T(8,128)S(1)} %residual.1.res_ref), channel_id=1, source_target_pairs={{0,128},{64,192},{128,0},{192,64},{1,129},{65,193},{129,1},{193,65... | collective-permute-start | bytes 245768 | tf_op jit(solution)/shard_map/ppermute | solution.py:19

commit v3 on v2

--- a/solution.py
+++ b/solution.py
@@ -86,7 +86,7 @@
 
 
 def ghost_kernel(
-    rec_ref, src_ref, w_ref, cell_ref, state_ref, f_ref, x0_ref, x1_ref, y_ref, z_ref
+    rec_ref, src_ref, w_ref, cell_ref, state_ref, f_ref, y_ref, z_ref
 ):
     tabs = []
     for v in range(5):
@@ -141,8 +141,6 @@
         old = state_ref[32 * v : 32 * v + 32, :]
         new = jnp.where(covered, hi + (mid + lo), old)
         f_ref[32 * v : 32 * v + 32, :] = new
-        x0_ref[v] = new[0:16]
-        x1_ref[v] = new[16:32]
         for x in range(2):
             plane = new[16 * x : 16 * x + 16]
             row = 2 * v + x
@@ -154,11 +152,12 @@
 
 
 def residual_kernel(
-    f_ref, xm_ref, xp_ref, ym_ref, yp_ref, zm_ref, zp_ref, source_ref, scale_ref, fluid_ref,
-    couple_ref, out_ref,
+    f_ref, ym_ref, yp_ref, zm_ref, zp_ref, source_ref, scale_ref, fluid_ref,
+    couple_ref, same_ref, other_ref,
 ):
     s, a, b = (lax.axis_index(n) for n in ("stream", "cy", "cz"))
-    ns, na, nb = (lax.axis_size(n) for n in ("stream", "cy", "cz"))
+    na, nb = (lax.axis_size(n) for n in ("cy", "cz"))
+    half = lax.rem(s, 2)
     shape = (16, LANES)
     subs = lax.broadcasted_iota(jnp.int32, shape, 0)
     lanes = lax.broadcasted_iota(jnp.int32, shape, 1)
@@ -175,17 +174,12 @@
             row = 2 * v + x
             mid = f_ref[32 * v + 16 * x : 32 * v + 16 * x + 16, :]
             other = f_ref[32 * v + 16 * (1 - x) : 32 * v + 16 * (1 - x) + 16, :]
-            if x == 0:
-                xm, xp = jnp.where(s > 0, xm_ref[v], 0.0), other
-            else:
-                xm, xp = other, jnp.where(s < ns - 1, xp_ref[v], 0.0)
             ym = jnp.where(a > 0, ym_ref[row : row + 1, :], 0.0)
             yp = jnp.where(a < na - 1, yp_ref[row : row + 1, :], 0.0)
             zm = jnp.where(b > 0, column(zm_ref, row), 0.0)
             zp = jnp.where(b < nb - 1, column(zp_ref, row), 0.0)
             near[0].append(mid)
-            near[1].append(xm)
-            near[2].append(xp)
+            near[2 - x].append(other)
             near[3].append(jnp.where(subs == 0, ym, pltpu.roll(mid, 1, 0)))
             near[4].append(jnp.where(subs == 15, yp, pltpu.roll(mid, 15, 0)))
             near[5].append(jnp.where(lanes == 0, zm, pltpu.roll(mid, 1, 1)))
@@ -193,45 +187,67 @@
         wet = fluid_ref[x].astype(F32)
         for i in range(5):
             image = scale_ref[i, x] * near[0][i]
-            for d in range(7):
+            for d in (0, 2 - x, 3, 4, 5, 6):
                 for j in range(5):
                     image = image + couple_ref[d, i, j] * near[d][j]
-            out_ref[x, i] = wet * (source_ref[i, x] - image)
+            res = wet * (source_ref[i, x] - image)
+            same_ref[x, i] = jnp.where(half == 0, res[0:8], res[8:16])
+            other_ref[x, i] = jnp.where(half == 0, res[8:16], res[0:8])
+            same_ref[2 + x, i] = jnp.where(half == 0, near[0][i][0:8], near[0][i][8:16])
+            other_ref[2 + x, i] = jnp.where(half == 0, near[0][i][8:16], near[0][i][0:8])
 
 
 def sweep_kernel(
-    res_ref, prev_ref, next_ref, far_ref, inv_ref, f_ref, fluid_ref, couple_ref, out_ref, low_ref
+    res_ref, prev_ref, next_ref, far_ref, inv_ref, couple_ref, mine_ref, theirs_ref, low_ref
 ):
     s = lax.axis_index("stream")
+    pair = s + 1 - 2 * lax.rem(s, 2)
     count = 4
-    zero = jnp.zeros((16, LANES), F32)
+    zero = jnp.zeros((8, LANES), F32)
+    offset = [lax.rem(q - s + count, count) for q in range(count)]
+
+    def block(q, k):
+        o = offset[q]
+        return [
+            jnp.where(
+                o == 0,
+                res_ref[k, i],
+                jnp.where(
+                    o == 1, next_ref[k, i], jnp.where(o == 2, far_ref[k, i], prev_ref[k, i])
+                ),
+            )
+            for i in range(5)
+        ]
+
     prev = [zero] * 5
     for q in range(count):
-        o = lax.rem(q - s + count, count)
+        o = offset[q]
         for x in range(2):
-            t = []
+            t = block(q, x)
+            wet = inv_ref[o, 25, x]
+            if x == 0 and q > 0:
+                prev = [p + wet * f for p, f in zip(prev, block(q - 1, 3))]
+            if x == 1 and q < count - 1:
+                ahead = block(q + 1, 2)
+                for i in range(5):
+                    c = couple_ref[2, i, 0] * ahead[0]
+                    for j in range(1, 5):
+                        c = c + couple_ref[2, i, j] * ahead[j]
+                    t[i] = t[i] - wet * c
             for i in range(5):
-                r = jnp.where(
-                    o == 0,
-                    res_ref[x, i],
-                    jnp.where(
-                        o == 1, next_ref[x, i], jnp.where(o == 2, far_ref[x, i], prev_ref[x, i])
-                    ),
-                )
                 for j in range(5):
-                    r = r - couple_ref[1, i, j] * prev[j]
-                t.append(r)
+                    t[i] = t[i] - couple_ref[1, i, j] * prev[j]
             cur = []
             for i in range(5):
-                c = inv_ref[o, i, 0, x] * t[0]
+                c = inv_ref[o, 5 * i, x] * t[0]
                 for j in range(1, 5):
-                    c = c + inv_ref[o, i, j, x] * t[j]
+                    c = c + inv_ref[o, 5 * i + j, x] * t[j]
                 cur.append(c)
                 low_ref[2 * q + x, i] = c
             prev = cur
     prev = [zero] * 5
     for q in reversed(range(count)):
-        o = lax.rem(q - s + count, count)
+        o = offset[q]
         for x in (1, 0):
             t = []
             for i in range(5):
@@ -243,16 +259,15 @@
             for i in range(5):
                 c = low_ref[2 * q + x, i]
                 for j in range(5):
-                    c = c - inv_ref[o, i, j, x] * t[j]
+                    c = c - inv_ref[o, 5 * i + j, x] * t[j]
                 cur.append(c)
             prev = cur
-
-            @pl.when(o == 0)
-            def _():
-                wet = RELAX * fluid_ref[x].astype(F32)
-                for i in range(5):
-                    at = 32 * i + 16 * x
-                    out_ref[i, x] = f_ref[at : at + 16, :] + wet * cur[i]
+            for where, to_ref in ((s, mine_ref), (pair, theirs_ref)):
+
+                @pl.when(where == q)
+                def _():
+                    for i in range(5):
+                        to_ref[i, x] = cur[i]
 
 
 def on_device(
@@ -297,15 +312,17 @@
         "stage_lists",
     )
     received = lax.all_to_all(sent, ("cy", "cz"), split_axis=0, concat_axis=0, tiled=True)
-    inv_prev = ring(diag_inverse, "stream", 1)
-    inv_next = ring(diag_inverse, "stream", -1)
-    received, inv_prev, inv_next = lax.optimization_barrier((received, inv_prev, inv_next))
-    far_a, far_b = ring(inv_prev[:3], "stream", 1), ring(inv_next[3:], "stream", -1)
-    plane = jax.ShapeDtypeStruct((5, 16, LANES), F32)
+    half = lax.rem(lax.axis_index("stream"), 2)
+    frozen = jnp.concatenate([diag_inverse.reshape(25, 2, 16, LANES), fluid.astype(F32)[None]])
+    inv_same, inv_other = (
+        lax.dynamic_slice_in_dim(frozen, 8 * h, 8, 2) for h in (half, 1 - half)
+    )
+    inv_prev, inv_next = ring(inv_other, "stream", 1), ring(inv_other, "stream", -1)
+    inv_far = ring(inv_same, "stream", 2)
     faces = jax.ShapeDtypeStruct((2, 10, LANES), F32)
-    filled, first, last, yface, zface = call(
+    filled, yface, zface = call(
         ghost_kernel,
-        (jax.ShapeDtypeStruct((160, LANES), F32), plane, plane, faces, faces),
+        (jax.ShapeDtypeStruct((160, LANES), F32), faces, faces),
         (
             received,
             entries,
@@ -316,30 +333,39 @@
         [VMEM] * 5,
         "ghost_fill",
     )
-    filled, first, last, yface, zface, far_a, far_b = lax.optimization_barrier(
-        (filled, first, last, yface, zface, far_a, far_b)
-    )
-    inv = jnp.stack([diag_inverse, inv_next, jnp.concatenate([far_a, far_b]), inv_prev])
-    xm, xp = ring(last, "stream", 1), ring(first, "stream", -1)
+    filled, yface, zface, inv_prev, inv_next, inv_far = lax.optimization_barrier(
+        (filled, yface, zface, inv_prev, inv_next, inv_far)
+    )
+    inv = jnp.stack([inv_same, inv_next, inv_far, inv_prev])
     ym, yp = ring(yface[1], "cy", 1), ring(yface[0], "cy", -1)
     zm, zp = ring(zface[1], "cz", 1), ring(zface[0], "cz", -1)
-    residual = call(
+    part = jax.ShapeDtypeStruct((4, 5, 8, LANES), F32)
+    same, other = call(
         residual_kernel,
-        jax.ShapeDtypeStruct((2, 5, 16, LANES), F32),
-        (filled, xm, xp, ym, yp, zm, zp, source, diag_scale, fluid, couple),
-        [VMEM] * 10 + [SMEM],
+        (part, part),
+        (filled, ym, yp, zm, zp, source, diag_scale, fluid, couple),
+        [VMEM] * 8 + [SMEM],
         "residual",
     )
-    after, far, before = (ring(residual, "stream", step) for step in (-1, 2, 1))
-    return pl.pallas_call(
+    before, after = ring(other, "stream", 1), ring(other, "stream", -1)
+    far = ring(same, "stream", 2)
+    part = jax.ShapeDtypeStruct((5, 2, 8, LANES), F32)
+    mine, theirs = pl.pallas_call(
         sweep_kernel,
-        out_shape=jax.ShapeDtypeStruct((5, 2, 16, LANES), F32),
-        in_specs=[VMEM] * 7 + [SMEM],
-        out_specs=VMEM,
-        scratch_shapes=[pltpu.VMEM((8, 5, 16, LANES), F32)],
+        out_shape=(part, part),
+        in_specs=[VMEM] * 5 + [SMEM],
+        out_specs=(VMEM, VMEM),
+        scratch_shapes=[pltpu.VMEM((8, 5, 8, LANES), F32)],
         name="sweeps",
         compiler_params=pltpu.CompilerParams(vmem_limit_bytes=BYTES),
-    )(residual, before, after, far, inv, filled, fluid, couple)
+    )(same, before, after, far, inv, couple)
+    swapped = lax.ppermute(
+        theirs, "stream", [(i, i ^ 1) for i in range(lax.axis_size("stream"))]
+    )
+    first_half = jnp.where(half == 0, mine, swapped)
+    second_half = jnp.where(half == 0, swapped, mine)
+    upper = jnp.concatenate([first_half, second_half], axis=2)
+    return filled.reshape(5, 2, 16, LANES) + RELAX * fluid.astype(F32)[None] * upper
 
 
 def solution(mesh):

time: 64.7 us -> 60.7 us (0.938); the launches traced: 63.7 us -> 60.5 us
  starting transfers between devices: 29.9 us -> 27.5 us
  waiting for transfers between devices: 19.6 us -> 18.3 us
  Pallas kernels: 13.8 us -> 12.9 us
  local copies, waits for them, and re-layouts: 0.08 us -> 0.76 us
    ppermute x13 -> x10, waiting for transfers between devices: 18.8 us -> 6.72 us  [ring(): lax.ppermute(x, axis, [(i, (i + steps) % count) for i in range(count)])]
    all_to_all x1, waiting for transfers between devices: 0.85 us -> 7.89 us  [on_device(): lax.all_to_all(sent, ('cy', 'cz'), split_axis=0, concat_axis=0, tiled=True)]
    ppermute x0 -> x1, waiting for transfers between devices: none -> 3.73 us  [on_device(): lax.ppermute(theirs, 'stream', [(i, i ^ 1) for i in range(lax.axis_size('...]
    ppermute x13 -> x10, starting transfers between devices: 18 us -> 15.2 us  [ring(): lax.ppermute(x, axis, [(i, (i + steps) % count) for i in range(count)])]
    pallas_call x1, Pallas kernels: 2.19 us -> 1.45 us  [on_device(): pl.pallas_call(sweep_kernel, out_shape=(part, part), in_specs=[VMEM] * 5...]
    unnamed x19, local copies, waits for them, and re-layouts: 0.05 us -> 0.75 us
    add x0 -> x1, other arithmetic: none -> 0.65 us  [on_device(): filled.reshape(5, 2, 16, LANES) + RELAX * fluid.astype(F32)[None] * upper]
  transfers between devices with their start and end apart: 14 -> 12, of which waited for: 9 -> 7; matrix products, arithmetic and copies ran while one was open for 0% -> 0% of each run, Pallas kernels for 8% -> 8%
where the time goes in v3:
time: 60.7 us; the launch traced here: 60.5 us
  starting transfers between devices  27.5 us (45%)
  waiting for transfers between devices  18.3 us (30%)
  Pallas kernels  12.9 us (21%)
  other arithmetic  0.77 us (1%)
  local copies, waits for them, and re-layouts  0.76 us (1%)
    ppermute x10, starting transfers between devices, ring(): lax.ppermute(x, axis, [(i, (i + steps) % count) for i in range(count)])  15.2 us
    all_to_all x1, starting transfers between devices, on_device(): lax.all_to_all(sent, ('cy', 'cz'), split_axis=0, concat_axis=0, tiled=True)  11.9 us
    all_to_all x1, waiting for transfers between devices, on_device(): lax.all_to_all(sent, ('cy', 'cz'), split_axis=0, concat_axis=0, tiled=True)  7.89 us
    ppermute x10, waiting for transfers between devices, ring(): lax.ppermute(x, axis, [(i, (i + steps) % count) for i in range(count)])  6.72 us
    pallas_call x3, Pallas kernels, call(): pl.pallas_call(kernel, out_shape=outs, in_specs=specs, out_specs=jax.tree...  6.43 us
    pallas_call x1, Pallas kernels, on_device(): pl.pallas_call(donor_kernel, out_shape=jax.ShapeDtypeStruct((64, 1, 1280)...  5.02 us
    ppermute x1, waiting for transfers between devices, on_device(): lax.ppermute(theirs, 'stream', [(i, i ^ 1) for i in range(lax.axis_size('...  3.73 us
    pallas_call x1, Pallas kernels, on_device(): pl.pallas_call(sweep_kernel, out_shape=(part, part), in_specs=[VMEM] * 5...  1.45 us
  transfers between devices with their start and end apart: 12, of which 7 were waited for; matrix products, arithmetic and copies ran while one was open for 0% of the time, Pallas kernels for 8%

profile of v3, /device:TPU:32, one launch (start us, length us, event | category | flops | bytes accessed | tf_op | source)
XLA Modules:
  0.0 60.5 jit_solution(3588236104465002956)
XLA Ops:
  0.0 5.0 %donor_pick.1 = f32[64,1,1280]{2,1,0:T(1,128)} custom-call(s32[64,256]{1,0:T(8,128)} %bitcast.37, s32[1,64]{1,0:T(1,128)} %bitcast.38, f32[160,128]{1,0:T(8,128)} %bitcast.27), custom_call_target="tpu_custom_call" | custom-call | tf_op jit(solution)/shard_map/donor_pick/pallas_call | solution.py:287
  5.0 11.9 %all-to-all-start = ((f32[64,1,1280]{2,1,0:T(1,128)}), f32[64,1,1280]{2,1,0:T(1,128)S(1)}, u32[]{:S(2)}, u32[]{:S(2)}) async-start(f32[64,1,1280]{2,1,0:T(1,128)} %donor_pick.1), calls=%async_computation | async-start | bytes 655360 | tf_op jit(solution)/shard_map/all_to_all | solution.py:314
  17.0 0.7 %copy-done.1 = s32[2,16,128]{2,1,0:T(8,128)S(1)} copy-done((s32[2,16,128]{2,1,0:T(8,128)S(1)}, s32[2,16,128]{2,1,0:T(8,128)}, u32[]{:S(2)}) %copy-start.1) | copy-done | bytes 16408
  17.8 1.6 %collective-permute-start = (f32[26,2,8,128]{3,2,1,0:T(8,128)S(1)}, f32[26,2,8,128]{3,2,1,0:T(8,128)S(1)}, u32[]{:S(2)}, u32[]{:S(2)}) collective-permute-start(f32[26,2,8,128]{3,2,1,0:T(8,128)S(1)} %get-tuple-element.40), channel_id=1, source_target_pairs={{0,64},{64,128},{128,192},{192,0},{1,65},{65,129},{129,193},{193,1... | collective-permute-start | bytes 638984 | tf_op jit(solution)/shard_map/ppermute | solution.py:19
  19.3 1.7 %collective-permute-start.1 = (f32[26,2,8,128]{3,2,1,0:T(8,128)S(1)}, f32[26,2,8,128]{3,2,1,0:T(8,128)S(1)}, u32[]{:S(2)}, u32[]{:S(2)}) collective-permute-start(f32[26,2,8,128]{3,2,1,0:T(8,128)S(1)} %get-tuple-element.40), channel_id=1, source_target_pairs={{0,192},{64,0},{128,64},{192,128},{1,193},{65,1},{129,65},{193,129... | collective-permute-start | bytes 638984 | tf_op jit(solution)/shard_map/ppermute | solution.py:19
  21.1 1.8 %collective-permute-start.2 = (f32[26,2,8,128]{3,2,1,0:T(8,128)S(1)}, f32[26,2,8,128]{3,2,1,0:T(8,128)S(1)}, u32[]{:S(2)}, u32[]{:S(2)}) collective-permute-start(f32[26,2,8,128]{3,2,1,0:T(8,128)S(1)} %get-tuple-element.39), channel_id=1, source_target_pairs={{0,128},{64,192},{128,0},{192,64},{1,129},{65,193},{129,1},{193,65... | collective-permute-start | bytes 638984 | tf_op jit(solution)/shard_map/ppermute | solution.py:19
  22.9 7.9 %all-to-all-done.rec_ref = f32[64,1,1280]{2,1,0:T(1,128)S(1)} async-done(((f32[64,1,1280]{2,1,0:T(1,128)}), f32[64,1,1280]{2,1,0:T(1,128)S(1)}, u32[]{:S(2)}, u32[]{:S(2)}) %all-to-all-start) | async-done | bytes 327712 | tf_op jit(solution)/shard_map/all_to_all | solution.py:314
  30.8 5.1 %ghost_fill.1 = (f32[160,128]{1,0:T(8,128)S(1)}, f32[2,10,128]{2,1,0:T(8,128)S(1)}, f32[2,10,128]{2,1,0:T(8,128)S(1)}) custom-call(f32[64,1,1280]{2,1,0:T(1,128)S(1)} %all-to-all-done.rec_ref, s32[8,1024]{1,0:T(8,128)S(1)} %get-tuple-element.22.src_ref, f32[8,1024]{1,0:T(8,128)S(1)} %get-tuple-element.23.w_ref, s32[1,1024]{1,0:T(1,128)S(1)} %get-tuple-element.24.cell_ref, ...), custom_call_target="tpu_custom_call" | custom-call | tf_op jit(solution)/shard_map/ghost_fill/pallas_call | solution.py:23
  36.0 2.9 %collective-permute-start.4 = (f32[10,128]{1,0:T(8,128)S(1)}, f32[10,128]{1,0:T(8,128)S(1)}, u32[]{:S(2)}, u32[]{:S(2)}) collective-permute-start(f32[10,128]{1,0:T(8,128)S(1)} %get-tuple-element.45), channel_id=1, source_target_pairs={{0,56},{8,0},{16,8},{24,16},{32,24},{40,32},{48,40},{56,48},{1,57}... | collective-permute-start | bytes 15368 | tf_op jit(solution)/shard_map/ppermute | solution.py:19
  39.0 1.0 %collective-permute-start.5 = (f32[10,128]{1,0:T(8,128)S(1)}, f32[10,128]{1,0:T(8,128)S(1)}, u32[]{:S(2)}, u32[]{:S(2)}) collective-permute-start(f32[10,128]{1,0:T(8,128)S(1)} %get-tuple-element.44), channel_id=1, source_target_pairs={{0,1},{1,2},{2,3},{3,4},{4,5},{5,6},{6,7},{7,0},{8,9},{9,10},{10,1... | collective-permute-start | bytes 15368 | tf_op jit(solution)/shard_map/ppermute | solution.py:19
  40.0 1.0 %collective-permute-start.6 = (f32[10,128]{1,0:T(8,128)S(1)}, f32[10,128]{1,0:T(8,128)S(1)}, u32[]{:S(2)}, u32[]{:S(2)}) collective-permute-start(f32[10,128]{1,0:T(8,128)S(1)} %get-tuple-element.43), channel_id=1, source_target_pairs={{0,7},{1,0},{2,1},{3,2},{4,3},{5,4},{6,5},{7,6},{8,15},{9,8},{10,9... | collective-permute-start | bytes 15368 | tf_op jit(solution)/shard_map/ppermute | solution.py:19
  41.0 1.6 %collective-permute-done.5.zm_ref = f32[10,128]{1,0:T(8,128)S(1)} collective-permute-done((f32[10,128]{1,0:T(8,128)S(1)}, f32[10,128]{1,0:T(8,128)S(1)}, u32[]{:S(2)}, u32[]{:S(2)}) %collective-permute-start.5) | collective-permute-done | bytes 5152 | tf_op jit(solution)/shard_map/ppermute | solution.py:19
  42.6 1.0 %collective-permute-done.6.zp_ref = f32[10,128]{1,0:T(8,128)S(1)} collective-permute-done((f32[10,128]{1,0:T(8,128)S(1)}, f32[10,128]{1,0:T(8,128)S(1)}, u32[]{:S(2)}, u32[]{:S(2)}) %collective-permute-start.6) | collective-permute-done | bytes 5152 | tf_op jit(solution)/shard_map/ppermute | solution.py:19
  43.7 1.3 %residual.1 = (f32[4,5,8,128]{3,2,1,0:T(8,128)S(1)}, f32[4,5,8,128]{3,2,1,0:T(8,128)S(1)}) custom-call(f32[160,128]{1,0:T(8,128)S(1)} %get-tuple-element.29.f_ref, f32[10,128]{1,0:T(8,128)S(1)} %collective-permute-done.3.ym_ref, f32[10,128]{1,0:T(8,128)S(1)} %collective-permute-done.4.yp_ref, f32[10,128]{1,0:T(8,128)S(1)} %collective-permute-done.5.zm_ref, ...), custom_call_target="tpu_custom_call" | custom-call | tf_op jit(solution)/shard_map/residual/pallas_call | solution.py:23
  45.0 1.6 %collective-permute-start.7 = (f32[4,5,8,128]{3,2,1,0:T(8,128)S(1)}, f32[4,5,8,128]{3,2,1,0:T(8,128)S(1)}, u32[]{:S(2)}, u32[]{:S(2)}) collective-permute-start(f32[4,5,8,128]{3,2,1,0:T(8,128)S(1)} %get-tuple-element.33), channel_id=1, source_target_pairs={{0,64},{64,128},{128,192},{192,0},{1,65},{65,129},{129,193},{193,1... | collective-permute-start | bytes 245768 | tf_op jit(solution)/shard_map/ppermute | solution.py:19
  46.6 1.8 %collective-permute-start.8 = (f32[4,5,8,128]{3,2,1,0:T(8,128)S(1)}, f32[4,5,8,128]{3,2,1,0:T(8,128)S(1)}, u32[]{:S(2)}, u32[]{:S(2)}) collective-permute-start(f32[4,5,8,128]{3,2,1,0:T(8,128)S(1)} %get-tuple-element.33), channel_id=1, source_target_pairs={{0,192},{64,0},{128,64},{192,128},{1,193},{65,1},{129,65},{193,129... | collective-permute-start | bytes 245768 | tf_op jit(solution)/shard_map/ppermute | solution.py:19
  48.3 1.8 %collective-permute-start.9 = (f32[4,5,8,128]{3,2,1,0:T(8,128)S(1)}, f32[4,5,8,128]{3,2,1,0:T(8,128)S(1)}, u32[]{:S(2)}, u32[]{:S(2)}) collective-permute-start(f32[4,5,8,128]{3,2,1,0:T(8,128)S(1)} %get-tuple-element.32.res_ref), channel_id=1, source_target_pairs={{0,128},{64,192},{128,0},{192,64},{1,129},{65,193},{129,1},{193,65... | collective-permute-start | bytes 245768 | tf_op jit(solution)/shard_map/ppermute | solution.py:19
  50.2 0.5 collective-permute-done.7.prev_ref
  50.7 0.3 collective-permute-done.8.next_ref
  51.0 3.3 %collective-permute-done.9.far_ref = f32[4,5,8,128]{3,2,1,0:T(8,128)S(1)} collective-permute-done((f32[4,5,8,128]{3,2,1,0:T(8,128)S(1)}, f32[4,5,8,128]{3,2,1,0:T(8,128)S(1)}, u32[]{:S(2)}, u32[]{:S(2)}) %collective-permute-start.9) | collective-permute-done | bytes 81952 | tf_op jit(solution)/shard_map/ppermute | solution.py:19
  54.3 1.5 %sweeps.1 = (f32[5,2,8,128]{3,2,1,0:T(8,128)S(1)}, f32[5,2,8,128]{3,2,1,0:T(8,128)S(1)}) custom-call(f32[4,5,8,128]{3,2,1,0:T(8,128)S(1)} %get-tuple-element.32.res_ref, f32[4,5,8,128]{3,2,1,0:T(8,128)S(1)} %collective-permute-done.7.prev_ref, f32[4,5,8,128]{3,2,1,0:T(8,128)S(1)} %collective-permute-done.8.next_ref, ...), custom_call_target="tpu_custom_call" | custom-call | tf_op jit(solution)/shard_map/sweeps/pallas_call | solution.py:353
  55.7 0.4 collective-permute-start.10
  56.1 3.7 %collective-permute-done.10 = f32[5,2,8,128]{3,2,1,0:T(8,128)S(1)} collective-permute-done((f32[5,2,8,128]{3,2,1,0:T(8,128)S(1)}, f32[5,2,8,128]{3,2,1,0:T(8,128)S(1)}, u32[]{:S(2)}, u32[]{:S(2)}) %collective-permute-start.10) | collective-permute-done | bytes 40992 | tf_op jit(solution)/shard_map/ppermute | solution.py:362
  59.8 0.7 %fusion.2 = f32[5,2,16,128]{3,2,1,0:T(8,128)} fusion(f32[5,2,16,128]{3,2,1,0:T(8,128)S(1)} %bitcast.26, f32[5,2,8,128]{3,2,1,0:T(8,128)S(1)} %get-tuple-element.42, f32[5,2,8,128]{3,2,1,0:T(8,128)S(1)} %get-tuple-element.41, f32[2,16,128]{2,1,0:T(8,128)S(1)} %convert_multiply_fusion), kind=kLoop, calls=%fused_computation.8 | loop fusion | flops 61440 | bytes 262144 | tf_op jit(solution)/shard_map/add | solution.py:368
  (32 shorter events, 0.2 us)
Async XLA Ops:
  5.0 12.7 %copy-start.7 = (f32[5,5,2,16,128]{4,3,2,1,0:T(8,128)S(1)}, f32[5,5,2,16,128]{4,3,2,1,0:T(8,128)}, u32[]{:S(2)}) copy-start(f32[5,5,2,16,128]{4,3,2,1,0:T(8,128)} %param.14) | copy-start | bytes 1228804
  5.0 25.8 %all-to-all-start = ((f32[64,1,1280]{2,1,0:T(1,128)}), f32[64,1,1280]{2,1,0:T(1,128)S(1)}, u32[]{:S(2)}, u32[]{:S(2)}) async-start(f32[64,1,1280]{2,1,0:T(1,128)} %donor_pick.1), calls=%async_computation | async-start | bytes 655360 | tf_op jit(solution)/shard_map/all_to_all | solution.py:314
  17.0 0.7 %copy-start.1 = (s32[2,16,128]{2,1,0:T(8,128)S(1)}, s32[2,16,128]{2,1,0:T(8,128)}, u32[]{:S(2)}) copy-start(s32[2,16,128]{2,1,0:T(8,128)} %fluid_ref.1) | copy-start | bytes 49156
  17.7 5.2 %copy-start = (f32[5,2,16,128]{3,2,1,0:T(8,128)S(1)}, f32[5,2,16,128]{3,2,1,0:T(8,128)}, u32[]{:S(2)}) copy-start(f32[5,2,16,128]{3,2,1,0:T(8,128)} %param.11) | copy-start | bytes 245764
  17.7 5.2 %copy-start.4 = (s32[1,1,1,1024,8]{3,4,2,1,0:T(8,128)S(1)}, s32[1,1,1,1024,8]{3,4,2,1,0:T(8,128)}, u32[]{:S(2)}) copy-start(s32[1,1,1,1024,8]{3,4,2,1,0:T(8,128)} %param.20) | copy-start | bytes 98308
  17.7 5.2 %copy-start.5 = (f32[1,1,1,1024,8]{3,4,2,1,0:T(8,128)S(1)}, f32[1,1,1,1024,8]{3,4,2,1,0:T(8,128)}, u32[]{:S(2)}) copy-start(f32[1,1,1,1024,8]{3,4,2,1,0:T(8,128)} %param.21) | copy-start | bytes 98308
  17.8 5.2 %copy-start.6 = (s32[1,1,1,1024]{3,2,1,0:T(1,128)S(1)}, s32[1,1,1,1024]{3,2,1,0:T(1,128)}, u32[]{:S(2)}) copy-start(s32[1,1,1,1024]{3,2,1,0:T(1,128)} %param.19) | copy-start | bytes 12292
  17.8 18.2 %collective-permute-start = (f32[26,2,8,128]{3,2,1,0:T(8,128)S(1)}, f32[26,2,8,128]{3,2,1,0:T(8,128)S(1)}, u32[]{:S(2)}, u32[]{:S(2)}) collective-permute-start(f32[26,2,8,128]{3,2,1,0:T(8,128)S(1)} %get-tuple-element.40), channel_id=1, source_target_pairs={{0,64},{64,128},{128,192},{192,0},{1,65},{65,129},{129,193},{193,1... | collective-permute-start | bytes 638984 | tf_op jit(solution)/shard_map/ppermute | solution.py:19
  19.3 16.6 %collective-permute-start.1 = (f32[26,2,8,128]{3,2,1,0:T(8,128)S(1)}, f32[26,2,8,128]{3,2,1,0:T(8,128)S(1)}, u32[]{:S(2)}, u32[]{:S(2)}) collective-permute-start(f32[26,2,8,128]{3,2,1,0:T(8,128)S(1)} %get-tuple-element.40), channel_id=1, source_target_pairs={{0,192},{64,0},{128,64},{192,128},{1,193},{65,1},{129,65},{193,129... | collective-permute-start | bytes 638984 | tf_op jit(solution)/shard_map/ppermute | solution.py:19
  21.1 14.9 %collective-permute-start.2 = (f32[26,2,8,128]{3,2,1,0:T(8,128)S(1)}, f32[26,2,8,128]{3,2,1,0:T(8,128)S(1)}, u32[]{:S(2)}, u32[]{:S(2)}) collective-permute-start(f32[26,2,8,128]{3,2,1,0:T(8,128)S(1)} %get-tuple-element.39), channel_id=1, source_target_pairs={{0,128},{64,192},{128,0},{192,64},{1,129},{65,193},{129,1},{193,65... | collective-permute-start | bytes 638984 | tf_op jit(solution)/shard_map/ppermute | solution.py:19
  30.8 10.2 %copy-start.8 = (f32[7,5,5]{2,0,1:T(8,128)S(1)}, f32[7,5,5]{2,0,1:T(8,128)}, u32[]{:S(2)}) copy-start(f32[7,5,5]{2,0,1:T(8,128)} %param.15) | copy-start | bytes 2104
  30.8 12.8 %copy-start.3 = (f32[5,2,16,128]{3,2,1,0:T(8,128)S(1)}, f32[5,2,16,128]{3,2,1,0:T(8,128)}, u32[]{:S(2)}) copy-start(f32[5,2,16,128]{3,2,1,0:T(8,128)} %scale_ref.1) | copy-start | bytes 245764
  35.9 7.7 %copy-start.2 = (f32[5,2,16,128]{3,2,1,0:T(8,128)S(1)}, f32[5,2,16,128]{3,2,1,0:T(8,128)}, u32[]{:S(2)}) copy-start(f32[5,2,16,128]{3,2,1,0:T(8,128)} %source_ref.1) | copy-start | bytes 245764
  36.0 5.0 %collective-permute-start.3 = (f32[10,128]{1,0:T(8,128)S(1)}, f32[10,128]{1,0:T(8,128)S(1)}, u32[]{:S(2)}, u32[]{:S(2)}) collective-permute-start(f32[10,128]{1,0:T(8,128)S(1)} %get-tuple-element.46), channel_id=1, source_target_pairs={{0,8},{8,16},{16,24},{24,32},{32,40},{40,48},{48,56},{56,0},{1,9},... | collective-permute-start | bytes 15368 | tf_op jit(solution)/shard_map/ppermute | solution.py:19
  36.0 5.0 %collective-permute-start.4 = (f32[10,128]{1,0:T(8,128)S(1)}, f32[10,128]{1,0:T(8,128)S(1)}, u32[]{:S(2)}, u32[]{:S(2)}) collective-permute-start(f32[10,128]{1,0:T(8,128)S(1)} %get-tuple-element.45), channel_id=1, source_target_pairs={{0,56},{8,0},{16,8},{24,16},{32,24},{40,32},{48,40},{56,48},{1,57}... | collective-permute-start | bytes 15368 | tf_op jit(solution)/shard_map/ppermute | solution.py:19
  39.0 3.7 %collective-permute-start.5 = (f32[10,128]{1,0:T(8,128)S(1)}, f32[10,128]{1,0:T(8,128)S(1)}, u32[]{:S(2)}, u32[]{:S(2)}) collective-permute-start(f32[10,128]{1,0:T(8,128)S(1)} %get-tuple-element.44), channel_id=1, source_target_pairs={{0,1},{1,2},{2,3},{3,4},{4,5},{5,6},{6,7},{7,0},{8,9},{9,10},{10,1... | collective-permute-start | bytes 15368 | tf_op jit(solution)/shard_map/ppermute | solution.py:19
  40.0 3.7 %collective-permute-start.6 = (f32[10,128]{1,0:T(8,128)S(1)}, f32[10,128]{1,0:T(8,128)S(1)}, u32[]{:S(2)}, u32[]{:S(2)}) collective-permute-start(f32[10,128]{1,0:T(8,128)S(1)} %get-tuple-element.43), channel_id=1, source_target_pairs={{0,7},{1,0},{2,1},{3,2},{4,3},{5,4},{6,5},{7,6},{8,15},{9,8},{10,9... | collective-permute-start | bytes 15368 | tf_op jit(solution)/shard_map/ppermute | solution.py:19
  45.0 5.7 %collective-permute-start.7 = (f32[4,5,8,128]{3,2,1,0:T(8,128)S(1)}, f32[4,5,8,128]{3,2,1,0:T(8,128)S(1)}, u32[]{:S(2)}, u32[]{:S(2)}) collective-permute-start(f32[4,5,8,128]{3,2,1,0:T(8,128)S(1)} %get-tuple-element.33), channel_id=1, source_target_pairs={{0,64},{64,128},{128,192},{192,0},{1,65},{65,129},{129,193},{193,1... | collective-permute-start | bytes 245768 | tf_op jit(solution)/shard_map/ppermute | solution.py:19
  46.6 4.4 %collective-permute-start.8 = (f32[4,5,8,128]{3,2,1,0:T(8,128)S(1)}, f32[4,5,8,128]{3,2,1,0:T(8,128)S(1)}, u32[]{:S(2)}, u32[]{:S(2)}) collective-permute-start(f32[4,5,8,128]{3,2,1,0:T(8,128)S(1)} %get-tuple-element.33), channel_id=1, source_target_pairs={{0,192},{64,0},{128,64},{192,128},{1,193},{65,1},{129,65},{193,129... | collective-permute-start | bytes 245768 | tf_op jit(solution)/shard_map/ppermute | solution.py:19
  48.3 5.9 %collective-permute-start.9 = (f32[4,5,8,128]{3,2,1,0:T(8,128)S(1)}, f32[4,5,8,128]{3,2,1,0:T(8,128)S(1)}, u32[]{:S(2)}, u32[]{:S(2)}) collective-permute-start(f32[4,5,8,128]{3,2,1,0:T(8,128)S(1)} %get-tuple-element.32.res_ref), channel_id=1, source_target_pairs={{0,128},{64,192},{128,0},{192,64},{1,129},{65,193},{129,1},{193,65... | collective-permute-start | bytes 245768 | tf_op jit(solution)/shard_map/ppermute | solution.py:19
  55.7 4.1 %collective-permute-start.10 = (f32[5,2,8,128]{3,2,1,0:T(8,128)S(1)}, f32[5,2,8,128]{3,2,1,0:T(8,128)S(1)}, u32[]{:S(2)}, u32[]{:S(2)}) collective-permute-start(f32[5,2,8,128]{3,2,1,0:T(8,128)S(1)} %get-tuple-element.38), channel_id=1, source_target_pairs={{0,64},{64,0},{128,192},{192,128},{1,65},{65,1},{129,193},{193,129... | collective-permute-start | bytes 122888 | tf_op jit(solution)/shard_map/ppermute | solution.py:362

commit v4 on v3

--- a/solution.py
+++ b/solution.py
@@ -35,16 +35,12 @@
 
 
 def donor_kernel(
-    idx_hbm, count_hbm, state_hbm, out_ref, idx_ref, count_ref, state_ref, sems
+    idx_hbm, count_hbm, state_hbm, out_ref, idx_ref, count_ref, state_ref, tab_ref, sems
 ):
     moves = [
         pltpu.make_async_copy(src, dst, sems.at[n])
         for n, (src, dst) in enumerate(
-            (
-                (count_hbm, count_ref),
-                (state_hbm, state_ref),
-                (idx_hbm, idx_ref),
-            )
+            ((count_hbm, count_ref), (state_hbm, state_ref), (idx_hbm, idx_ref))
         )
     ]
     for move in moves:
@@ -53,14 +49,20 @@
         move.wait()
     lanes = lax.broadcasted_iota(jnp.int32, (8, LANES), 1)
     subs = lax.broadcasted_iota(jnp.int32, (8, LANES), 0)
-
-    def body(g, carry):
-        base = pl.multiple_of(g * 8, 8)
+    lane_ids = lax.broadcasted_iota(jnp.int32, (LANES, 256), 0)
+    slots = lax.broadcasted_iota(jnp.int32, (1, 256), 1)
+    tab_ref[...] = jnp.zeros_like(tab_ref)
+    for v in range(5):
+        tab_ref[pl.ds(v, 32, stride=8), :] = state_ref[v * 32 : v * 32 + 32, :]
+    whole = tab_ref[...]
+    hi = whole.astype(BF16)
+    tab = jnp.concatenate([hi, (whole - hi.astype(F32)).astype(BF16)], axis=1)
+    for g in range(4):
         count = jnp.zeros((8, LANES), jnp.int32)
         for q in range(8):
             count = jnp.where(subs == q, count_ref[0, g * 8 + q], count)
         for h in range(2):
-            idx = idx_ref[pl.ds(base, 8), h * LANES : (h + 1) * LANES]
+            idx = idx_ref[g * 8 : g * 8 + 8, h * LANES : (h + 1) * LANES]
             lane = idx & (LANES - 1)
             row = idx >> 7
             acc = [jnp.zeros((8, LANES), F32) for _ in range(5)]
@@ -72,11 +74,21 @@
                     acc[v] = jnp.where(hit, lane_pick(line, lane), acc[v])
             live = lanes + h * LANES < count
             for v in range(5):
-                at = (v * 2 + h) * LANES
-                out_ref[pl.ds(base, 8), 0, at : at + LANES] = jnp.where(live, acc[v], 0.0)
-        return carry
-
-    lax.fori_loop(0, 8, body, 0)
+                at = pl.ds(g * 80 + v * 2 + h, 8, stride=10)
+                out_ref[at, :] = jnp.where(live, acc[v], 0.0)
+        for d in range(32 + g * 8, 40 + g * 8):
+            idx = idx_ref[d : d + 1, :]
+            onehot = (lane_ids == (idx & (LANES - 1))).astype(BF16)
+            onehot = jnp.concatenate([onehot, onehot], axis=0)
+            p = jnp.dot(tab, onehot, preferred_element_type=F32)
+            row = jnp.where(slots < count_ref[0, d], idx >> 7, -1)
+            row = jnp.broadcast_to(row, (8, 256))
+            acc = jnp.zeros((8, 256), F32)
+            for r in range(32):
+                acc = jnp.where(row == r, p[r * 8 : r * 8 + 8], acc)
+            for h in range(2):
+                at = pl.ds(d * 10 + h, 5, stride=2)
+                out_ref[at, :] = acc[0:5, h * LANES : (h + 1) * LANES]
 
 
 def stage_kernel(*refs):
@@ -88,13 +100,15 @@
 def ghost_kernel(
     rec_ref, src_ref, w_ref, cell_ref, state_ref, f_ref, y_ref, z_ref
 ):
-    tabs = []
+    his, los = [], []
     for v in range(5):
-        t = rec_ref[:, 0, v * 256 : (v + 1) * 256]
+        t = jnp.concatenate(
+            [rec_ref[pl.ds(v * 2 + h, 64, stride=10), :] for h in range(2)], axis=1
+        )
         hi = t.astype(BF16)
-        lo = (t - hi.astype(F32)).astype(BF16)
-        tabs.append(jnp.concatenate([hi, lo], axis=1))
-    tab = jnp.concatenate(tabs, axis=0)
+        his.append(hi)
+        los.append((t - hi.astype(F32)).astype(BF16))
+    tab = jnp.concatenate(his + los, axis=0)
     width = 256
     lane_ids = lax.broadcasted_iota(jnp.int32, (256, width), 0)
     row_ids = lax.broadcasted_iota(jnp.int32, (64, width), 0)
@@ -106,11 +120,10 @@
             entry = src_ref[k : k + 1, at]
             weight = w_ref[k : k + 1, at]
             onehot = (lane_ids == (entry & 255)).astype(BF16)
-            onehot = jnp.concatenate([onehot, onehot], axis=0)
             p = jnp.dot(tab, onehot, preferred_element_type=F32)
             m = jnp.where(row_ids == (entry >> 8), weight, 0.0)
             for v in range(5):
-                q = p[v * 64 : (v + 1) * 64] * m
+                q = (p[64 * v : 64 * v + 64] + p[320 + 64 * v : 384 + 64 * v]) * m
                 acc[v] = acc[v] + jnp.sum(q.reshape(8, 8, width), axis=0)
         for v in range(5):
             parts[v].append(jnp.sum(acc[v], axis=0, keepdims=True))
@@ -286,13 +299,14 @@
     table = state.reshape(160, LANES)
     sent = pl.pallas_call(
         donor_kernel,
-        out_shape=jax.ShapeDtypeStruct((64, 1, 1280), F32),
+        out_shape=jax.ShapeDtypeStruct((640, LANES), F32),
         in_specs=[pl.BlockSpec(memory_space=pl.ANY)] * 3,
         out_specs=VMEM,
         scratch_shapes=[
             pltpu.VMEM((64, 256), jnp.int32),
             pltpu.SMEM((1, 64), jnp.int32),
             pltpu.VMEM((160, LANES), F32),
+            pltpu.VMEM((256, LANES), F32),
             pltpu.SemaphoreType.DMA((3,)),
         ],
         name="donor_pick",
@@ -311,6 +325,7 @@
         [VMEM] * 4,
         "stage_lists",
     )
+    sent = sent.reshape(64, 1, 1280)
     received = lax.all_to_all(sent, ("cy", "cz"), split_axis=0, concat_axis=0, tiled=True)
     half = lax.rem(lax.axis_index("stream"), 2)
     frozen = jnp.concatenate([diag_inverse.reshape(25, 2, 16, LANES), fluid.astype(F32)[None]])
@@ -324,7 +339,7 @@
         ghost_kernel,
         (jax.ShapeDtypeStruct((160, LANES), F32), faces, faces),
         (
-            received,
+            received.reshape(640, LANES),
             entries,
             weights,
             cells,

time: 60.7 us -> 57.8 us (0.952)
  Pallas kernels: 12.9 us -> 9.94 us
    pallas_call x3, Pallas kernels: 6.43 us -> 4.88 us  [call(): pl.pallas_call(kernel, out_shape=outs, in_specs=specs, out_specs=jax.tree...]
    pallas_call x1, Pallas kernels: 5.02 us -> 3.6 us  [on_device(): pl.pallas_call(donor_kernel, out_shape=jax.ShapeDtypeStruct((640, LANES),...]
  transfers between devices with their start and end apart: 12 -> 12, of which waited for: 7 -> 7; matrix products, arithmetic and copies ran while one was open for 0% -> 0% of each run, Pallas kernels for 8% -> 6%
where the time goes in v4:
time: 57.8 us; the launch traced here: 57.5 us
  starting transfers between devices  27.5 us (48%)
  waiting for transfers between devices  18.3 us (32%)
  Pallas kernels  9.94 us (17%)
  other arithmetic  0.77 us (1%)
  local copies, waits for them, and re-layouts  0.76 us (1%)
    ppermute x10, starting transfers between devices, ring(): lax.ppermute(x, axis, [(i, (i + steps) % count) for i in range(count)])  15.2 us
    all_to_all x1, starting transfers between devices, on_device(): lax.all_to_all(sent, ('cy', 'cz'), split_axis=0, concat_axis=0, tiled=True)  11.9 us
    all_to_all x1, waiting for transfers between devices, on_device(): lax.all_to_all(sent, ('cy', 'cz'), split_axis=0, concat_axis=0, tiled=True)  7.89 us
    ppermute x10, waiting for transfers between devices, ring(): lax.ppermute(x, axis, [(i, (i + steps) % count) for i in range(count)])  6.69 us
    pallas_call x3, Pallas kernels, call(): pl.pallas_call(kernel, out_shape=outs, in_specs=specs, out_specs=jax.tree...  4.88 us
    ppermute x1, waiting for transfers between devices, on_device(): lax.ppermute(theirs, 'stream', [(i, i ^ 1) for i in range(lax.axis_size('...  3.73 us
    pallas_call x1, Pallas kernels, on_device(): pl.pallas_call(donor_kernel, out_shape=jax.ShapeDtypeStruct((640, LANES),...  3.6 us
    pallas_call x1, Pallas kernels, on_device(): pl.pallas_call(sweep_kernel, out_shape=(part, part), in_specs=[VMEM] * 5...  1.45 us
  transfers between devices with their start and end apart: 12, of which 7 were waited for; matrix products, arithmetic and copies ran while one was open for 0% of the time, Pallas kernels for 6%

profile of v4, /device:TPU:32, one launch (start us, length us, event | category | flops | bytes accessed | tf_op | source)
XLA Modules:
  0.0 57.5 jit_solution(6684086545661868786)
XLA Ops:
  0.0 3.6 %donor_pick.1 = f32[640,128]{1,0:T(8,128)} custom-call(s32[64,256]{1,0:T(8,128)} %bitcast.41, s32[1,64]{1,0:T(1,128)} %bitcast.42, f32[160,128]{1,0:T(8,128)} %bitcast.30), custom_call_target="tpu_custom_call" | custom-call | tf_op jit(solution)/shard_map/donor_pick/pallas_call | solution.py:300
  3.6 11.9 %all-to-all-start = ((f32[64,1,1280]{2,1,0:T(1,128)}), f32[64,1,1280]{2,1,0:T(1,128)S(1)}, u32[]{:S(2)}, u32[]{:S(2)}) async-start(f32[64,1,1280]{2,1,0:T(1,128)} %bitcast.35), calls=%async_computation | async-start | bytes 655360 | tf_op jit(solution)/shard_map/all_to_all | solution.py:329
  15.6 0.7 %copy-done.1 = s32[2,16,128]{2,1,0:T(8,128)S(1)} copy-done((s32[2,16,128]{2,1,0:T(8,128)S(1)}, s32[2,16,128]{2,1,0:T(8,128)}, u32[]{:S(2)}) %copy-start.1) | copy-done | bytes 16408
  16.4 1.6 %collective-permute-start = (f32[26,2,8,128]{3,2,1,0:T(8,128)S(1)}, f32[26,2,8,128]{3,2,1,0:T(8,128)S(1)}, u32[]{:S(2)}, u32[]{:S(2)}) collective-permute-start(f32[26,2,8,128]{3,2,1,0:T(8,128)S(1)} %get-tuple-element.40), channel_id=1, source_target_pairs={{0,64},{64,128},{128,192},{192,0},{1,65},{65,129},{129,193},{193,1... | collective-permute-start | bytes 638984 | tf_op jit(solution)/shard_map/ppermute | solution.py:19
  17.9 1.8 %collective-permute-start.1 = (f32[26,2,8,128]{3,2,1,0:T(8,128)S(1)}, f32[26,2,8,128]{3,2,1,0:T(8,128)S(1)}, u32[]{:S(2)}, u32[]{:S(2)}) collective-permute-start(f32[26,2,8,128]{3,2,1,0:T(8,128)S(1)} %get-tuple-element.40), channel_id=1, source_target_pairs={{0,192},{64,0},{128,64},{192,128},{1,193},{65,1},{129,65},{193,129... | collective-permute-start | bytes 638984 | tf_op jit(solution)/shard_map/ppermute | solution.py:19
  19.7 1.8 %collective-permute-start.2 = (f32[26,2,8,128]{3,2,1,0:T(8,128)S(1)}, f32[26,2,8,128]{3,2,1,0:T(8,128)S(1)}, u32[]{:S(2)}, u32[]{:S(2)}) collective-permute-start(f32[26,2,8,128]{3,2,1,0:T(8,128)S(1)} %get-tuple-element.39), channel_id=1, source_target_pairs={{0,128},{64,192},{128,0},{192,64},{1,129},{65,193},{129,1},{193,65... | collective-permute-start | bytes 638984 | tf_op jit(solution)/shard_map/ppermute | solution.py:19
  21.5 7.9 %all-to-all-done = f32[64,1,1280]{2,1,0:T(1,128)S(1)} async-done(((f32[64,1,1280]{2,1,0:T(1,128)}), f32[64,1,1280]{2,1,0:T(1,128)S(1)}, u32[]{:S(2)}, u32[]{:S(2)}) %all-to-all-start) | async-done | bytes 327712 | tf_op jit(solution)/shard_map/all_to_all | solution.py:329
  29.4 3.5 %ghost_fill.1 = (f32[160,128]{1,0:T(8,128)S(1)}, f32[2,10,128]{2,1,0:T(8,128)S(1)}, f32[2,10,128]{2,1,0:T(8,128)S(1)}) custom-call(f32[640,128]{1,0:T(8,128)S(1)} %bitcast.28, s32[8,1024]{1,0:T(8,128)S(1)} %get-tuple-element.22.src_ref, f32[8,1024]{1,0:T(8,128)S(1)} %get-tuple-element.23.w_ref, s32[1,1024]{1,0:T(1,128)S(1)} %get-tuple-element.24.cell_ref, ...), custom_call_target="tpu_custom_call" | custom-call | tf_op jit(solution)/shard_map/ghost_fill/pallas_call | solution.py:23
  33.1 2.9 %collective-permute-start.4 = (f32[10,128]{1,0:T(8,128)S(1)}, f32[10,128]{1,0:T(8,128)S(1)}, u32[]{:S(2)}, u32[]{:S(2)}) collective-permute-start(f32[10,128]{1,0:T(8,128)S(1)} %get-tuple-element.45), channel_id=1, source_target_pairs={{0,56},{8,0},{16,8},{24,16},{32,24},{40,32},{48,40},{56,48},{1,57}... | collective-permute-start | bytes 15368 | tf_op jit(solution)/shard_map/ppermute | solution.py:19
  36.0 1.0 %collective-permute-start.5 = (f32[10,128]{1,0:T(8,128)S(1)}, f32[10,128]{1,0:T(8,128)S(1)}, u32[]{:S(2)}, u32[]{:S(2)}) collective-permute-start(f32[10,128]{1,0:T(8,128)S(1)} %get-tuple-element.44), channel_id=1, source_target_pairs={{0,1},{1,2},{2,3},{3,4},{4,5},{5,6},{6,7},{7,0},{8,9},{9,10},{10,1... | collective-permute-start | bytes 15368 | tf_op jit(solution)/shard_map/ppermute | solution.py:19
  37.0 1.0 %collective-permute-start.6 = (f32[10,128]{1,0:T(8,128)S(1)}, f32[10,128]{1,0:T(8,128)S(1)}, u32[]{:S(2)}, u32[]{:S(2)}) collective-permute-start(f32[10,128]{1,0:T(8,128)S(1)} %get-tuple-element.43), channel_id=1, source_target_pairs={{0,7},{1,0},{2,1},{3,2},{4,3},{5,4},{6,5},{7,6},{8,15},{9,8},{10,9... | collective-permute-start | bytes 15368 | tf_op jit(solution)/shard_map/ppermute | solution.py:19
  38.1 1.6 %collective-permute-done.5.zm_ref = f32[10,128]{1,0:T(8,128)S(1)} collective-permute-done((f32[10,128]{1,0:T(8,128)S(1)}, f32[10,128]{1,0:T(8,128)S(1)}, u32[]{:S(2)}, u32[]{:S(2)}) %collective-permute-start.5) | collective-permute-done | bytes 5152 | tf_op jit(solution)/shard_map/ppermute | solution.py:19
  39.7 1.0 %collective-permute-done.6.zp_ref = f32[10,128]{1,0:T(8,128)S(1)} collective-permute-done((f32[10,128]{1,0:T(8,128)S(1)}, f32[10,128]{1,0:T(8,128)S(1)}, u32[]{:S(2)}, u32[]{:S(2)}) %collective-permute-start.6) | collective-permute-done | bytes 5152 | tf_op jit(solution)/shard_map/ppermute | solution.py:19
  40.7 1.3 %residual.1 = (f32[4,5,8,128]{3,2,1,0:T(8,128)S(1)}, f32[4,5,8,128]{3,2,1,0:T(8,128)S(1)}) custom-call(f32[160,128]{1,0:T(8,128)S(1)} %get-tuple-element.29.f_ref, f32[10,128]{1,0:T(8,128)S(1)} %collective-permute-done.3.ym_ref, f32[10,128]{1,0:T(8,128)S(1)} %collective-permute-done.4.yp_ref, f32[10,128]{1,0:T(8,128)S(1)} %collective-permute-done.5.zm_ref, ...), custom_call_target="tpu_custom_call" | custom-call | tf_op jit(solution)/shard_map/residual/pallas_call | solution.py:23
  42.0 1.6 %collective-permute-start.7 = (f32[4,5,8,128]{3,2,1,0:T(8,128)S(1)}, f32[4,5,8,128]{3,2,1,0:T(8,128)S(1)}, u32[]{:S(2)}, u32[]{:S(2)}) collective-permute-start(f32[4,5,8,128]{3,2,1,0:T(8,128)S(1)} %get-tuple-element.33), channel_id=1, source_target_pairs={{0,64},{64,128},{128,192},{192,0},{1,65},{65,129},{129,193},{193,1... | collective-permute-start | bytes 245768 | tf_op jit(solution)/shard_map/ppermute | solution.py:19
  43.6 1.8 %collective-permute-start.8 = (f32[4,5,8,128]{3,2,1,0:T(8,128)S(1)}, f32[4,5,8,128]{3,2,1,0:T(8,128)S(1)}, u32[]{:S(2)}, u32[]{:S(2)}) collective-permute-start(f32[4,5,8,128]{3,2,1,0:T(8,128)S(1)} %get-tuple-element.33), channel_id=1, source_target_pairs={{0,192},{64,0},{128,64},{192,128},{1,193},{65,1},{129,65},{193,129... | collective-permute-start | bytes 245768 | tf_op jit(solution)/shard_map/ppermute | solution.py:19
  45.3 1.8 %collective-permute-start.9 = (f32[4,5,8,128]{3,2,1,0:T(8,128)S(1)}, f32[4,5,8,128]{3,2,1,0:T(8,128)S(1)}, u32[]{:S(2)}, u32[]{:S(2)}) collective-permute-start(f32[4,5,8,128]{3,2,1,0:T(8,128)S(1)} %get-tuple-element.32.res_ref), channel_id=1, source_target_pairs={{0,128},{64,192},{128,0},{192,64},{1,129},{65,193},{129,1},{193,65... | collective-permute-start | bytes 245768 | tf_op jit(solution)/shard_map/ppermute | solution.py:19
  47.2 0.5 collective-permute-done.7.prev_ref
  47.8 0.3 collective-permute-done.8.next_ref
  48.0 3.3 %collective-permute-done.9.far_ref = f32[4,5,8,128]{3,2,1,0:T(8,128)S(1)} collective-permute-done((f32[4,5,8,128]{3,2,1,0:T(8,128)S(1)}, f32[4,5,8,128]{3,2,1,0:T(8,128)S(1)}, u32[]{:S(2)}, u32[]{:S(2)}) %collective-permute-start.9) | collective-permute-done | bytes 81952 | tf_op jit(solution)/shard_map/ppermute | solution.py:19
  51.3 1.5 %sweeps.1 = (f32[5,2,8,128]{3,2,1,0:T(8,128)S(1)}, f32[5,2,8,128]{3,2,1,0:T(8,128)S(1)}) custom-call(f32[4,5,8,128]{3,2,1,0:T(8,128)S(1)} %get-tuple-element.32.res_ref, f32[4,5,8,128]{3,2,1,0:T(8,128)S(1)} %collective-permute-done.7.prev_ref, f32[4,5,8,128]{3,2,1,0:T(8,128)S(1)} %collective-permute-done.8.next_ref, ...), custom_call_target="tpu_custom_call" | custom-call | tf_op jit(solution)/shard_map/sweeps/pallas_call | solution.py:368
  52.7 0.4 collective-permute-start.10
  53.1 3.7 %collective-permute-done.10 = f32[5,2,8,128]{3,2,1,0:T(8,128)S(1)} collective-permute-done((f32[5,2,8,128]{3,2,1,0:T(8,128)S(1)}, f32[5,2,8,128]{3,2,1,0:T(8,128)S(1)}, u32[]{:S(2)}, u32[]{:S(2)}) %collective-permute-start.10) | collective-permute-done | bytes 40992 | tf_op jit(solution)/shard_map/ppermute | solution.py:377
  56.9 0.7 %fusion.2 = f32[5,2,16,128]{3,2,1,0:T(8,128)} fusion(f32[5,2,16,128]{3,2,1,0:T(8,128)S(1)} %bitcast.29, f32[5,2,8,128]{3,2,1,0:T(8,128)S(1)} %get-tuple-element.42, f32[5,2,8,128]{3,2,1,0:T(8,128)S(1)} %get-tuple-element.41, f32[2,16,128]{2,1,0:T(8,128)S(1)} %convert_multiply_fusion), kind=kLoop, calls=%fused_computation.8 | loop fusion | flops 61440 | bytes 262144 | tf_op jit(solution)/shard_map/add | solution.py:383
  (32 shorter events, 0.2 us)
Async XLA Ops:
  3.6 12.7 %copy-start.7 = (f32[5,5,2,16,128]{4,3,2,1,0:T(8,128)S(1)}, f32[5,5,2,16,128]{4,3,2,1,0:T(8,128)}, u32[]{:S(2)}) copy-start(f32[5,5,2,16,128]{4,3,2,1,0:T(8,128)} %param.14) | copy-start | bytes 1228804
  3.6 25.8 %all-to-all-start = ((f32[64,1,1280]{2,1,0:T(1,128)}), f32[64,1,1280]{2,1,0:T(1,128)S(1)}, u32[]{:S(2)}, u32[]{:S(2)}) async-start(f32[64,1,1280]{2,1,0:T(1,128)} %bitcast.35), calls=%async_computation | async-start | bytes 655360 | tf_op jit(solution)/shard_map/all_to_all | solution.py:329
  15.5 0.7 %copy-start.1 = (s32[2,16,128]{2,1,0:T(8,128)S(1)}, s32[2,16,128]{2,1,0:T(8,128)}, u32[]{:S(2)}) copy-start(s32[2,16,128]{2,1,0:T(8,128)} %fluid_ref.1) | copy-start | bytes 49156
  16.3 5.2 %copy-start = (f32[5,2,16,128]{3,2,1,0:T(8,128)S(1)}, f32[5,2,16,128]{3,2,1,0:T(8,128)}, u32[]{:S(2)}) copy-start(f32[5,2,16,128]{3,2,1,0:T(8,128)} %param.11) | copy-start | bytes 245764
  16.3 5.2 %copy-start.4 = (s32[1,1,1,1024,8]{3,4,2,1,0:T(8,128)S(1)}, s32[1,1,1,1024,8]{3,4,2,1,0:T(8,128)}, u32[]{:S(2)}) copy-start(s32[1,1,1,1024,8]{3,4,2,1,0:T(8,128)} %param.20) | copy-start | bytes 98308
  16.3 5.2 %copy-start.5 = (f32[1,1,1,1024,8]{3,4,2,1,0:T(8,128)S(1)}, f32[1,1,1,1024,8]{3,4,2,1,0:T(8,128)}, u32[]{:S(2)}) copy-start(f32[1,1,1,1024,8]{3,4,2,1,0:T(8,128)} %param.21) | copy-start | bytes 98308
  16.4 5.2 %copy-start.6 = (s32[1,1,1,1024]{3,2,1,0:T(1,128)S(1)}, s32[1,1,1,1024]{3,2,1,0:T(1,128)}, u32[]{:S(2)}) copy-start(s32[1,1,1,1024]{3,2,1,0:T(1,128)} %param.19) | copy-start | bytes 12292
  16.4 16.6 %collective-permute-start = (f32[26,2,8,128]{3,2,1,0:T(8,128)S(1)}, f32[26,2,8,128]{3,2,1,0:T(8,128)S(1)}, u32[]{:S(2)}, u32[]{:S(2)}) collective-permute-start(f32[26,2,8,128]{3,2,1,0:T(8,128)S(1)} %get-tuple-element.40), channel_id=1, source_target_pairs={{0,64},{64,128},{128,192},{192,0},{1,65},{65,129},{129,193},{193,1... | collective-permute-start | bytes 638984 | tf_op jit(solution)/shard_map/ppermute | solution.py:19
  17.9 15.1 %collective-permute-start.1 = (f32[26,2,8,128]{3,2,1,0:T(8,128)S(1)}, f32[26,2,8,128]{3,2,1,0:T(8,128)S(1)}, u32[]{:S(2)}, u32[]{:S(2)}) collective-permute-start(f32[26,2,8,128]{3,2,1,0:T(8,128)S(1)} %get-tuple-element.40), channel_id=1, source_target_pairs={{0,192},{64,0},{128,64},{192,128},{1,193},{65,1},{129,65},{193,129... | collective-permute-start | bytes 638984 | tf_op jit(solution)/shard_map/ppermute | solution.py:19
  19.7 13.3 %collective-permute-start.2 = (f32[26,2,8,128]{3,2,1,0:T(8,128)S(1)}, f32[26,2,8,128]{3,2,1,0:T(8,128)S(1)}, u32[]{:S(2)}, u32[]{:S(2)}) collective-permute-start(f32[26,2,8,128]{3,2,1,0:T(8,128)S(1)} %get-tuple-element.39), channel_id=1, source_target_pairs={{0,128},{64,192},{128,0},{192,64},{1,129},{65,193},{129,1},{193,65... | collective-permute-start | bytes 638984 | tf_op jit(solution)/shard_map/ppermute | solution.py:19
  29.4 8.6 %copy-start.8 = (f32[7,5,5]{2,0,1:T(8,128)S(1)}, f32[7,5,5]{2,0,1:T(8,128)}, u32[]{:S(2)}) copy-start(f32[7,5,5]{2,0,1:T(8,128)} %param.15) | copy-start | bytes 2104
  29.4 11.3 %copy-start.3 = (f32[5,2,16,128]{3,2,1,0:T(8,128)S(1)}, f32[5,2,16,128]{3,2,1,0:T(8,128)}, u32[]{:S(2)}) copy-start(f32[5,2,16,128]{3,2,1,0:T(8,128)} %scale_ref.1) | copy-start | bytes 245764
  33.0 7.7 %copy-start.2 = (f32[5,2,16,128]{3,2,1,0:T(8,128)S(1)}, f32[5,2,16,128]{3,2,1,0:T(8,128)}, u32[]{:S(2)}) copy-start(f32[5,2,16,128]{3,2,1,0:T(8,128)} %source_ref.1) | copy-start | bytes 245764
  33.0 5.0 %collective-permute-start.3 = (f32[10,128]{1,0:T(8,128)S(1)}, f32[10,128]{1,0:T(8,128)S(1)}, u32[]{:S(2)}, u32[]{:S(2)}) collective-permute-start(f32[10,128]{1,0:T(8,128)S(1)} %get-tuple-element.46), channel_id=1, source_target_pairs={{0,8},{8,16},{16,24},{24,32},{32,40},{40,48},{48,56},{56,0},{1,9},... | collective-permute-start | bytes 15368 | tf_op jit(solution)/shard_map/ppermute | solution.py:19
  33.1 5.0 %collective-permute-start.4 = (f32[10,128]{1,0:T(8,128)S(1)}, f32[10,128]{1,0:T(8,128)S(1)}, u32[]{:S(2)}, u32[]{:S(2)}) collective-permute-start(f32[10,128]{1,0:T(8,128)S(1)} %get-tuple-element.45), channel_id=1, source_target_pairs={{0,56},{8,0},{16,8},{24,16},{32,24},{40,32},{48,40},{56,48},{1,57}... | collective-permute-start | bytes 15368 | tf_op jit(solution)/shard_map/ppermute | solution.py:19
  36.0 3.7 %collective-permute-start.5 = (f32[10,128]{1,0:T(8,128)S(1)}, f32[10,128]{1,0:T(8,128)S(1)}, u32[]{:S(2)}, u32[]{:S(2)}) collective-permute-start(f32[10,128]{1,0:T(8,128)S(1)} %get-tuple-element.44), channel_id=1, source_target_pairs={{0,1},{1,2},{2,3},{3,4},{4,5},{5,6},{6,7},{7,0},{8,9},{9,10},{10,1... | collective-permute-start | bytes 15368 | tf_op jit(solution)/shard_map/ppermute | solution.py:19
  37.0 3.7 %collective-permute-start.6 = (f32[10,128]{1,0:T(8,128)S(1)}, f32[10,128]{1,0:T(8,128)S(1)}, u32[]{:S(2)}, u32[]{:S(2)}) collective-permute-start(f32[10,128]{1,0:T(8,128)S(1)} %get-tuple-element.43), channel_id=1, source_target_pairs={{0,7},{1,0},{2,1},{3,2},{4,3},{5,4},{6,5},{7,6},{8,15},{9,8},{10,9... | collective-permute-start | bytes 15368 | tf_op jit(solution)/shard_map/ppermute | solution.py:19
  42.0 5.7 %collective-permute-start.7 = (f32[4,5,8,128]{3,2,1,0:T(8,128)S(1)}, f32[4,5,8,128]{3,2,1,0:T(8,128)S(1)}, u32[]{:S(2)}, u32[]{:S(2)}) collective-permute-start(f32[4,5,8,128]{3,2,1,0:T(8,128)S(1)} %get-tuple-element.33), channel_id=1, source_target_pairs={{0,64},{64,128},{128,192},{192,0},{1,65},{65,129},{129,193},{193,1... | collective-permute-start | bytes 245768 | tf_op jit(solution)/shard_map/ppermute | solution.py:19
  43.6 4.4 %collective-permute-start.8 = (f32[4,5,8,128]{3,2,1,0:T(8,128)S(1)}, f32[4,5,8,128]{3,2,1,0:T(8,128)S(1)}, u32[]{:S(2)}, u32[]{:S(2)}) collective-permute-start(f32[4,5,8,128]{3,2,1,0:T(8,128)S(1)} %get-tuple-element.33), channel_id=1, source_target_pairs={{0,192},{64,0},{128,64},{192,128},{1,193},{65,1},{129,65},{193,129... | collective-permute-start | bytes 245768 | tf_op jit(solution)/shard_map/ppermute | solution.py:19
  45.3 5.9 %collective-permute-start.9 = (f32[4,5,8,128]{3,2,1,0:T(8,128)S(1)}, f32[4,5,8,128]{3,2,1,0:T(8,128)S(1)}, u32[]{:S(2)}, u32[]{:S(2)}) collective-permute-start(f32[4,5,8,128]{3,2,1,0:T(8,128)S(1)} %get-tuple-element.32.res_ref), channel_id=1, source_target_pairs={{0,128},{64,192},{128,0},{192,64},{1,129},{65,193},{129,1},{193,65... | collective-permute-start | bytes 245768 | tf_op jit(solution)/shard_map/ppermute | solution.py:19
  52.7 4.1 %collective-permute-start.10 = (f32[5,2,8,128]{3,2,1,0:T(8,128)S(1)}, f32[5,2,8,128]{3,2,1,0:T(8,128)S(1)}, u32[]{:S(2)}, u32[]{:S(2)}) collective-permute-start(f32[5,2,8,128]{3,2,1,0:T(8,128)S(1)} %get-tuple-element.38), channel_id=1, source_target_pairs={{0,64},{64,0},{128,192},{192,128},{1,65},{65,1},{129,193},{193,129... | collective-permute-start | bytes 122888 | tf_op jit(solution)/shard_map/ppermute | solution.py:377

commit v5 on v4

--- a/solution.py
+++ b/solution.py
@@ -91,10 +91,19 @@
                 out_ref[at, :] = acc[0:5, h * LANES : (h + 1) * LANES]
 
 
+def coef(ref, d, i, j):
+    return ref[25 * d + 5 * i + j : 25 * d + 5 * i + j + 1, :]
+
+
 def stage_kernel(*refs):
-    half = len(refs) // 2
-    for src, dst in zip(refs[:half], refs[half:]):
+    for src, dst in zip(refs[:4], refs[5:9]):
         dst[...] = src[...]
+    couple_ref, coef_ref = refs[4], refs[9]
+    for d in range(7):
+        for i in range(5):
+            for j in range(5):
+                at = 25 * d + 5 * i + j
+                coef_ref[at : at + 1, :] = jnp.full((1, LANES), couple_ref[d, i, j], F32)
 
 
 def ghost_kernel(
@@ -164,50 +173,67 @@
                 z_ref[side, row : row + 1, :] = jnp.sum(face, axis=0, keepdims=True)
 
 
+def interior_kernel(f_ref, source_ref, scale_ref, couple_ref, out_ref):
+    shape = (16, LANES)
+    subs = lax.broadcasted_iota(jnp.int32, shape, 0)
+    lanes = lax.broadcasted_iota(jnp.int32, shape, 1)
+    for x in range(2):
+        near = [[] for _ in range(6)]
+        for v in range(5):
+            mid = f_ref[32 * v + 16 * x : 32 * v + 16 * x + 16, :]
+            near[0].append(mid)
+            near[1].append(f_ref[32 * v + 16 * (1 - x) : 32 * v + 16 * (1 - x) + 16, :])
+            near[2].append(jnp.where(subs == 0, 0.0, pltpu.roll(mid, 1, 0)))
+            near[3].append(jnp.where(subs == 15, 0.0, pltpu.roll(mid, 15, 0)))
+            near[4].append(jnp.where(lanes == 0, 0.0, pltpu.roll(mid, 1, 1)))
+            near[5].append(jnp.where(lanes == LANES - 1, 0.0, pltpu.roll(mid, LANES - 1, 1)))
+        for i in range(5):
+            image = scale_ref[i, x] * near[0][i]
+            for n, d in enumerate((0, 2 - x, 3, 4, 5, 6)):
+                for j in range(5):
+                    image = image + coef(couple_ref, d, i, j) * near[n][j]
+            out_ref[x, i] = source_ref[i, x] - image
+
+
 def residual_kernel(
-    f_ref, ym_ref, yp_ref, zm_ref, zp_ref, source_ref, scale_ref, fluid_ref,
-    couple_ref, same_ref, other_ref,
+    part_ref, f_ref, ym_ref, yp_ref, zm_ref, zp_ref, fluid_ref, couple_ref, same_ref, other_ref
 ):
     s, a, b = (lax.axis_index(n) for n in ("stream", "cy", "cz"))
     na, nb = (lax.axis_size(n) for n in ("cy", "cz"))
     half = lax.rem(s, 2)
-    shape = (16, LANES)
-    subs = lax.broadcasted_iota(jnp.int32, shape, 0)
-    lanes = lax.broadcasted_iota(jnp.int32, shape, 1)
-
-    def column(ref, row):
-        line = jnp.broadcast_to(ref[row : row + 1, :], shape)
-        return jnp.concatenate(
-            [lane_pick(line[0:8], subs[0:8]), lane_pick(line[8:16], subs[8:16])], axis=0
-        )
-
+    subs = lax.broadcasted_iota(jnp.int32, (8, LANES), 0)
+    lanes = lax.broadcasted_iota(jnp.int32, (8, LANES), 1)
+
+    def applied(d, ref, inside):
+        rows = [jnp.where(inside, ref[2 * j : 2 * j + 2, :], 0.0) for j in range(5)]
+        out = []
+        for i in range(5):
+            c = coef(couple_ref, d, i, 0) * rows[0]
+            for j in range(1, 5):
+                c = c + coef(couple_ref, d, i, j) * rows[j]
+            out.append(c)
+        return out
+
+    ym, yp = applied(3, ym_ref, a > 0), applied(4, yp_ref, a < na - 1)
+    zm, zp = applied(5, zm_ref, b > 0), applied(6, zp_ref, b < nb - 1)
     for x in range(2):
-        near = [[] for _ in range(7)]
-        for v in range(5):
-            row = 2 * v + x
-            mid = f_ref[32 * v + 16 * x : 32 * v + 16 * x + 16, :]
-            other = f_ref[32 * v + 16 * (1 - x) : 32 * v + 16 * (1 - x) + 16, :]
-            ym = jnp.where(a > 0, ym_ref[row : row + 1, :], 0.0)
-            yp = jnp.where(a < na - 1, yp_ref[row : row + 1, :], 0.0)
-            zm = jnp.where(b > 0, column(zm_ref, row), 0.0)
-            zp = jnp.where(b < nb - 1, column(zp_ref, row), 0.0)
-            near[0].append(mid)
-            near[2 - x].append(other)
-            near[3].append(jnp.where(subs == 0, ym, pltpu.roll(mid, 1, 0)))
-            near[4].append(jnp.where(subs == 15, yp, pltpu.roll(mid, 15, 0)))
-            near[5].append(jnp.where(lanes == 0, zm, pltpu.roll(mid, 1, 1)))
-            near[6].append(jnp.where(lanes == LANES - 1, zp, pltpu.roll(mid, LANES - 1, 1)))
-        wet = fluid_ref[x].astype(F32)
         for i in range(5):
-            image = scale_ref[i, x] * near[0][i]
-            for d in (0, 2 - x, 3, 4, 5, 6):
-                for j in range(5):
-                    image = image + couple_ref[d, i, j] * near[d][j]
-            res = wet * (source_ref[i, x] - image)
-            same_ref[x, i] = jnp.where(half == 0, res[0:8], res[8:16])
-            other_ref[x, i] = jnp.where(half == 0, res[8:16], res[0:8])
-            same_ref[2 + x, i] = jnp.where(half == 0, near[0][i][0:8], near[0][i][8:16])
-            other_ref[2 + x, i] = jnp.where(half == 0, near[0][i][8:16], near[0][i][0:8])
+            tiles, filled = [], []
+            for t in range(2):
+                r = part_ref[x, i, 8 * t : 8 * t + 8, :]
+                edge = (ym if t == 0 else yp)[i][x : x + 1]
+                r = r - jnp.where(subs == 7 * t, edge, 0.0)
+                left, right = (
+                    lane_pick(jnp.broadcast_to(z[i][x : x + 1], (8, LANES)), subs + 8 * t)
+                    for z in (zm, zp)
+                )
+                r = r - jnp.where(lanes == 0, left, jnp.where(lanes == LANES - 1, right, 0.0))
+                tiles.append(fluid_ref[x, 8 * t : 8 * t + 8, :].astype(F32) * r)
+                at = 32 * i + 16 * x + 8 * t
+                filled.append(f_ref[at : at + 8, :])
+            for k, (first, second) in ((x, tiles), (2 + x, filled)):
+                same_ref[k, i] = jnp.where(half == 0, first, second)
+                other_ref[k, i] = jnp.where(half == 0, second, first)
 
 
 def sweep_kernel(
@@ -243,13 +269,13 @@
             if x == 1 and q < count - 1:
                 ahead = block(q + 1, 2)
                 for i in range(5):
-                    c = couple_ref[2, i, 0] * ahead[0]
+                    c = coef(couple_ref, 2, i, 0) * ahead[0]
                     for j in range(1, 5):
-                        c = c + couple_ref[2, i, j] * ahead[j]
+                        c = c + coef(couple_ref, 2, i, j) * ahead[j]
                     t[i] = t[i] - wet * c
             for i in range(5):
                 for j in range(5):
-                    t[i] = t[i] - couple_ref[1, i, j] * prev[j]
+                    t[i] = t[i] - coef(couple_ref, 1, i, j) * prev[j]
             cur = []
             for i in range(5):
                 c = inv_ref[o, 5 * i, x] * t[0]
@@ -264,9 +290,9 @@
         for x in (1, 0):
             t = []
             for i in range(5):
-                r = couple_ref[2, i, 0] * prev[0]
+                r = coef(couple_ref, 2, i, 0) * prev[0]
                 for j in range(1, 5):
-                    r = r + couple_ref[2, i, j] * prev[j]
+                    r = r + coef(couple_ref, 2, i, j) * prev[j]
                 t.append(r)
             cur = []
             for i in range(5):
@@ -318,11 +344,12 @@
         ghost_cell.reshape(1, 1024),
         table,
     )
-    entries, weights, cells, table = call(
+    entries, weights, cells, table, coefs = call(
         stage_kernel,
-        tuple(jax.ShapeDtypeStruct(x.shape, x.dtype) for x in lists),
-        lists,
-        [VMEM] * 4,
+        tuple(jax.ShapeDtypeStruct(x.shape, x.dtype) for x in lists)
+        + (jax.ShapeDtypeStruct((175, LANES), F32),),
+        lists + (couple,),
+        [VMEM] * 4 + [SMEM],
         "stage_lists",
     )
     sent = sent.reshape(64, 1, 1280)
@@ -355,11 +382,18 @@
     ym, yp = ring(yface[1], "cy", 1), ring(yface[0], "cy", -1)
     zm, zp = ring(zface[1], "cz", 1), ring(zface[0], "cz", -1)
     part = jax.ShapeDtypeStruct((4, 5, 8, LANES), F32)
+    inside = call(
+        interior_kernel,
+        jax.ShapeDtypeStruct((2, 5, 16, LANES), F32),
+        (filled, source, diag_scale, coefs),
+        [VMEM] * 4,
+        "interior",
+    )
     same, other = call(
         residual_kernel,
         (part, part),
-        (filled, ym, yp, zm, zp, source, diag_scale, fluid, couple),
-        [VMEM] * 8 + [SMEM],
+        (inside, filled, ym, yp, zm, zp, fluid, coefs),
+        [VMEM] * 7 + [VMEM],
         "residual",
     )
     before, after = ring(other, "stream", 1), ring(other, "stream", -1)
@@ -368,12 +402,12 @@
     mine, theirs = pl.pallas_call(
         sweep_kernel,
         out_shape=(part, part),
-        in_specs=[VMEM] * 5 + [SMEM],
+        in_specs=[VMEM] * 6,
         out_specs=(VMEM, VMEM),
         scratch_shapes=[pltpu.VMEM((8, 5, 8, LANES), F32)],
         name="sweeps",
         compiler_params=pltpu.CompilerParams(vmem_limit_bytes=BYTES),
-    )(same, before, after, far, inv, couple)
+    )(same, before, after, far, inv, coefs)
     swapped = lax.ppermute(
         theirs, "stream", [(i, i ^ 1) for i in range(lax.axis_size("stream"))]
     )

time: 57.8 us -> 55.9 us (0.967)
  waiting for transfers between devices: 18.3 us -> 16.8 us
  Pallas kernels: 9.94 us -> 8.93 us
  local copies, waits for them, and re-layouts: 0.76 us -> 1.4 us
    all_to_all x1, waiting for transfers between devices: 7.89 us -> 6.16 us  [on_device(): lax.all_to_all(sent, ('cy', 'cz'), split_axis=0, concat_axis=0, tiled=True)]
    pallas_call x1, Pallas kernels: 1.45 us -> 0.36 us  [on_device(): pl.pallas_call(sweep_kernel, out_shape=(part, part), in_specs=[VMEM] * 6,...]
    unnamed x19, local copies, waits for them, and re-layouts: 0.75 us -> 1.4 us
    pallas_call x3 -> x4, Pallas kernels: 4.88 us -> 4.97 us  [call(): pl.pallas_call(kernel, out_shape=outs, in_specs=specs, out_specs=jax.tree...]
  transfers between devices with their start and end apart: 12 -> 12, of which waited for: 7 -> 7; matrix products, arithmetic and copies ran while one was open for 0% -> 0% of each run, Pallas kernels for 6% -> 9%
where the time goes in v5:
time: 55.9 us; the launch traced here: 55.6 us
  starting transfers between devices  27.5 us (49%)
  waiting for transfers between devices  16.8 us (30%)
  Pallas kernels  8.93 us (16%)
  local copies, waits for them, and re-layouts  1.4 us (3%)
  other arithmetic  0.76 us (1%)
    ppermute x10, starting transfers between devices, ring(): lax.ppermute(x, axis, [(i, (i + steps) % count) for i in range(count)])  15.2 us
    all_to_all x1, starting transfers between devices, on_device(): lax.all_to_all(sent, ('cy', 'cz'), split_axis=0, concat_axis=0, tiled=True)  11.9 us
    ppermute x10, waiting for transfers between devices, ring(): lax.ppermute(x, axis, [(i, (i + steps) % count) for i in range(count)])  6.9 us
    all_to_all x1, waiting for transfers between devices, on_device(): lax.all_to_all(sent, ('cy', 'cz'), split_axis=0, concat_axis=0, tiled=True)  6.16 us
    pallas_call x4, Pallas kernels, call(): pl.pallas_call(kernel, out_shape=outs, in_specs=specs, out_specs=jax.tree...  4.97 us
    ppermute x1, waiting for transfers between devices, on_device(): lax.ppermute(theirs, 'stream', [(i, i ^ 1) for i in range(lax.axis_size('...  3.77 us
    pallas_call x1, Pallas kernels, on_device(): pl.pallas_call(donor_kernel, out_shape=jax.ShapeDtypeStruct((640, LANES),...  3.6 us
    unnamed x19, local copies, waits for them, and re-layouts  1.4 us
  transfers between devices with their start and end apart: 12, of which 7 were waited for; matrix products, arithmetic and copies ran while one was open for 0% of the time, Pallas kernels for 9%

profile of v5, /device:TPU:32, one launch (start us, length us, event | category | flops | bytes accessed | tf_op | source)
XLA Modules:
  0.0 55.6 jit_solution(17411559237877367138)
XLA Ops:
  0.0 3.6 %donor_pick.1 = f32[640,128]{1,0:T(8,128)} custom-call(s32[64,256]{1,0:T(8,128)} %bitcast.41, s32[1,64]{1,0:T(1,128)} %bitcast.42, f32[160,128]{1,0:T(8,128)} %bitcast.30), custom_call_target="tpu_custom_call" | custom-call | tf_op jit(solution)/shard_map/donor_pick/pallas_call | solution.py:326
  3.6 11.9 %all-to-all-start = ((f32[64,1,1280]{2,1,0:T(1,128)}), f32[64,1,1280]{2,1,0:T(1,128)S(1)}, u32[]{:S(2)}, u32[]{:S(2)}) async-start(f32[64,1,1280]{2,1,0:T(1,128)} %bitcast.35), calls=%async_computation | async-start | bytes 655360 | tf_op jit(solution)/shard_map/all_to_all | solution.py:356
  15.6 0.7 %copy-done.1 = s32[2,16,128]{2,1,0:T(8,128)S(1)} copy-done((s32[2,16,128]{2,1,0:T(8,128)S(1)}, s32[2,16,128]{2,1,0:T(8,128)}, u32[]{:S(2)}) %copy-start.1) | copy-done | bytes 16408
  16.4 1.6 %collective-permute-start = (f32[26,2,8,128]{3,2,1,0:T(8,128)S(1)}, f32[26,2,8,128]{3,2,1,0:T(8,128)S(1)}, u32[]{:S(2)}, u32[]{:S(2)}) collective-permute-start(f32[26,2,8,128]{3,2,1,0:T(8,128)S(1)} %get-tuple-element.42), channel_id=1, source_target_pairs={{0,64},{64,128},{128,192},{192,0},{1,65},{65,129},{129,193},{193,1... | collective-permute-start | bytes 638984 | tf_op jit(solution)/shard_map/ppermute | solution.py:19
  17.9 1.8 %collective-permute-start.1 = (f32[26,2,8,128]{3,2,1,0:T(8,128)S(1)}, f32[26,2,8,128]{3,2,1,0:T(8,128)S(1)}, u32[]{:S(2)}, u32[]{:S(2)}) collective-permute-start(f32[26,2,8,128]{3,2,1,0:T(8,128)S(1)} %get-tuple-element.42), channel_id=1, source_target_pairs={{0,192},{64,0},{128,64},{192,128},{1,193},{65,1},{129,65},{193,129... | collective-permute-start | bytes 638984 | tf_op jit(solution)/shard_map/ppermute | solution.py:19
  19.7 1.8 %collective-permute-start.2 = (f32[26,2,8,128]{3,2,1,0:T(8,128)S(1)}, f32[26,2,8,128]{3,2,1,0:T(8,128)S(1)}, u32[]{:S(2)}, u32[]{:S(2)}) collective-permute-start(f32[26,2,8,128]{3,2,1,0:T(8,128)S(1)} %get-tuple-element.41), channel_id=1, source_target_pairs={{0,128},{64,192},{128,0},{192,64},{1,129},{65,193},{129,1},{193,65... | collective-permute-start | bytes 638984 | tf_op jit(solution)/shard_map/ppermute | solution.py:19
  21.5 0.6 %copy-done.6 = s32[1,1,1,1024]{3,2,1,0:T(1,128)S(1)} copy-done((s32[1,1,1,1024]{3,2,1,0:T(1,128)S(1)}, s32[1,1,1,1024]{3,2,1,0:T(1,128)}, u32[]{:S(2)}) %copy-start.6) | copy-done | bytes 4120
  22.2 1.1 %stage_lists.1 = (s32[8,1024]{1,0:T(8,128)S(1)}, f32[8,1024]{1,0:T(8,128)S(1)}, s32[1,1024]{1,0:T(1,128)S(1)}, f32[160,128]{1,0:T(8,128)S(1)}, f32[175,128]{1,0:T(8,128)S(1)}) custom-call(s32[8,1024]{1,0:T(8,128)S(1)} %bitcast.32, f32[8,1024]{1,0:T(8,128)S(1)} %bitcast.33, s32[1,1024]{1,0:T(1,128)S(1)} %bitcast.34, f32[160,128]{1,0:T(8,128)S(1)} %bitcast.31, ...), custom_call_target="tpu_custom_call" | custom-call | tf_op jit(solution)/shard_map/stage_lists/pallas_call | solution.py:23
  23.3 6.2 %all-to-all-done = f32[64,1,1280]{2,1,0:T(1,128)S(1)} async-done(((f32[64,1,1280]{2,1,0:T(1,128)}), f32[64,1,1280]{2,1,0:T(1,128)S(1)}, u32[]{:S(2)}, u32[]{:S(2)}) %all-to-all-start) | async-done | bytes 327712 | tf_op jit(solution)/shard_map/all_to_all | solution.py:356
  29.4 3.5 %ghost_fill.1 = (f32[160,128]{1,0:T(8,128)S(1)}, f32[2,10,128]{2,1,0:T(8,128)S(1)}, f32[2,10,128]{2,1,0:T(8,128)S(1)}) custom-call(f32[640,128]{1,0:T(8,128)S(1)} %bitcast.28, s32[8,1024]{1,0:T(8,128)S(1)} %get-tuple-element.23.src_ref, f32[8,1024]{1,0:T(8,128)S(1)} %get-tuple-element.24.w_ref, s32[1,1024]{1,0:T(1,128)S(1)} %get-tuple-element.25.cell_ref, ...), custom_call_target="tpu_custom_call" | custom-call | tf_op jit(solution)/shard_map/ghost_fill/pallas_call | solution.py:23
  33.0 2.9 %collective-permute-start.4 = (f32[10,128]{1,0:T(8,128)S(1)}, f32[10,128]{1,0:T(8,128)S(1)}, u32[]{:S(2)}, u32[]{:S(2)}) collective-permute-start(f32[10,128]{1,0:T(8,128)S(1)} %get-tuple-element.47), channel_id=1, source_target_pairs={{0,56},{8,0},{16,8},{24,16},{32,24},{40,32},{48,40},{56,48},{1,57}... | collective-permute-start | bytes 15368 | tf_op jit(solution)/shard_map/ppermute | solution.py:19
  36.0 1.0 %collective-permute-start.5 = (f32[10,128]{1,0:T(8,128)S(1)}, f32[10,128]{1,0:T(8,128)S(1)}, u32[]{:S(2)}, u32[]{:S(2)}) collective-permute-start(f32[10,128]{1,0:T(8,128)S(1)} %get-tuple-element.46), channel_id=1, source_target_pairs={{0,1},{1,2},{2,3},{3,4},{4,5},{5,6},{6,7},{7,0},{8,9},{9,10},{10,1... | collective-permute-start | bytes 15368 | tf_op jit(solution)/shard_map/ppermute | solution.py:19
  37.0 1.0 %collective-permute-start.6 = (f32[10,128]{1,0:T(8,128)S(1)}, f32[10,128]{1,0:T(8,128)S(1)}, u32[]{:S(2)}, u32[]{:S(2)}) collective-permute-start(f32[10,128]{1,0:T(8,128)S(1)} %get-tuple-element.45), channel_id=1, source_target_pairs={{0,7},{1,0},{2,1},{3,2},{4,3},{5,4},{6,5},{7,6},{8,15},{9,8},{10,9... | collective-permute-start | bytes 15368 | tf_op jit(solution)/shard_map/ppermute | solution.py:19
  38.3 1.4 %collective-permute-done.5.zm_ref = f32[10,128]{1,0:T(8,128)S(1)} collective-permute-done((f32[10,128]{1,0:T(8,128)S(1)}, f32[10,128]{1,0:T(8,128)S(1)}, u32[]{:S(2)}, u32[]{:S(2)}) %collective-permute-start.5) | collective-permute-done | bytes 5152 | tf_op jit(solution)/shard_map/ppermute | solution.py:19
  39.6 1.0 %collective-permute-done.6.zp_ref = f32[10,128]{1,0:T(8,128)S(1)} collective-permute-done((f32[10,128]{1,0:T(8,128)S(1)}, f32[10,128]{1,0:T(8,128)S(1)}, u32[]{:S(2)}, u32[]{:S(2)}) %collective-permute-start.6) | collective-permute-done | bytes 5152 | tf_op jit(solution)/shard_map/ppermute | solution.py:19
  40.8 1.6 %collective-permute-start.7 = (f32[4,5,8,128]{3,2,1,0:T(8,128)S(1)}, f32[4,5,8,128]{3,2,1,0:T(8,128)S(1)}, u32[]{:S(2)}, u32[]{:S(2)}) collective-permute-start(f32[4,5,8,128]{3,2,1,0:T(8,128)S(1)} %get-tuple-element.35), channel_id=1, source_target_pairs={{0,64},{64,128},{128,192},{192,0},{1,65},{65,129},{129,193},{193,1... | collective-permute-start | bytes 245768 | tf_op jit(solution)/shard_map/ppermute | solution.py:19
  42.4 1.8 %collective-permute-start.8 = (f32[4,5,8,128]{3,2,1,0:T(8,128)S(1)}, f32[4,5,8,128]{3,2,1,0:T(8,128)S(1)}, u32[]{:S(2)}, u32[]{:S(2)}) collective-permute-start(f32[4,5,8,128]{3,2,1,0:T(8,128)S(1)} %get-tuple-element.35), channel_id=1, source_target_pairs={{0,192},{64,0},{128,64},{192,128},{1,193},{65,1},{129,65},{193,129... | collective-permute-start | bytes 245768 | tf_op jit(solution)/shard_map/ppermute | solution.py:19
  44.2 1.8 %collective-permute-start.9 = (f32[4,5,8,128]{3,2,1,0:T(8,128)S(1)}, f32[4,5,8,128]{3,2,1,0:T(8,128)S(1)}, u32[]{:S(2)}, u32[]{:S(2)}) collective-permute-start(f32[4,5,8,128]{3,2,1,0:T(8,128)S(1)} %get-tuple-element.34.res_ref), channel_id=1, source_target_pairs={{0,128},{64,192},{128,0},{192,64},{1,129},{65,193},{129,1},{193,65... | collective-permute-start | bytes 245768 | tf_op jit(solution)/shard_map/ppermute | solution.py:19
  46.0 0.5 collective-permute-done.7.prev_ref
  46.8 3.7 %collective-permute-done.9.far_ref = f32[4,5,8,128]{3,2,1,0:T(8,128)S(1)} collective-permute-done((f32[4,5,8,128]{3,2,1,0:T(8,128)S(1)}, f32[4,5,8,128]{3,2,1,0:T(8,128)S(1)}, u32[]{:S(2)}, u32[]{:S(2)}) %collective-permute-start.9) | collective-permute-done | bytes 81952 | tf_op jit(solution)/shard_map/ppermute | solution.py:19
  50.5 0.4 sweeps.1
  50.9 0.3 collective-permute-start.10
  51.2 3.8 %collective-permute-done.10 = f32[5,2,8,128]{3,2,1,0:T(8,128)S(1)} collective-permute-done((f32[5,2,8,128]{3,2,1,0:T(8,128)S(1)}, f32[5,2,8,128]{3,2,1,0:T(8,128)S(1)}, u32[]{:S(2)}, u32[]{:S(2)}) %collective-permute-start.10) | collective-permute-done | bytes 40992 | tf_op jit(solution)/shard_map/ppermute | solution.py:411
  55.0 0.7 %fusion.2 = f32[5,2,16,128]{3,2,1,0:T(8,128)} fusion(f32[5,2,16,128]{3,2,1,0:T(8,128)S(1)} %bitcast.29, f32[5,2,8,128]{3,2,1,0:T(8,128)S(1)} %get-tuple-element.44, f32[5,2,8,128]{3,2,1,0:T(8,128)S(1)} %get-tuple-element.43, f32[2,16,128]{2,1,0:T(8,128)S(1)} %convert_multiply_fusion), kind=kLoop, calls=%fused_computation.8 | loop fusion | flops 61440 | bytes 262144 | tf_op jit(solution)/shard_map/add | solution.py:417
  (33 shorter events, 0.8 us)
Async XLA Ops:
  3.6 12.7 %copy-start.7 = (f32[5,5,2,16,128]{4,3,2,1,0:T(8,128)S(1)}, f32[5,5,2,16,128]{4,3,2,1,0:T(8,128)}, u32[]{:S(2)}) copy-start(f32[5,5,2,16,128]{4,3,2,1,0:T(8,128)} %param.14) | copy-start | bytes 1228804
  3.6 25.8 %all-to-all-start = ((f32[64,1,1280]{2,1,0:T(1,128)}), f32[64,1,1280]{2,1,0:T(1,128)S(1)}, u32[]{:S(2)}, u32[]{:S(2)}) async-start(f32[64,1,1280]{2,1,0:T(1,128)} %bitcast.35), calls=%async_computation | async-start | bytes 655360 | tf_op jit(solution)/shard_map/all_to_all | solution.py:356
  15.5 0.7 %copy-start.1 = (s32[2,16,128]{2,1,0:T(8,128)S(1)}, s32[2,16,128]{2,1,0:T(8,128)}, u32[]{:S(2)}) copy-start(s32[2,16,128]{2,1,0:T(8,128)} %fluid_ref.1) | copy-start | bytes 49156
  16.3 5.2 %copy-start.8 = (f32[7,5,5]{2,0,1:T(8,128)S(1)}, f32[7,5,5]{2,0,1:T(8,128)}, u32[]{:S(2)}) copy-start(f32[7,5,5]{2,0,1:T(8,128)} %param.15) | copy-start | bytes 2104
  16.3 5.2 %copy-start = (f32[5,2,16,128]{3,2,1,0:T(8,128)S(1)}, f32[5,2,16,128]{3,2,1,0:T(8,128)}, u32[]{:S(2)}) copy-start(f32[5,2,16,128]{3,2,1,0:T(8,128)} %param.11) | copy-start | bytes 245764
  16.3 5.2 %copy-start.5 = (f32[1,1,1,1024,8]{3,4,2,1,0:T(8,128)S(1)}, f32[1,1,1,1024,8]{3,4,2,1,0:T(8,128)}, u32[]{:S(2)}) copy-start(f32[1,1,1,1024,8]{3,4,2,1,0:T(8,128)} %param.21) | copy-start | bytes 98308
  16.4 5.2 %copy-start.4 = (s32[1,1,1,1024,8]{3,4,2,1,0:T(8,128)S(1)}, s32[1,1,1,1024,8]{3,4,2,1,0:T(8,128)}, u32[]{:S(2)}) copy-start(s32[1,1,1,1024,8]{3,4,2,1,0:T(8,128)} %param.20) | copy-start | bytes 98308
  16.4 16.6 %collective-permute-start = (f32[26,2,8,128]{3,2,1,0:T(8,128)S(1)}, f32[26,2,8,128]{3,2,1,0:T(8,128)S(1)}, u32[]{:S(2)}, u32[]{:S(2)}) collective-permute-start(f32[26,2,8,128]{3,2,1,0:T(8,128)S(1)} %get-tuple-element.42), channel_id=1, source_target_pairs={{0,64},{64,128},{128,192},{192,0},{1,65},{65,129},{129,193},{193,1... | collective-permute-start | bytes 638984 | tf_op jit(solution)/shard_map/ppermute | solution.py:19
  17.9 15.1 %collective-permute-start.1 = (f32[26,2,8,128]{3,2,1,0:T(8,128)S(1)}, f32[26,2,8,128]{3,2,1,0:T(8,128)S(1)}, u32[]{:S(2)}, u32[]{:S(2)}) collective-permute-start(f32[26,2,8,128]{3,2,1,0:T(8,128)S(1)} %get-tuple-element.42), channel_id=1, source_target_pairs={{0,192},{64,0},{128,64},{192,128},{1,193},{65,1},{129,65},{193,129... | collective-permute-start | bytes 638984 | tf_op jit(solution)/shard_map/ppermute | solution.py:19
  19.7 13.3 %collective-permute-start.2 = (f32[26,2,8,128]{3,2,1,0:T(8,128)S(1)}, f32[26,2,8,128]{3,2,1,0:T(8,128)S(1)}, u32[]{:S(2)}, u32[]{:S(2)}) collective-permute-start(f32[26,2,8,128]{3,2,1,0:T(8,128)S(1)} %get-tuple-element.41), channel_id=1, source_target_pairs={{0,128},{64,192},{128,0},{192,64},{1,129},{65,193},{129,1},{193,65... | collective-permute-start | bytes 638984 | tf_op jit(solution)/shard_map/ppermute | solution.py:19
  21.5 0.7 %copy-start.6 = (s32[1,1,1,1024]{3,2,1,0:T(1,128)S(1)}, s32[1,1,1,1024]{3,2,1,0:T(1,128)}, u32[]{:S(2)}) copy-start(s32[1,1,1,1024]{3,2,1,0:T(1,128)} %param.19) | copy-start | bytes 12292
  29.4 8.6 %copy-start.2 = (f32[5,2,16,128]{3,2,1,0:T(8,128)S(1)}, f32[5,2,16,128]{3,2,1,0:T(8,128)}, u32[]{:S(2)}) copy-start(f32[5,2,16,128]{3,2,1,0:T(8,128)} %source_ref.1) | copy-start | bytes 245764
  29.4 8.6 %copy-start.3 = (f32[5,2,16,128]{3,2,1,0:T(8,128)S(1)}, f32[5,2,16,128]{3,2,1,0:T(8,128)}, u32[]{:S(2)}) copy-start(f32[5,2,16,128]{3,2,1,0:T(8,128)} %scale_ref.1) | copy-start | bytes 245764
  33.0 5.2 %collective-permute-start.3 = (f32[10,128]{1,0:T(8,128)S(1)}, f32[10,128]{1,0:T(8,128)S(1)}, u32[]{:S(2)}, u32[]{:S(2)}) collective-permute-start(f32[10,128]{1,0:T(8,128)S(1)} %get-tuple-element.48), channel_id=1, source_target_pairs={{0,8},{8,16},{16,24},{24,32},{32,40},{40,48},{48,56},{56,0},{1,9},... | collective-permute-start | bytes 15368 | tf_op jit(solution)/shard_map/ppermute | solution.py:19
  33.0 5.2 %collective-permute-start.4 = (f32[10,128]{1,0:T(8,128)S(1)}, f32[10,128]{1,0:T(8,128)S(1)}, u32[]{:S(2)}, u32[]{:S(2)}) collective-permute-start(f32[10,128]{1,0:T(8,128)S(1)} %get-tuple-element.47), channel_id=1, source_target_pairs={{0,56},{8,0},{16,8},{24,16},{32,24},{40,32},{48,40},{56,48},{1,57}... | collective-permute-start | bytes 15368 | tf_op jit(solution)/shard_map/ppermute | solution.py:19
  36.0 3.7 %collective-permute-start.5 = (f32[10,128]{1,0:T(8,128)S(1)}, f32[10,128]{1,0:T(8,128)S(1)}, u32[]{:S(2)}, u32[]{:S(2)}) collective-permute-start(f32[10,128]{1,0:T(8,128)S(1)} %get-tuple-element.46), channel_id=1, source_target_pairs={{0,1},{1,2},{2,3},{3,4},{4,5},{5,6},{6,7},{7,0},{8,9},{9,10},{10,1... | collective-permute-start | bytes 15368 | tf_op jit(solution)/shard_map/ppermute | solution.py:19
  37.0 3.7 %collective-permute-start.6 = (f32[10,128]{1,0:T(8,128)S(1)}, f32[10,128]{1,0:T(8,128)S(1)}, u32[]{:S(2)}, u32[]{:S(2)}) collective-permute-start(f32[10,128]{1,0:T(8,128)S(1)} %get-tuple-element.45), channel_id=1, source_target_pairs={{0,7},{1,0},{2,1},{3,2},{4,3},{5,4},{6,5},{7,6},{8,15},{9,8},{10,9... | collective-permute-start | bytes 15368 | tf_op jit(solution)/shard_map/ppermute | solution.py:19
  40.8 5.7 %collective-permute-start.7 = (f32[4,5,8,128]{3,2,1,0:T(8,128)S(1)}, f32[4,5,8,128]{3,2,1,0:T(8,128)S(1)}, u32[]{:S(2)}, u32[]{:S(2)}) collective-permute-start(f32[4,5,8,128]{3,2,1,0:T(8,128)S(1)} %get-tuple-element.35), channel_id=1, source_target_pairs={{0,64},{64,128},{128,192},{192,0},{1,65},{65,129},{129,193},{193,1... | collective-permute-start | bytes 245768 | tf_op jit(solution)/shard_map/ppermute | solution.py:19
  42.4 4.4 %collective-permute-start.8 = (f32[4,5,8,128]{3,2,1,0:T(8,128)S(1)}, f32[4,5,8,128]{3,2,1,0:T(8,128)S(1)}, u32[]{:S(2)}, u32[]{:S(2)}) collective-permute-start(f32[4,5,8,128]{3,2,1,0:T(8,128)S(1)} %get-tuple-element.35), channel_id=1, source_target_pairs={{0,192},{64,0},{128,64},{192,128},{1,193},{65,1},{129,65},{193,129... | collective-permute-start | bytes 245768 | tf_op jit(solution)/shard_map/ppermute | solution.py:19
  44.2 6.3 %collective-permute-start.9 = (f32[4,5,8,128]{3,2,1,0:T(8,128)S(1)}, f32[4,5,8,128]{3,2,1,0:T(8,128)S(1)}, u32[]{:S(2)}, u32[]{:S(2)}) collective-permute-start(f32[4,5,8,128]{3,2,1,0:T(8,128)S(1)} %get-tuple-element.34.res_ref), channel_id=1, source_target_pairs={{0,128},{64,192},{128,0},{192,64},{1,129},{65,193},{129,1},{193,65... | collective-permute-start | bytes 245768 | tf_op jit(solution)/shard_map/ppermute | solution.py:19
  50.9 4.1 %collective-permute-start.10 = (f32[5,2,8,128]{3,2,1,0:T(8,128)S(1)}, f32[5,2,8,128]{3,2,1,0:T(8,128)S(1)}, u32[]{:S(2)}, u32[]{:S(2)}) collective-permute-start(f32[5,2,8,128]{3,2,1,0:T(8,128)S(1)} %get-tuple-element.40), channel_id=1, source_target_pairs={{0,64},{64,0},{128,192},{192,128},{1,65},{65,1},{129,193},{193,129... | collective-permute-start | bytes 122888 | tf_op jit(solution)/shard_map/ppermute | solution.py:411

commit v6 on v5

--- a/solution.py
+++ b/solution.py
@@ -122,20 +122,37 @@
     lane_ids = lax.broadcasted_iota(jnp.int32, (256, width), 0)
     row_ids = lax.broadcasted_iota(jnp.int32, (64, width), 0)
     parts = [[] for _ in range(5)]
-    for j in range(1024 // width):
+    tiles = [slice(t * LANES, (t + 1) * LANES) for t in (6, 7)]
+    lane = [src_ref[:, t] & (LANES - 1) for t in tiles]
+    line = [src_ref[:, t] >> 7 for t in tiles]
+    found = [[jnp.zeros((8, LANES), F32) for _ in tiles] for _ in range(5)]
+    for step in range(24):
+        j, k = step // 8, step % 8
+        if k == 0:
+            acc = [jnp.zeros((8, width), F32) for _ in range(5)]
         at = slice(j * width, (j + 1) * width)
-        acc = [jnp.zeros((8, width), F32) for _ in range(5)]
-        for k in range(8):
-            entry = src_ref[k : k + 1, at]
-            weight = w_ref[k : k + 1, at]
-            onehot = (lane_ids == (entry & 255)).astype(BF16)
-            p = jnp.dot(tab, onehot, preferred_element_type=F32)
-            m = jnp.where(row_ids == (entry >> 8), weight, 0.0)
+        entry = src_ref[k : k + 1, at]
+        weight = w_ref[k : k + 1, at]
+        onehot = (lane_ids == (entry & 255)).astype(BF16)
+        p = jnp.dot(tab, onehot, preferred_element_type=F32)
+        m = jnp.where(row_ids == (entry >> 8), weight, 0.0)
+        for v in range(5):
+            q = (p[64 * v : 64 * v + 64] + p[320 + 64 * v : 384 + 64 * v]) * m
+            acc[v] = acc[v] + jnp.sum(q.reshape(8, 8, width), axis=0)
+        for r in range(128 * step // 24, 128 * (step + 1) // 24):
+            hit = [n == r for n in line]
             for v in range(5):
-                q = (p[64 * v : 64 * v + 64] + p[320 + 64 * v : 384 + 64 * v]) * m
-                acc[v] = acc[v] + jnp.sum(q.reshape(8, 8, width), axis=0)
-        for v in range(5):
-            parts[v].append(jnp.sum(acc[v], axis=0, keepdims=True))
+                at = (r // 2) * 10 + v * 2 + r % 2
+                values = jnp.broadcast_to(rec_ref[at : at + 1, :], (8, LANES))
+                for t in range(2):
+                    found[v][t] = jnp.where(hit[t], lane_pick(values, lane[t]), found[v][t])
+        if k == 7:
+            for v in range(5):
+                parts[v].append(jnp.sum(acc[v], axis=0, keepdims=True))
+    for v in range(5):
+        for t in range(2):
+            weighted = found[v][t] * w_ref[:, tiles[t]]
+            parts[v].append(jnp.sum(weighted, axis=0, keepdims=True))
     values = [jnp.concatenate(p, axis=1) for p in parts]
 
     cell = cell_ref[...]

time: 55.9 us -> 55.6 us (level)
  transfers between devices with their start and end apart: 12 -> 12, of which waited for: 7 -> 7; matrix products, arithmetic and copies ran while one was open for 0% -> 0% of each run, Pallas kernels for 9% -> 8%
where the time goes in v6:
time: 55.6 us; the launch traced here: 55.3 us
  starting transfers between devices  27.5 us (49%)
  waiting for transfers between devices  16.8 us (30%)
  Pallas kernels  8.58 us (15%)
  local copies, waits for them, and re-layouts  1.4 us (3%)
  other arithmetic  0.76 us (1%)
    ppermute x10, starting transfers between devices, ring(): lax.ppermute(x, axis, [(i, (i + steps) % count) for i in range(count)])  15.2 us
    all_to_all x1, starting transfers between devices, on_device(): lax.all_to_all(sent, ('cy', 'cz'), split_axis=0, concat_axis=0, tiled=True)  11.9 us
    ppermute x10, waiting for transfers between devices, ring(): lax.ppermute(x, axis, [(i, (i + steps) % count) for i in range(count)])  6.89 us
    all_to_all x1, waiting for transfers between devices, on_device(): lax.all_to_all(sent, ('cy', 'cz'), split_axis=0, concat_axis=0, tiled=True)  6.16 us
    pallas_call x4, Pallas kernels, call(): pl.pallas_call(kernel, out_shape=outs, in_specs=specs, out_specs=jax.tree...  4.62 us
    ppermute x1, waiting for transfers between devices, on_device(): lax.ppermute(theirs, 'stream', [(i, i ^ 1) for i in range(lax.axis_size('...  3.77 us
    pallas_call x1, Pallas kernels, on_device(): pl.pallas_call(donor_kernel, out_shape=jax.ShapeDtypeStruct((640, LANES),...  3.6 us
    unnamed x19, local copies, waits for them, and re-layouts  1.4 us
  transfers between devices with their start and end apart: 12, of which 7 were waited for; matrix products, arithmetic and copies ran while one was open for 0% of the time, Pallas kernels for 8%

profile of v6, /device:TPU:32, one launch (start us, length us, event | category | flops | bytes accessed | tf_op | source)
XLA Modules:
  0.0 55.3 jit_solution(6213373778079166740)
XLA Ops:
  0.0 3.6 %donor_pick.1 = f32[640,128]{1,0:T(8,128)} custom-call(s32[64,256]{1,0:T(8,128)} %bitcast.41, s32[1,64]{1,0:T(1,128)} %bitcast.42, f32[160,128]{1,0:T(8,128)} %bitcast.30), custom_call_target="tpu_custom_call" | custom-call | tf_op jit(solution)/shard_map/donor_pick/pallas_call | solution.py:343
  3.6 11.9 %all-to-all-start = ((f32[64,1,1280]{2,1,0:T(1,128)}), f32[64,1,1280]{2,1,0:T(1,128)S(1)}, u32[]{:S(2)}, u32[]{:S(2)}) async-start(f32[64,1,1280]{2,1,0:T(1,128)} %bitcast.35), calls=%async_computation | async-start | bytes 655360 | tf_op jit(solution)/shard_map/all_to_all | solution.py:373
  15.6 0.7 %copy-done.1 = s32[2,16,128]{2,1,0:T(8,128)S(1)} copy-done((s32[2,16,128]{2,1,0:T(8,128)S(1)}, s32[2,16,128]{2,1,0:T(8,128)}, u32[]{:S(2)}) %copy-start.1) | copy-done | bytes 16408
  16.4 1.6 %collective-permute-start = (f32[26,2,8,128]{3,2,1,0:T(8,128)S(1)}, f32[26,2,8,128]{3,2,1,0:T(8,128)S(1)}, u32[]{:S(2)}, u32[]{:S(2)}) collective-permute-start(f32[26,2,8,128]{3,2,1,0:T(8,128)S(1)} %get-tuple-element.42), channel_id=1, source_target_pairs={{0,64},{64,128},{128,192},{192,0},{1,65},{65,129},{129,193},{193,1... | collective-permute-start | bytes 638984 | tf_op jit(solution)/shard_map/ppermute | solution.py:19
  17.9 1.8 %collective-permute-start.1 = (f32[26,2,8,128]{3,2,1,0:T(8,128)S(1)}, f32[26,2,8,128]{3,2,1,0:T(8,128)S(1)}, u32[]{:S(2)}, u32[]{:S(2)}) collective-permute-start(f32[26,2,8,128]{3,2,1,0:T(8,128)S(1)} %get-tuple-element.42), channel_id=1, source_target_pairs={{0,192},{64,0},{128,64},{192,128},{1,193},{65,1},{129,65},{193,129... | collective-permute-start | bytes 638984 | tf_op jit(solution)/shard_map/ppermute | solution.py:19
  19.7 1.8 %collective-permute-start.2 = (f32[26,2,8,128]{3,2,1,0:T(8,128)S(1)}, f32[26,2,8,128]{3,2,1,0:T(8,128)S(1)}, u32[]{:S(2)}, u32[]{:S(2)}) collective-permute-start(f32[26,2,8,128]{3,2,1,0:T(8,128)S(1)} %get-tuple-element.41), channel_id=1, source_target_pairs={{0,128},{64,192},{128,0},{192,64},{1,129},{65,193},{129,1},{193,65... | collective-permute-start | bytes 638984 | tf_op jit(solution)/shard_map/ppermute | solution.py:19
  21.5 0.6 %copy-done.6 = s32[1,1,1,1024]{3,2,1,0:T(1,128)S(1)} copy-done((s32[1,1,1,1024]{3,2,1,0:T(1,128)S(1)}, s32[1,1,1,1024]{3,2,1,0:T(1,128)}, u32[]{:S(2)}) %copy-start.6) | copy-done | bytes 4120
  22.2 1.1 %stage_lists.1 = (s32[8,1024]{1,0:T(8,128)S(1)}, f32[8,1024]{1,0:T(8,128)S(1)}, s32[1,1024]{1,0:T(1,128)S(1)}, f32[160,128]{1,0:T(8,128)S(1)}, f32[175,128]{1,0:T(8,128)S(1)}) custom-call(s32[8,1024]{1,0:T(8,128)S(1)} %bitcast.32, f32[8,1024]{1,0:T(8,128)S(1)} %bitcast.33, s32[1,1024]{1,0:T(1,128)S(1)} %bitcast.34, f32[160,128]{1,0:T(8,128)S(1)} %bitcast.31, ...), custom_call_target="tpu_custom_call" | custom-call | tf_op jit(solution)/shard_map/stage_lists/pallas_call | solution.py:23
  23.3 6.2 %all-to-all-done = f32[64,1,1280]{2,1,0:T(1,128)S(1)} async-done(((f32[64,1,1280]{2,1,0:T(1,128)}), f32[64,1,1280]{2,1,0:T(1,128)S(1)}, u32[]{:S(2)}, u32[]{:S(2)}) %all-to-all-start) | async-done | bytes 327712 | tf_op jit(solution)/shard_map/all_to_all | solution.py:373
  29.4 3.2 %ghost_fill.1 = (f32[160,128]{1,0:T(8,128)S(1)}, f32[2,10,128]{2,1,0:T(8,128)S(1)}, f32[2,10,128]{2,1,0:T(8,128)S(1)}) custom-call(f32[640,128]{1,0:T(8,128)S(1)} %bitcast.28, s32[8,1024]{1,0:T(8,128)S(1)} %get-tuple-element.23.src_ref, f32[8,1024]{1,0:T(8,128)S(1)} %get-tuple-element.24.w_ref, s32[1,1024]{1,0:T(1,128)S(1)} %get-tuple-element.25.cell_ref, ...), custom_call_target="tpu_custom_call" | custom-call | tf_op jit(solution)/shard_map/ghost_fill/pallas_call | solution.py:23
  32.7 2.9 %collective-permute-start.4 = (f32[10,128]{1,0:T(8,128)S(1)}, f32[10,128]{1,0:T(8,128)S(1)}, u32[]{:S(2)}, u32[]{:S(2)}) collective-permute-start(f32[10,128]{1,0:T(8,128)S(1)} %get-tuple-element.47), channel_id=1, source_target_pairs={{0,56},{8,0},{16,8},{24,16},{32,24},{40,32},{48,40},{56,48},{1,57}... | collective-permute-start | bytes 15368 | tf_op jit(solution)/shard_map/ppermute | solution.py:19
  35.6 1.0 %collective-permute-start.5 = (f32[10,128]{1,0:T(8,128)S(1)}, f32[10,128]{1,0:T(8,128)S(1)}, u32[]{:S(2)}, u32[]{:S(2)}) collective-permute-start(f32[10,128]{1,0:T(8,128)S(1)} %get-tuple-element.46), channel_id=1, source_target_pairs={{0,1},{1,2},{2,3},{3,4},{4,5},{5,6},{6,7},{7,0},{8,9},{9,10},{10,1... | collective-permute-start | bytes 15368 | tf_op jit(solution)/shard_map/ppermute | solution.py:19
  36.7 1.0 %collective-permute-start.6 = (f32[10,128]{1,0:T(8,128)S(1)}, f32[10,128]{1,0:T(8,128)S(1)}, u32[]{:S(2)}, u32[]{:S(2)}) collective-permute-start(f32[10,128]{1,0:T(8,128)S(1)} %get-tuple-element.45), channel_id=1, source_target_pairs={{0,7},{1,0},{2,1},{3,2},{4,3},{5,4},{6,5},{7,6},{8,15},{9,8},{10,9... | collective-permute-start | bytes 15368 | tf_op jit(solution)/shard_map/ppermute | solution.py:19
  37.9 1.4 %collective-permute-done.5.zm_ref = f32[10,128]{1,0:T(8,128)S(1)} collective-permute-done((f32[10,128]{1,0:T(8,128)S(1)}, f32[10,128]{1,0:T(8,128)S(1)}, u32[]{:S(2)}, u32[]{:S(2)}) %collective-permute-start.5) | collective-permute-done | bytes 5152 | tf_op jit(solution)/shard_map/ppermute | solution.py:19
  39.3 1.0 %collective-permute-done.6.zp_ref = f32[10,128]{1,0:T(8,128)S(1)} collective-permute-done((f32[10,128]{1,0:T(8,128)S(1)}, f32[10,128]{1,0:T(8,128)S(1)}, u32[]{:S(2)}, u32[]{:S(2)}) %collective-permute-start.6) | collective-permute-done | bytes 5152 | tf_op jit(solution)/shard_map/ppermute | solution.py:19
  40.5 1.6 %collective-permute-start.7 = (f32[4,5,8,128]{3,2,1,0:T(8,128)S(1)}, f32[4,5,8,128]{3,2,1,0:T(8,128)S(1)}, u32[]{:S(2)}, u32[]{:S(2)}) collective-permute-start(f32[4,5,8,128]{3,2,1,0:T(8,128)S(1)} %get-tuple-element.35), channel_id=1, source_target_pairs={{0,64},{64,128},{128,192},{192,0},{1,65},{65,129},{129,193},{193,1... | collective-permute-start | bytes 245768 | tf_op jit(solution)/shard_map/ppermute | solution.py:19
  42.0 1.8 %collective-permute-start.8 = (f32[4,5,8,128]{3,2,1,0:T(8,128)S(1)}, f32[4,5,8,128]{3,2,1,0:T(8,128)S(1)}, u32[]{:S(2)}, u32[]{:S(2)}) collective-permute-start(f32[4,5,8,128]{3,2,1,0:T(8,128)S(1)} %get-tuple-element.35), channel_id=1, source_target_pairs={{0,192},{64,0},{128,64},{192,128},{1,193},{65,1},{129,65},{193,129... | collective-permute-start | bytes 245768 | tf_op jit(solution)/shard_map/ppermute | solution.py:19
  43.8 1.8 %collective-permute-start.9 = (f32[4,5,8,128]{3,2,1,0:T(8,128)S(1)}, f32[4,5,8,128]{3,2,1,0:T(8,128)S(1)}, u32[]{:S(2)}, u32[]{:S(2)}) collective-permute-start(f32[4,5,8,128]{3,2,1,0:T(8,128)S(1)} %get-tuple-element.34.res_ref), channel_id=1, source_target_pairs={{0,128},{64,192},{128,0},{192,64},{1,129},{65,193},{129,1},{193,65... | collective-permute-start | bytes 245768 | tf_op jit(solution)/shard_map/ppermute | solution.py:19
  45.7 0.5 collective-permute-done.7.prev_ref
  46.5 3.7 %collective-permute-done.9.far_ref = f32[4,5,8,128]{3,2,1,0:T(8,128)S(1)} collective-permute-done((f32[4,5,8,128]{3,2,1,0:T(8,128)S(1)}, f32[4,5,8,128]{3,2,1,0:T(8,128)S(1)}, u32[]{:S(2)}, u32[]{:S(2)}) %collective-permute-start.9) | collective-permute-done | bytes 81952 | tf_op jit(solution)/shard_map/ppermute | solution.py:19
  50.1 0.4 sweeps.1
  50.5 0.3 collective-permute-start.10
  50.8 3.8 %collective-permute-done.10 = f32[5,2,8,128]{3,2,1,0:T(8,128)S(1)} collective-permute-done((f32[5,2,8,128]{3,2,1,0:T(8,128)S(1)}, f32[5,2,8,128]{3,2,1,0:T(8,128)S(1)}, u32[]{:S(2)}, u32[]{:S(2)}) %collective-permute-start.10) | collective-permute-done | bytes 40992 | tf_op jit(solution)/shard_map/ppermute | solution.py:428
  54.6 0.7 %fusion.2 = f32[5,2,16,128]{3,2,1,0:T(8,128)} fusion(f32[5,2,16,128]{3,2,1,0:T(8,128)S(1)} %bitcast.29, f32[5,2,8,128]{3,2,1,0:T(8,128)S(1)} %get-tuple-element.44, f32[5,2,8,128]{3,2,1,0:T(8,128)S(1)} %get-tuple-element.43, f32[2,16,128]{2,1,0:T(8,128)S(1)} %convert_multiply_fusion), kind=kLoop, calls=%fused_computation.8 | loop fusion | flops 61440 | bytes 262144 | tf_op jit(solution)/shard_map/add | solution.py:434
  (33 shorter events, 0.8 us)
Async XLA Ops:
  3.6 12.7 %copy-start.7 = (f32[5,5,2,16,128]{4,3,2,1,0:T(8,128)S(1)}, f32[5,5,2,16,128]{4,3,2,1,0:T(8,128)}, u32[]{:S(2)}) copy-start(f32[5,5,2,16,128]{4,3,2,1,0:T(8,128)} %param.14) | copy-start | bytes 1228804
  3.6 25.8 %all-to-all-start = ((f32[64,1,1280]{2,1,0:T(1,128)}), f32[64,1,1280]{2,1,0:T(1,128)S(1)}, u32[]{:S(2)}, u32[]{:S(2)}) async-start(f32[64,1,1280]{2,1,0:T(1,128)} %bitcast.35), calls=%async_computation | async-start | bytes 655360 | tf_op jit(solution)/shard_map/all_to_all | solution.py:373
  15.5 0.7 %copy-start.1 = (s32[2,16,128]{2,1,0:T(8,128)S(1)}, s32[2,16,128]{2,1,0:T(8,128)}, u32[]{:S(2)}) copy-start(s32[2,16,128]{2,1,0:T(8,128)} %fluid_ref.1) | copy-start | bytes 49156
  16.3 5.2 %copy-start.8 = (f32[7,5,5]{2,0,1:T(8,128)S(1)}, f32[7,5,5]{2,0,1:T(8,128)}, u32[]{:S(2)}) copy-start(f32[7,5,5]{2,0,1:T(8,128)} %param.15) | copy-start | bytes 2104
  16.3 5.2 %copy-start = (f32[5,2,16,128]{3,2,1,0:T(8,128)S(1)}, f32[5,2,16,128]{3,2,1,0:T(8,128)}, u32[]{:S(2)}) copy-start(f32[5,2,16,128]{3,2,1,0:T(8,128)} %param.11) | copy-start | bytes 245764
  16.3 5.2 %copy-start.5 = (f32[1,1,1,1024,8]{3,4,2,1,0:T(8,128)S(1)}, f32[1,1,1,1024,8]{3,4,2,1,0:T(8,128)}, u32[]{:S(2)}) copy-start(f32[1,1,1,1024,8]{3,4,2,1,0:T(8,128)} %param.21) | copy-start | bytes 98308
  16.4 5.2 %copy-start.4 = (s32[1,1,1,1024,8]{3,4,2,1,0:T(8,128)S(1)}, s32[1,1,1,1024,8]{3,4,2,1,0:T(8,128)}, u32[]{:S(2)}) copy-start(s32[1,1,1,1024,8]{3,4,2,1,0:T(8,128)} %param.20) | copy-start | bytes 98308
  16.4 16.3 %collective-permute-start = (f32[26,2,8,128]{3,2,1,0:T(8,128)S(1)}, f32[26,2,8,128]{3,2,1,0:T(8,128)S(1)}, u32[]{:S(2)}, u32[]{:S(2)}) collective-permute-start(f32[26,2,8,128]{3,2,1,0:T(8,128)S(1)} %get-tuple-element.42), channel_id=1, source_target_pairs={{0,64},{64,128},{128,192},{192,0},{1,65},{65,129},{129,193},{193,1... | collective-permute-start | bytes 638984 | tf_op jit(solution)/shard_map/ppermute | solution.py:19
  17.9 14.7 %collective-permute-start.1 = (f32[26,2,8,128]{3,2,1,0:T(8,128)S(1)}, f32[26,2,8,128]{3,2,1,0:T(8,128)S(1)}, u32[]{:S(2)}, u32[]{:S(2)}) collective-permute-start(f32[26,2,8,128]{3,2,1,0:T(8,128)S(1)} %get-tuple-element.42), channel_id=1, source_target_pairs={{0,192},{64,0},{128,64},{192,128},{1,193},{65,1},{129,65},{193,129... | collective-permute-start | bytes 638984 | tf_op jit(solution)/shard_map/ppermute | solution.py:19
  19.7 13.0 %collective-permute-start.2 = (f32[26,2,8,128]{3,2,1,0:T(8,128)S(1)}, f32[26,2,8,128]{3,2,1,0:T(8,128)S(1)}, u32[]{:S(2)}, u32[]{:S(2)}) collective-permute-start(f32[26,2,8,128]{3,2,1,0:T(8,128)S(1)} %get-tuple-element.41), channel_id=1, source_target_pairs={{0,128},{64,192},{128,0},{192,64},{1,129},{65,193},{129,1},{193,65... | collective-permute-start | bytes 638984 | tf_op jit(solution)/shard_map/ppermute | solution.py:19
  21.5 0.7 %copy-start.6 = (s32[1,1,1,1024]{3,2,1,0:T(1,128)S(1)}, s32[1,1,1,1024]{3,2,1,0:T(1,128)}, u32[]{:S(2)}) copy-start(s32[1,1,1,1024]{3,2,1,0:T(1,128)} %param.19) | copy-start | bytes 12292
  29.4 8.2 %copy-start.2 = (f32[5,2,16,128]{3,2,1,0:T(8,128)S(1)}, f32[5,2,16,128]{3,2,1,0:T(8,128)}, u32[]{:S(2)}) copy-start(f32[5,2,16,128]{3,2,1,0:T(8,128)} %source_ref.1) | copy-start | bytes 245764
  29.4 8.2 %copy-start.3 = (f32[5,2,16,128]{3,2,1,0:T(8,128)S(1)}, f32[5,2,16,128]{3,2,1,0:T(8,128)}, u32[]{:S(2)}) copy-start(f32[5,2,16,128]{3,2,1,0:T(8,128)} %scale_ref.1) | copy-start | bytes 245764
  32.7 5.2 %collective-permute-start.3 = (f32[10,128]{1,0:T(8,128)S(1)}, f32[10,128]{1,0:T(8,128)S(1)}, u32[]{:S(2)}, u32[]{:S(2)}) collective-permute-start(f32[10,128]{1,0:T(8,128)S(1)} %get-tuple-element.48), channel_id=1, source_target_pairs={{0,8},{8,16},{16,24},{24,32},{32,40},{40,48},{48,56},{56,0},{1,9},... | collective-permute-start | bytes 15368 | tf_op jit(solution)/shard_map/ppermute | solution.py:19
  32.7 5.2 %collective-permute-start.4 = (f32[10,128]{1,0:T(8,128)S(1)}, f32[10,128]{1,0:T(8,128)S(1)}, u32[]{:S(2)}, u32[]{:S(2)}) collective-permute-start(f32[10,128]{1,0:T(8,128)S(1)} %get-tuple-element.47), channel_id=1, source_target_pairs={{0,56},{8,0},{16,8},{24,16},{32,24},{40,32},{48,40},{56,48},{1,57}... | collective-permute-start | bytes 15368 | tf_op jit(solution)/shard_map/ppermute | solution.py:19
  35.6 3.7 %collective-permute-start.5 = (f32[10,128]{1,0:T(8,128)S(1)}, f32[10,128]{1,0:T(8,128)S(1)}, u32[]{:S(2)}, u32[]{:S(2)}) collective-permute-start(f32[10,128]{1,0:T(8,128)S(1)} %get-tuple-element.46), channel_id=1, source_target_pairs={{0,1},{1,2},{2,3},{3,4},{4,5},{5,6},{6,7},{7,0},{8,9},{9,10},{10,1... | collective-permute-start | bytes 15368 | tf_op jit(solution)/shard_map/ppermute | solution.py:19
  36.7 3.7 %collective-permute-start.6 = (f32[10,128]{1,0:T(8,128)S(1)}, f32[10,128]{1,0:T(8,128)S(1)}, u32[]{:S(2)}, u32[]{:S(2)}) collective-permute-start(f32[10,128]{1,0:T(8,128)S(1)} %get-tuple-element.45), channel_id=1, source_target_pairs={{0,7},{1,0},{2,1},{3,2},{4,3},{5,4},{6,5},{7,6},{8,15},{9,8},{10,9... | collective-permute-start | bytes 15368 | tf_op jit(solution)/shard_map/ppermute | solution.py:19
  40.5 5.7 %collective-permute-start.7 = (f32[4,5,8,128]{3,2,1,0:T(8,128)S(1)}, f32[4,5,8,128]{3,2,1,0:T(8,128)S(1)}, u32[]{:S(2)}, u32[]{:S(2)}) collective-permute-start(f32[4,5,8,128]{3,2,1,0:T(8,128)S(1)} %get-tuple-element.35), channel_id=1, source_target_pairs={{0,64},{64,128},{128,192},{192,0},{1,65},{65,129},{129,193},{193,1... | collective-permute-start | bytes 245768 | tf_op jit(solution)/shard_map/ppermute | solution.py:19
  42.0 4.4 %collective-permute-start.8 = (f32[4,5,8,128]{3,2,1,0:T(8,128)S(1)}, f32[4,5,8,128]{3,2,1,0:T(8,128)S(1)}, u32[]{:S(2)}, u32[]{:S(2)}) collective-permute-start(f32[4,5,8,128]{3,2,1,0:T(8,128)S(1)} %get-tuple-element.35), channel_id=1, source_target_pairs={{0,192},{64,0},{128,64},{192,128},{1,193},{65,1},{129,65},{193,129... | collective-permute-start | bytes 245768 | tf_op jit(solution)/shard_map/ppermute | solution.py:19
  43.8 6.3 %collective-permute-start.9 = (f32[4,5,8,128]{3,2,1,0:T(8,128)S(1)}, f32[4,5,8,128]{3,2,1,0:T(8,128)S(1)}, u32[]{:S(2)}, u32[]{:S(2)}) collective-permute-start(f32[4,5,8,128]{3,2,1,0:T(8,128)S(1)} %get-tuple-element.34.res_ref), channel_id=1, source_target_pairs={{0,128},{64,192},{128,0},{192,64},{1,129},{65,193},{129,1},{193,65... | collective-permute-start | bytes 245768 | tf_op jit(solution)/shard_map/ppermute | solution.py:19
  50.5 4.1 %collective-permute-start.10 = (f32[5,2,8,128]{3,2,1,0:T(8,128)S(1)}, f32[5,2,8,128]{3,2,1,0:T(8,128)S(1)}, u32[]{:S(2)}, u32[]{:S(2)}) collective-permute-start(f32[5,2,8,128]{3,2,1,0:T(8,128)S(1)} %get-tuple-element.40), channel_id=1, source_target_pairs={{0,64},{64,0},{128,192},{192,128},{1,65},{65,1},{129,193},{193,129... | collective-permute-start | bytes 122888 | tf_op jit(solution)/shard_map/ppermute | solution.py:428

commit v7 on v6

--- a/solution.py
+++ b/solution.py
@@ -158,16 +158,13 @@
     cell = cell_ref[...]
     in_row = lax.broadcasted_iota(jnp.int32, (32, 1024), 0) == (cell >> 7)
     in_lane = lax.broadcasted_iota(jnp.int32, (LANES, 1024), 0) == (cell & (LANES - 1))
-    pieces = [[], [], []]
+    pieces = [[], []]
     for v in range(5):
         x = jnp.where(in_row, values[v], 0.0)
         hi = x.astype(BF16)
-        rest = x - hi.astype(F32)
-        mid = rest.astype(BF16)
         pieces[0].append(hi)
-        pieces[1].append(mid)
-        pieces[2].append((rest - mid.astype(F32)).astype(BF16))
-    left = jnp.concatenate([in_row.astype(BF16)] + pieces[0] + pieces[1] + pieces[2], axis=0)
+        pieces[1].append((x - hi.astype(F32)).astype(BF16))
+    left = jnp.concatenate([in_row.astype(BF16)] + pieces[0] + pieces[1], axis=0)
     placed = lax.dot_general(
         left, in_lane.astype(BF16), (((1,), (1,)), ((), ())), preferred_element_type=F32
     )
@@ -176,9 +173,9 @@
         jnp.int32, (16, LANES), 1
     )
     for v in range(5):
-        hi, mid, lo = (placed[32 * (1 + v + 5 * p) : 32 * (2 + v + 5 * p)] for p in range(3))
+        hi, lo = (placed[32 * (1 + v + 5 * p) : 32 * (2 + v + 5 * p)] for p in range(2))
         old = state_ref[32 * v : 32 * v + 32, :]
-        new = jnp.where(covered, hi + (mid + lo), old)
+        new = jnp.where(covered, hi + lo, old)
         f_ref[32 * v : 32 * v + 32, :] = new
         for x in range(2):
             plane = new[16 * x : 16 * x + 16]

time: 55.6 us -> 55.3 us (level)
  no operation moved by 1% of the time
where the time goes in v7:
time: 55.3 us; the launch traced here: 55 us
  starting transfers between devices  27.5 us (50%)
  waiting for transfers between devices  16.8 us (30%)
  Pallas kernels  8.34 us (15%)
  local copies, waits for them, and re-layouts  1.4 us (3%)
  other arithmetic  0.76 us (1%)
    ppermute x10, starting transfers between devices, ring(): lax.ppermute(x, axis, [(i, (i + steps) % count) for i in range(count)])  15.2 us
    all_to_all x1, starting transfers between devices, on_device(): lax.all_to_all(sent, ('cy', 'cz'), split_axis=0, concat_axis=0, tiled=True)  11.9 us
    ppermute x10, waiting for transfers between devices, ring(): lax.ppermute(x, axis, [(i, (i + steps) % count) for i in range(count)])  6.88 us
    all_to_all x1, waiting for transfers between devices, on_device(): lax.all_to_all(sent, ('cy', 'cz'), split_axis=0, concat_axis=0, tiled=True)  6.16 us
    pallas_call x4, Pallas kernels, call(): pl.pallas_call(kernel, out_shape=outs, in_specs=specs, out_specs=jax.tree...  4.38 us
    ppermute x1, waiting for transfers between devices, on_device(): lax.ppermute(theirs, 'stream', [(i, i ^ 1) for i in range(lax.axis_size('...  3.77 us
    pallas_call x1, Pallas kernels, on_device(): pl.pallas_call(donor_kernel, out_shape=jax.ShapeDtypeStruct((640, LANES),...  3.6 us
    unnamed x19, local copies, waits for them, and re-layouts  1.4 us
  transfers between devices with their start and end apart: 12, of which 7 were waited for; matrix products, arithmetic and copies ran while one was open for 0% of the time, Pallas kernels for 8%

profile of v7, /device:TPU:32, one launch (start us, length us, event | category | flops | bytes accessed | tf_op | source)
XLA Modules:
  0.0 55.0 jit_solution(17003420491558197279)
XLA Ops:
  0.0 3.6 %donor_pick.1 = f32[640,128]{1,0:T(8,128)} custom-call(s32[64,256]{1,0:T(8,128)} %bitcast.41, s32[1,64]{1,0:T(1,128)} %bitcast.42, f32[160,128]{1,0:T(8,128)} %bitcast.30), custom_call_target="tpu_custom_call" | custom-call | tf_op jit(solution)/shard_map/donor_pick/pallas_call | solution.py:340
  3.6 11.9 %all-to-all-start = ((f32[64,1,1280]{2,1,0:T(1,128)}), f32[64,1,1280]{2,1,0:T(1,128)S(1)}, u32[]{:S(2)}, u32[]{:S(2)}) async-start(f32[64,1,1280]{2,1,0:T(1,128)} %bitcast.35), calls=%async_computation | async-start | bytes 655360 | tf_op jit(solution)/shard_map/all_to_all | solution.py:370
  15.6 0.7 %copy-done.1 = s32[2,16,128]{2,1,0:T(8,128)S(1)} copy-done((s32[2,16,128]{2,1,0:T(8,128)S(1)}, s32[2,16,128]{2,1,0:T(8,128)}, u32[]{:S(2)}) %copy-start.1) | copy-done | bytes 16408
  16.4 1.6 %collective-permute-start = (f32[26,2,8,128]{3,2,1,0:T(8,128)S(1)}, f32[26,2,8,128]{3,2,1,0:T(8,128)S(1)}, u32[]{:S(2)}, u32[]{:S(2)}) collective-permute-start(f32[26,2,8,128]{3,2,1,0:T(8,128)S(1)} %get-tuple-element.42), channel_id=1, source_target_pairs={{0,64},{64,128},{128,192},{192,0},{1,65},{65,129},{129,193},{193,1... | collective-permute-start | bytes 638984 | tf_op jit(solution)/shard_map/ppermute | solution.py:19
  17.9 1.8 %collective-permute-start.1 = (f32[26,2,8,128]{3,2,1,0:T(8,128)S(1)}, f32[26,2,8,128]{3,2,1,0:T(8,128)S(1)}, u32[]{:S(2)}, u32[]{:S(2)}) collective-permute-start(f32[26,2,8,128]{3,2,1,0:T(8,128)S(1)} %get-tuple-element.42), channel_id=1, source_target_pairs={{0,192},{64,0},{128,64},{192,128},{1,193},{65,1},{129,65},{193,129... | collective-permute-start | bytes 638984 | tf_op jit(solution)/shard_map/ppermute | solution.py:19
  19.7 1.8 %collective-permute-start.2 = (f32[26,2,8,128]{3,2,1,0:T(8,128)S(1)}, f32[26,2,8,128]{3,2,1,0:T(8,128)S(1)}, u32[]{:S(2)}, u32[]{:S(2)}) collective-permute-start(f32[26,2,8,128]{3,2,1,0:T(8,128)S(1)} %get-tuple-element.41), channel_id=1, source_target_pairs={{0,128},{64,192},{128,0},{192,64},{1,129},{65,193},{129,1},{193,65... | collective-permute-start | bytes 638984 | tf_op jit(solution)/shard_map/ppermute | solution.py:19
  21.5 0.6 %copy-done.6 = s32[1,1,1,1024]{3,2,1,0:T(1,128)S(1)} copy-done((s32[1,1,1,1024]{3,2,1,0:T(1,128)S(1)}, s32[1,1,1,1024]{3,2,1,0:T(1,128)}, u32[]{:S(2)}) %copy-start.6) | copy-done | bytes 4120
  22.2 1.1 %stage_lists.1 = (s32[8,1024]{1,0:T(8,128)S(1)}, f32[8,1024]{1,0:T(8,128)S(1)}, s32[1,1024]{1,0:T(1,128)S(1)}, f32[160,128]{1,0:T(8,128)S(1)}, f32[175,128]{1,0:T(8,128)S(1)}) custom-call(s32[8,1024]{1,0:T(8,128)S(1)} %bitcast.32, f32[8,1024]{1,0:T(8,128)S(1)} %bitcast.33, s32[1,1024]{1,0:T(1,128)S(1)} %bitcast.34, f32[160,128]{1,0:T(8,128)S(1)} %bitcast.31, ...), custom_call_target="tpu_custom_call" | custom-call | tf_op jit(solution)/shard_map/stage_lists/pallas_call | solution.py:23
  23.3 6.2 %all-to-all-done = f32[64,1,1280]{2,1,0:T(1,128)S(1)} async-done(((f32[64,1,1280]{2,1,0:T(1,128)}), f32[64,1,1280]{2,1,0:T(1,128)S(1)}, u32[]{:S(2)}, u32[]{:S(2)}) %all-to-all-start) | async-done | bytes 327712 | tf_op jit(solution)/shard_map/all_to_all | solution.py:370
  29.4 3.0 %ghost_fill.1 = (f32[160,128]{1,0:T(8,128)S(1)}, f32[2,10,128]{2,1,0:T(8,128)S(1)}, f32[2,10,128]{2,1,0:T(8,128)S(1)}) custom-call(f32[640,128]{1,0:T(8,128)S(1)} %bitcast.28, s32[8,1024]{1,0:T(8,128)S(1)} %get-tuple-element.23.src_ref, f32[8,1024]{1,0:T(8,128)S(1)} %get-tuple-element.24.w_ref, s32[1,1024]{1,0:T(1,128)S(1)} %get-tuple-element.25.cell_ref, ...), custom_call_target="tpu_custom_call" | custom-call | tf_op jit(solution)/shard_map/ghost_fill/pallas_call | solution.py:23
  32.5 2.9 %collective-permute-start.4 = (f32[10,128]{1,0:T(8,128)S(1)}, f32[10,128]{1,0:T(8,128)S(1)}, u32[]{:S(2)}, u32[]{:S(2)}) collective-permute-start(f32[10,128]{1,0:T(8,128)S(1)} %get-tuple-element.47), channel_id=1, source_target_pairs={{0,56},{8,0},{16,8},{24,16},{32,24},{40,32},{48,40},{56,48},{1,57}... | collective-permute-start | bytes 15368 | tf_op jit(solution)/shard_map/ppermute | solution.py:19
  35.4 1.0 %collective-permute-start.5 = (f32[10,128]{1,0:T(8,128)S(1)}, f32[10,128]{1,0:T(8,128)S(1)}, u32[]{:S(2)}, u32[]{:S(2)}) collective-permute-start(f32[10,128]{1,0:T(8,128)S(1)} %get-tuple-element.46), channel_id=1, source_target_pairs={{0,1},{1,2},{2,3},{3,4},{4,5},{5,6},{6,7},{7,0},{8,9},{9,10},{10,1... | collective-permute-start | bytes 15368 | tf_op jit(solution)/shard_map/ppermute | solution.py:19
  36.4 1.0 %collective-permute-start.6 = (f32[10,128]{1,0:T(8,128)S(1)}, f32[10,128]{1,0:T(8,128)S(1)}, u32[]{:S(2)}, u32[]{:S(2)}) collective-permute-start(f32[10,128]{1,0:T(8,128)S(1)} %get-tuple-element.45), channel_id=1, source_target_pairs={{0,7},{1,0},{2,1},{3,2},{4,3},{5,4},{6,5},{7,6},{8,15},{9,8},{10,9... | collective-permute-start | bytes 15368 | tf_op jit(solution)/shard_map/ppermute | solution.py:19
  37.7 1.4 %collective-permute-done.5.zm_ref = f32[10,128]{1,0:T(8,128)S(1)} collective-permute-done((f32[10,128]{1,0:T(8,128)S(1)}, f32[10,128]{1,0:T(8,128)S(1)}, u32[]{:S(2)}, u32[]{:S(2)}) %collective-permute-start.5) | collective-permute-done | bytes 5152 | tf_op jit(solution)/shard_map/ppermute | solution.py:19
  39.1 1.0 %collective-permute-done.6.zp_ref = f32[10,128]{1,0:T(8,128)S(1)} collective-permute-done((f32[10,128]{1,0:T(8,128)S(1)}, f32[10,128]{1,0:T(8,128)S(1)}, u32[]{:S(2)}, u32[]{:S(2)}) %collective-permute-start.6) | collective-permute-done | bytes 5152 | tf_op jit(solution)/shard_map/ppermute | solution.py:19
  40.2 1.6 %collective-permute-start.7 = (f32[4,5,8,128]{3,2,1,0:T(8,128)S(1)}, f32[4,5,8,128]{3,2,1,0:T(8,128)S(1)}, u32[]{:S(2)}, u32[]{:S(2)}) collective-permute-start(f32[4,5,8,128]{3,2,1,0:T(8,128)S(1)} %get-tuple-element.35), channel_id=1, source_target_pairs={{0,64},{64,128},{128,192},{192,0},{1,65},{65,129},{129,193},{193,1... | collective-permute-start | bytes 245768 | tf_op jit(solution)/shard_map/ppermute | solution.py:19
  41.8 1.8 %collective-permute-start.8 = (f32[4,5,8,128]{3,2,1,0:T(8,128)S(1)}, f32[4,5,8,128]{3,2,1,0:T(8,128)S(1)}, u32[]{:S(2)}, u32[]{:S(2)}) collective-permute-start(f32[4,5,8,128]{3,2,1,0:T(8,128)S(1)} %get-tuple-element.35), channel_id=1, source_target_pairs={{0,192},{64,0},{128,64},{192,128},{1,193},{65,1},{129,65},{193,129... | collective-permute-start | bytes 245768 | tf_op jit(solution)/shard_map/ppermute | solution.py:19
  43.6 1.8 %collective-permute-start.9 = (f32[4,5,8,128]{3,2,1,0:T(8,128)S(1)}, f32[4,5,8,128]{3,2,1,0:T(8,128)S(1)}, u32[]{:S(2)}, u32[]{:S(2)}) collective-permute-start(f32[4,5,8,128]{3,2,1,0:T(8,128)S(1)} %get-tuple-element.34.res_ref), channel_id=1, source_target_pairs={{0,128},{64,192},{128,0},{192,64},{1,129},{65,193},{129,1},{193,65... | collective-permute-start | bytes 245768 | tf_op jit(solution)/shard_map/ppermute | solution.py:19
  45.4 0.5 collective-permute-done.7.prev_ref
  46.2 3.7 %collective-permute-done.9.far_ref = f32[4,5,8,128]{3,2,1,0:T(8,128)S(1)} collective-permute-done((f32[4,5,8,128]{3,2,1,0:T(8,128)S(1)}, f32[4,5,8,128]{3,2,1,0:T(8,128)S(1)}, u32[]{:S(2)}, u32[]{:S(2)}) %collective-permute-start.9) | collective-permute-done | bytes 81952 | tf_op jit(solution)/shard_map/ppermute | solution.py:19
  49.9 0.4 sweeps.1
  50.3 0.3 collective-permute-start.10
  50.6 3.8 %collective-permute-done.10 = f32[5,2,8,128]{3,2,1,0:T(8,128)S(1)} collective-permute-done((f32[5,2,8,128]{3,2,1,0:T(8,128)S(1)}, f32[5,2,8,128]{3,2,1,0:T(8,128)S(1)}, u32[]{:S(2)}, u32[]{:S(2)}) %collective-permute-start.10) | collective-permute-done | bytes 40992 | tf_op jit(solution)/shard_map/ppermute | solution.py:425
  54.4 0.7 %fusion.2 = f32[5,2,16,128]{3,2,1,0:T(8,128)} fusion(f32[5,2,16,128]{3,2,1,0:T(8,128)S(1)} %bitcast.29, f32[5,2,8,128]{3,2,1,0:T(8,128)S(1)} %get-tuple-element.44, f32[5,2,8,128]{3,2,1,0:T(8,128)S(1)} %get-tuple-element.43, f32[2,16,128]{2,1,0:T(8,128)S(1)} %convert_multiply_fusion), kind=kLoop, calls=%fused_computation.8 | loop fusion | flops 61440 | bytes 262144 | tf_op jit(solution)/shard_map/add | solution.py:431
  (33 shorter events, 0.8 us)
Async XLA Ops:
  3.6 12.7 %copy-start.7 = (f32[5,5,2,16,128]{4,3,2,1,0:T(8,128)S(1)}, f32[5,5,2,16,128]{4,3,2,1,0:T(8,128)}, u32[]{:S(2)}) copy-start(f32[5,5,2,16,128]{4,3,2,1,0:T(8,128)} %param.14) | copy-start | bytes 1228804
  3.6 25.8 %all-to-all-start = ((f32[64,1,1280]{2,1,0:T(1,128)}), f32[64,1,1280]{2,1,0:T(1,128)S(1)}, u32[]{:S(2)}, u32[]{:S(2)}) async-start(f32[64,1,1280]{2,1,0:T(1,128)} %bitcast.35), calls=%async_computation | async-start | bytes 655360 | tf_op jit(solution)/shard_map/all_to_all | solution.py:370
  15.5 0.7 %copy-start.1 = (s32[2,16,128]{2,1,0:T(8,128)S(1)}, s32[2,16,128]{2,1,0:T(8,128)}, u32[]{:S(2)}) copy-start(s32[2,16,128]{2,1,0:T(8,128)} %fluid_ref.1) | copy-start | bytes 49156
  16.3 5.2 %copy-start.8 = (f32[7,5,5]{2,0,1:T(8,128)S(1)}, f32[7,5,5]{2,0,1:T(8,128)}, u32[]{:S(2)}) copy-start(f32[7,5,5]{2,0,1:T(8,128)} %param.15) | copy-start | bytes 2104
  16.3 5.2 %copy-start = (f32[5,2,16,128]{3,2,1,0:T(8,128)S(1)}, f32[5,2,16,128]{3,2,1,0:T(8,128)}, u32[]{:S(2)}) copy-start(f32[5,2,16,128]{3,2,1,0:T(8,128)} %param.11) | copy-start | bytes 245764
  16.3 5.2 %copy-start.5 = (f32[1,1,1,1024,8]{3,4,2,1,0:T(8,128)S(1)}, f32[1,1,1,1024,8]{3,4,2,1,0:T(8,128)}, u32[]{:S(2)}) copy-start(f32[1,1,1,1024,8]{3,4,2,1,0:T(8,128)} %param.21) | copy-start | bytes 98308
  16.4 5.2 %copy-start.4 = (s32[1,1,1,1024,8]{3,4,2,1,0:T(8,128)S(1)}, s32[1,1,1,1024,8]{3,4,2,1,0:T(8,128)}, u32[]{:S(2)}) copy-start(s32[1,1,1,1024,8]{3,4,2,1,0:T(8,128)} %param.20) | copy-start | bytes 98308
  16.4 16.0 %collective-permute-start = (f32[26,2,8,128]{3,2,1,0:T(8,128)S(1)}, f32[26,2,8,128]{3,2,1,0:T(8,128)S(1)}, u32[]{:S(2)}, u32[]{:S(2)}) collective-permute-start(f32[26,2,8,128]{3,2,1,0:T(8,128)S(1)} %get-tuple-element.42), channel_id=1, source_target_pairs={{0,64},{64,128},{128,192},{192,0},{1,65},{65,129},{129,193},{193,1... | collective-permute-start | bytes 638984 | tf_op jit(solution)/shard_map/ppermute | solution.py:19
  17.9 14.5 %collective-permute-start.1 = (f32[26,2,8,128]{3,2,1,0:T(8,128)S(1)}, f32[26,2,8,128]{3,2,1,0:T(8,128)S(1)}, u32[]{:S(2)}, u32[]{:S(2)}) collective-permute-start(f32[26,2,8,128]{3,2,1,0:T(8,128)S(1)} %get-tuple-element.42), channel_id=1, source_target_pairs={{0,192},{64,0},{128,64},{192,128},{1,193},{65,1},{129,65},{193,129... | collective-permute-start | bytes 638984 | tf_op jit(solution)/shard_map/ppermute | solution.py:19
  19.7 12.7 %collective-permute-start.2 = (f32[26,2,8,128]{3,2,1,0:T(8,128)S(1)}, f32[26,2,8,128]{3,2,1,0:T(8,128)S(1)}, u32[]{:S(2)}, u32[]{:S(2)}) collective-permute-start(f32[26,2,8,128]{3,2,1,0:T(8,128)S(1)} %get-tuple-element.41), channel_id=1, source_target_pairs={{0,128},{64,192},{128,0},{192,64},{1,129},{65,193},{129,1},{193,65... | collective-permute-start | bytes 638984 | tf_op jit(solution)/shard_map/ppermute | solution.py:19
  21.5 0.7 %copy-start.6 = (s32[1,1,1,1024]{3,2,1,0:T(1,128)S(1)}, s32[1,1,1,1024]{3,2,1,0:T(1,128)}, u32[]{:S(2)}) copy-start(s32[1,1,1,1024]{3,2,1,0:T(1,128)} %param.19) | copy-start | bytes 12292
  29.4 8.0 %copy-start.2 = (f32[5,2,16,128]{3,2,1,0:T(8,128)S(1)}, f32[5,2,16,128]{3,2,1,0:T(8,128)}, u32[]{:S(2)}) copy-start(f32[5,2,16,128]{3,2,1,0:T(8,128)} %source_ref.1) | copy-start | bytes 245764
  29.4 8.0 %copy-start.3 = (f32[5,2,16,128]{3,2,1,0:T(8,128)S(1)}, f32[5,2,16,128]{3,2,1,0:T(8,128)}, u32[]{:S(2)}) copy-start(f32[5,2,16,128]{3,2,1,0:T(8,128)} %scale_ref.1) | copy-start | bytes 245764
  32.4 5.2 %collective-permute-start.3 = (f32[10,128]{1,0:T(8,128)S(1)}, f32[10,128]{1,0:T(8,128)S(1)}, u32[]{:S(2)}, u32[]{:S(2)}) collective-permute-start(f32[10,128]{1,0:T(8,128)S(1)} %get-tuple-element.48), channel_id=1, source_target_pairs={{0,8},{8,16},{16,24},{24,32},{32,40},{40,48},{48,56},{56,0},{1,9},... | collective-permute-start | bytes 15368 | tf_op jit(solution)/shard_map/ppermute | solution.py:19
  32.5 5.2 %collective-permute-start.4 = (f32[10,128]{1,0:T(8,128)S(1)}, f32[10,128]{1,0:T(8,128)S(1)}, u32[]{:S(2)}, u32[]{:S(2)}) collective-permute-start(f32[10,128]{1,0:T(8,128)S(1)} %get-tuple-element.47), channel_id=1, source_target_pairs={{0,56},{8,0},{16,8},{24,16},{32,24},{40,32},{48,40},{56,48},{1,57}... | collective-permute-start | bytes 15368 | tf_op jit(solution)/shard_map/ppermute | solution.py:19
  35.4 3.7 %collective-permute-start.5 = (f32[10,128]{1,0:T(8,128)S(1)}, f32[10,128]{1,0:T(8,128)S(1)}, u32[]{:S(2)}, u32[]{:S(2)}) collective-permute-start(f32[10,128]{1,0:T(8,128)S(1)} %get-tuple-element.46), channel_id=1, source_target_pairs={{0,1},{1,2},{2,3},{3,4},{4,5},{5,6},{6,7},{7,0},{8,9},{9,10},{10,1... | collective-permute-start | bytes 15368 | tf_op jit(solution)/shard_map/ppermute | solution.py:19
  36.4 3.7 %collective-permute-start.6 = (f32[10,128]{1,0:T(8,128)S(1)}, f32[10,128]{1,0:T(8,128)S(1)}, u32[]{:S(2)}, u32[]{:S(2)}) collective-permute-start(f32[10,128]{1,0:T(8,128)S(1)} %get-tuple-element.45), channel_id=1, source_target_pairs={{0,7},{1,0},{2,1},{3,2},{4,3},{5,4},{6,5},{7,6},{8,15},{9,8},{10,9... | collective-permute-start | bytes 15368 | tf_op jit(solution)/shard_map/ppermute | solution.py:19
  40.2 5.7 %collective-permute-start.7 = (f32[4,5,8,128]{3,2,1,0:T(8,128)S(1)}, f32[4,5,8,128]{3,2,1,0:T(8,128)S(1)}, u32[]{:S(2)}, u32[]{:S(2)}) collective-permute-start(f32[4,5,8,128]{3,2,1,0:T(8,128)S(1)} %get-tuple-element.35), channel_id=1, source_target_pairs={{0,64},{64,128},{128,192},{192,0},{1,65},{65,129},{129,193},{193,1... | collective-permute-start | bytes 245768 | tf_op jit(solution)/shard_map/ppermute | solution.py:19
  41.8 4.4 %collective-permute-start.8 = (f32[4,5,8,128]{3,2,1,0:T(8,128)S(1)}, f32[4,5,8,128]{3,2,1,0:T(8,128)S(1)}, u32[]{:S(2)}, u32[]{:S(2)}) collective-permute-start(f32[4,5,8,128]{3,2,1,0:T(8,128)S(1)} %get-tuple-element.35), channel_id=1, source_target_pairs={{0,192},{64,0},{128,64},{192,128},{1,193},{65,1},{129,65},{193,129... | collective-permute-start | bytes 245768 | tf_op jit(solution)/shard_map/ppermute | solution.py:19
  43.6 6.3 %collective-permute-start.9 = (f32[4,5,8,128]{3,2,1,0:T(8,128)S(1)}, f32[4,5,8,128]{3,2,1,0:T(8,128)S(1)}, u32[]{:S(2)}, u32[]{:S(2)}) collective-permute-start(f32[4,5,8,128]{3,2,1,0:T(8,128)S(1)} %get-tuple-element.34.res_ref), channel_id=1, source_target_pairs={{0,128},{64,192},{128,0},{192,64},{1,129},{65,193},{129,1},{193,65... | collective-permute-start | bytes 245768 | tf_op jit(solution)/shard_map/ppermute | solution.py:19
  50.3 4.1 %collective-permute-start.10 = (f32[5,2,8,128]{3,2,1,0:T(8,128)S(1)}, f32[5,2,8,128]{3,2,1,0:T(8,128)S(1)}, u32[]{:S(2)}, u32[]{:S(2)}) collective-permute-start(f32[5,2,8,128]{3,2,1,0:T(8,128)S(1)} %get-tuple-element.40), channel_id=1, source_target_pairs={{0,64},{64,0},{128,192},{192,128},{1,65},{65,1},{129,193},{193,129... | collective-permute-start | bytes 122888 | tf_op jit(solution)/shard_map/ppermute | solution.py:425
